TPU v7x, 32 devices: a whole 2x2x4 slice. The times are simulated.
32 devices in a mesh: batch: 4 (over z), seq: 8 (over y, x, core).
Axes of the slice: x: 2, y: 2, z: 4, core: 2. Of those that a mesh axis runs over, the one named last changes fastest.
Arguments:
- tokens: bfloat16 [4, 1024, 2048], P('batch', 'seq'), may hold values from -6 to 6
- positions: int32 [4, 1024], P('batch', 'seq'), may hold values from 0 to 1535, as said below
- gain_attn: float32 [2048], P(('batch', 'seq')), may hold values from 0.1 to 1.9
- query_weight: float32 [2048, 2048], P(('batch', 'seq')), may hold values from -0.1875 to 0.1875
- key_weight: float32 [2048, 2048], P(('batch', 'seq')), may hold values from -0.1875 to 0.1875
- value_weight: float32 [2048, 2048], P(('batch', 'seq')), may hold values from -0.125 to 0.125
- out_weight: float32 [2048, 2048], P(None, ('batch', 'seq')), may hold values from -0.1875 to 0.1875
- gain_ffn: float32 [2048], P(('batch', 'seq')), may hold values from 0.1 to 1.9
- gate_weight: float32 [2048, 8192], P(('batch', 'seq')), may hold values from -0.125 to 0.125
- up_weight: float32 [2048, 8192], P(('batch', 'seq')), may hold values from -0.125 to 0.125
- down_weight: float32 [8192, 2048], P(None, ('batch', 'seq')), may hold values from -0.0625 to 0.0625
- cotangent: bfloat16 [4, 1024, 2048], P('batch', 'seq'), may hold values from -6 to 6
Outputs:
- layer_out: bfloat16 [4, 1024, 2048], P('batch', 'seq')
- input_grad: bfloat16 [4, 1024, 2048], P('batch', 'seq')
- attn_mass: float32 [4, 1024], P('batch', 'seq')
- gain_attn_grad: float32 [2048], P(('batch', 'seq'))
- query_grad: float32 [2048, 2048], P(('batch', 'seq'))
- key_grad: float32 [2048, 2048], P(('batch', 'seq'))
- value_grad: float32 [2048, 2048], P(('batch', 'seq'))
- out_grad: float32 [2048, 2048], P(None, ('batch', 'seq'))
- gain_ffn_grad: float32 [2048], P(('batch', 'seq'))
- gate_grad: float32 [2048, 8192], P(('batch', 'seq'))
- up_grad: float32 [2048, 8192], P(('batch', 'seq'))
- down_grad: float32 [8192, 2048], P(None, ('batch', 'seq'))
Inputs may be any that keep to these rules, and one draw needn't show every extreme that they name: Along each sequence the positions start at 0 and grow by 1 or 2 from token to token, by 2 at exactly 512 steps.
All inputs are finite; a program needn't handle non-finite values.
Results may differ from a plain program's by a relative error of at most 0.018.
The roundings to bfloat16 on the way count: a program that leaves them out, or rounds other values in their place, can miss the bound.
Values may be sent and summed in bfloat16 or wider, within the bound.
No kernel may reach another device: no remote copies, remote signals or barrier semaphores. Data moves between devices by JAX's collectives and lax.ppermute only.
A program may use at most 768 MiB of HBM per device.

v0:
```python
import math

import jax
import jax.numpy as jnp
from jax import lax
from jax.sharding import PartitionSpec as P

HEADS = 16
HD = 128


epsilon = 1e-05
rope_base = 10000.0
score_bias = -math.log(4096.0)


def norm_scale(values):
    return lax.rsqrt(jnp.mean(values * values, axis=-1, keepdims=True) + epsilon)


def norm_back(grad_normed, unit_rows, scale_rows, gain_vec):
    grad_unit = grad_normed * gain_vec
    return scale_rows * (
        grad_unit - unit_rows * jnp.mean(grad_unit * unit_rows, axis=-1, keepdims=True)
    )


def rotate(values, seq_pos, direction):
    length = values.shape[0]
    shaped = values.reshape(length, -1, HD)
    half_size = HD // 2
    frequency = jnp.exp(
        jnp.arange(half_size).astype(jnp.float32) * (-2.0 * math.log(rope_base) / HD)
    )
    angles = seq_pos.astype(jnp.float32)[:, None] * frequency[None, :]
    cosine = jnp.cos(angles)[:, None, :]
    sine_part = direction * jnp.sin(angles)[:, None, :]
    first_part = shaped[..., :half_size]
    second_part = shaped[..., half_size:]
    turned = jnp.concatenate(
        [
            first_part * cosine - second_part * sine_part,
            second_part * cosine + first_part * sine_part,
        ],
        axis=-1,
    )
    return turned.reshape(length, -1)


def times_transpose(left, right):
    return lax.dot_general(
        left, right, (((1,), (1,)), ((), ())), preferred_element_type=jnp.float32
    )


def transpose_times(left, right):
    return lax.dot_general(
        left, right, (((0,), (0,)), ((), ())), preferred_element_type=jnp.float32
    )


def sigmoid_weights(query_heads, key_heads, first_key, query_index):
    score_scale = 1.0 / math.sqrt(HD)
    scores = (
        jnp.einsum("qhd,khd->hqk", query_heads, key_heads, preferred_element_type=jnp.float32)
        * score_scale
        + score_bias
    )
    key_index = first_key + jnp.arange(key_heads.shape[0], dtype=jnp.int32)
    visible = key_index[None, None, :] <= query_index[None, :, None]
    return jnp.where(visible, jax.nn.sigmoid(scores), 0.0)


def flat_program(
    tokens,
    positions,
    gain_attn,
    query_weight,
    key_weight,
    value_weight,
    out_weight,
    gain_ffn,
    gate_weight,
    up_weight,
    down_weight,
    cotangent,
):
    inputs = tokens[0].astype(jnp.float32)
    row_count = inputs.shape[0]
    width = inputs.shape[1]
    seq_pos = positions[0]
    query_index = lax.axis_index("seq") * row_count + jnp.arange(row_count, dtype=jnp.int32)
    score_scale = 1.0 / math.sqrt(HD)
    attn_parts = (
        query_weight.astype(jnp.bfloat16),
        key_weight.astype(jnp.bfloat16),
        value_weight.astype(jnp.bfloat16),
        out_weight.astype(jnp.bfloat16),
        gain_attn.astype(jnp.bfloat16),
    )
    ffn_parts = (
        gate_weight.astype(jnp.bfloat16),
        up_weight.astype(jnp.bfloat16),
        down_weight.astype(jnp.bfloat16),
        gain_ffn.astype(jnp.bfloat16),
    )
    full_query, full_key, full_value, full_out, gain_one = (
        lax.all_gather(attn_parts[0], ("batch", "seq"), axis=0, tiled=True),
        lax.all_gather(attn_parts[1], ("batch", "seq"), axis=0, tiled=True),
        lax.all_gather(attn_parts[2], ("batch", "seq"), axis=0, tiled=True),
        lax.all_gather(attn_parts[3], ("batch", "seq"), axis=1, tiled=True),
        lax.all_gather(attn_parts[4], ("batch", "seq"), axis=0, tiled=True),
    )
    gain_one = gain_one.astype(jnp.float32)
    scale_one = norm_scale(inputs)
    unit_one = inputs * scale_one
    normed = (unit_one * gain_one).astype(jnp.bfloat16)
    query_raw = jnp.dot(normed, full_query, preferred_element_type=jnp.float32)
    key_raw = jnp.dot(normed, full_key, preferred_element_type=jnp.float32)
    values = jnp.dot(normed, full_value, preferred_element_type=jnp.float32).astype(jnp.bfloat16)
    queries = rotate(query_raw, seq_pos, 1.0).astype(jnp.bfloat16)
    key_rows = rotate(key_raw, seq_pos, 1.0).astype(jnp.bfloat16)
    query_heads = queries.reshape(row_count, HEADS, HD)
    key_piece = lax.all_gather(key_rows[None], "seq", axis=1, tiled=True)[0]
    value_piece = lax.all_gather(values[None], "seq", axis=1, tiled=True)[0]
    piece_rows = key_piece.shape[0]
    key_heads = key_piece.reshape(piece_rows, HEADS, HD)
    value_heads = value_piece.reshape(piece_rows, HEADS, HD)
    weights = sigmoid_weights(query_heads, key_heads, jnp.int32(0), query_index)
    total_out = jnp.einsum(
        "hqk,khd->qhd",
        weights.astype(jnp.bfloat16),
        value_heads,
        preferred_element_type=jnp.float32,
    )
    total_out, mass_sum = (total_out, jnp.sum(weights, axis=(0, 2)))
    attn_mass = mass_sum / HEADS
    attended = total_out.reshape(row_count, width).astype(jnp.bfloat16)
    hidden_state = inputs + jnp.dot(attended, full_out, preferred_element_type=jnp.float32)
    full_gate, full_up, full_down, gain_two = (
        lax.all_gather(ffn_parts[0], ("batch", "seq"), axis=0, tiled=True),
        lax.all_gather(ffn_parts[1], ("batch", "seq"), axis=0, tiled=True),
        lax.all_gather(ffn_parts[2], ("batch", "seq"), axis=1, tiled=True),
        lax.all_gather(ffn_parts[3], ("batch", "seq"), axis=0, tiled=True),
    )
    gain_two = gain_two.astype(jnp.float32)
    scale_two = norm_scale(hidden_state)
    unit_two = hidden_state * scale_two
    normed_ffn = (unit_two * gain_two).astype(jnp.bfloat16)
    gate_proj = jnp.dot(normed_ffn, full_gate, preferred_element_type=jnp.float32)
    up_proj = jnp.dot(normed_ffn, full_up, preferred_element_type=jnp.float32)
    gate_sigmoid = jax.nn.sigmoid(gate_proj)
    activation = (gate_proj * gate_sigmoid * up_proj).astype(jnp.bfloat16)
    outputs = hidden_state + jnp.dot(activation, full_down, preferred_element_type=jnp.float32)
    layer_out = outputs.astype(jnp.bfloat16)[None]
    grad_out = cotangent[0]
    full_gate, full_up, full_down, gain_two = (
        lax.all_gather(ffn_parts[0], ("batch", "seq"), axis=0, tiled=True),
        lax.all_gather(ffn_parts[1], ("batch", "seq"), axis=0, tiled=True),
        lax.all_gather(ffn_parts[2], ("batch", "seq"), axis=1, tiled=True),
        lax.all_gather(ffn_parts[3], ("batch", "seq"), axis=0, tiled=True),
    )
    gain_two = gain_two.astype(jnp.float32)
    grad_activ = times_transpose(grad_out, full_down)
    grad_gate = (
        grad_activ * up_proj * gate_sigmoid * (1.0 + gate_proj * (1.0 - gate_sigmoid))
    ).astype(jnp.bfloat16)
    grad_up = (grad_activ * gate_proj * gate_sigmoid).astype(jnp.bfloat16)
    grad_normed_ffn = times_transpose(grad_gate, full_gate) + times_transpose(grad_up, full_up)
    grad_gain_two = jnp.sum(grad_normed_ffn * unit_two, axis=0)
    grad_hidden = grad_out.astype(jnp.float32) + norm_back(
        grad_normed_ffn, unit_two, scale_two, gain_two
    )
    hidden_width = grad_gate.shape[1]
    ffn_grads = lax.psum_scatter(
        jnp.concatenate(
            [
                transpose_times(normed_ffn, grad_gate),
                transpose_times(normed_ffn, grad_up),
                transpose_times(grad_out, activation),
            ],
            axis=1,
        ),
        ("batch", "seq"),
        scatter_dimension=0,
        tiled=True,
    )
    gate_grad = ffn_grads[:, :hidden_width]
    up_grad = ffn_grads[:, hidden_width : 2 * hidden_width]
    down_grad = ffn_grads[:, 2 * hidden_width :].T
    full_query, full_key, full_value, full_out, gain_one = (
        lax.all_gather(attn_parts[0], ("batch", "seq"), axis=0, tiled=True),
        lax.all_gather(attn_parts[1], ("batch", "seq"), axis=0, tiled=True),
        lax.all_gather(attn_parts[2], ("batch", "seq"), axis=0, tiled=True),
        lax.all_gather(attn_parts[3], ("batch", "seq"), axis=1, tiled=True),
        lax.all_gather(attn_parts[4], ("batch", "seq"), axis=0, tiled=True),
    )
    gain_one = gain_one.astype(jnp.float32)
    grad_branch = grad_hidden.astype(jnp.bfloat16)
    grad_attended = times_transpose(grad_branch, full_out).astype(jnp.bfloat16)
    grad_heads = grad_attended.reshape(row_count, HEADS, HD)
    all_keys, all_values = (
        lax.all_gather(key_rows[None], "seq", axis=1, tiled=True),
        lax.all_gather(values[None], "seq", axis=1, tiled=True),
    )
    length = all_keys.shape[1]
    block_size = min(512, length)
    block_count = length // block_size
    key_blocks = all_keys[0].reshape(block_count, block_size, HEADS, HD)
    value_blocks = all_values[0].reshape(block_count, block_size, HEADS, HD)
    block_starts = jnp.arange(block_count, dtype=jnp.int32) * block_size

    def key_step(grad_query, step_items):
        key_heads, value_heads, first_key = step_items
        weights = sigmoid_weights(query_heads, key_heads, first_key, query_index)
        grad_weights = jnp.einsum(
            "qhd,khd->hqk", grad_heads, value_heads, preferred_element_type=jnp.float32
        )
        grad_scores = (grad_weights * weights * (1.0 - weights)).astype(jnp.bfloat16)
        grad_value = jnp.einsum(
            "hqk,qhd->khd",
            weights.astype(jnp.bfloat16),
            grad_heads,
            preferred_element_type=jnp.float32,
        )
        grad_key = (
            jnp.einsum("hqk,qhd->khd", grad_scores, query_heads, preferred_element_type=jnp.float32)
            * score_scale
        )
        grad_query = (
            grad_query
            + jnp.einsum("hqk,khd->qhd", grad_scores, key_heads, preferred_element_type=jnp.float32)
            * score_scale
        )
        return (grad_query, (grad_key, grad_value))

    grad_query, (key_terms, value_terms) = lax.scan(
        key_step,
        jnp.zeros((row_count, HEADS, HD), jnp.float32),
        (key_blocks, value_blocks, block_starts),
    )
    grad_keys, grad_values = (
        lax.psum_scatter(
            key_terms.reshape(1, length, width).astype(jnp.bfloat16),
            "seq",
            scatter_dimension=1,
            tiled=True,
        ).astype(jnp.float32),
        lax.psum_scatter(
            value_terms.reshape(1, length, width).astype(jnp.bfloat16),
            "seq",
            scatter_dimension=1,
            tiled=True,
        ).astype(jnp.float32),
    )
    grad_query_raw = rotate(grad_query.reshape(row_count, width), seq_pos, -1.0).astype(
        jnp.bfloat16
    )
    grad_key_raw = rotate(grad_keys[0], seq_pos, -1.0).astype(jnp.bfloat16)
    grad_value_low = grad_values[0].astype(jnp.bfloat16)
    grad_normed = (
        times_transpose(grad_query_raw, full_query)
        + times_transpose(grad_key_raw, full_key)
        + times_transpose(grad_value_low, full_value)
    )
    grad_gain_one = jnp.sum(grad_normed * unit_one, axis=0)
    input_grad = (grad_hidden + norm_back(grad_normed, unit_one, scale_one, gain_one)).astype(
        jnp.bfloat16
    )[None]
    summed = (
        lax.psum_scatter(
            transpose_times(normed, grad_query_raw),
            ("batch", "seq"),
            scatter_dimension=0,
            tiled=True,
        ),
        lax.psum_scatter(
            transpose_times(normed, grad_key_raw), ("batch", "seq"), scatter_dimension=0, tiled=True
        ),
        lax.psum_scatter(
            transpose_times(normed, grad_value_low),
            ("batch", "seq"),
            scatter_dimension=0,
            tiled=True,
        ),
        lax.psum_scatter(
            transpose_times(attended, grad_branch),
            ("batch", "seq"),
            scatter_dimension=1,
            tiled=True,
        ),
        lax.psum_scatter(grad_gain_one, ("batch", "seq"), scatter_dimension=0, tiled=True),
        lax.psum_scatter(grad_gain_two, ("batch", "seq"), scatter_dimension=0, tiled=True),
    )
    gradients = (
        summed[4],
        summed[0],
        summed[1],
        summed[2],
        summed[3],
        summed[5],
        gate_grad,
        up_grad,
        down_grad,
    )
    return (layer_out, input_grad, attn_mass, gradients)


def body(
    tokens,
    positions,
    gain_attn,
    query_weight,
    key_weight,
    value_weight,
    out_weight,
    gain_ffn,
    gate_weight,
    up_weight,
    down_weight,
    cotangent,
):
    layer_out, input_grad, attn_mass, gradients = flat_program(
        tokens,
        positions,
        gain_attn,
        query_weight,
        key_weight,
        value_weight,
        out_weight,
        gain_ffn,
        gate_weight,
        up_weight,
        down_weight,
        cotangent,
    )
    return (
        layer_out,
        input_grad,
        attn_mass[None],
        gradients[0],
        gradients[1],
        gradients[2],
        gradients[3],
        gradients[4],
        gradients[5],
        gradients[6],
        gradients[7],
        gradients[8],
    )


def solution(mesh):
    placed = (
        P("batch", "seq", None),
        P("batch", "seq"),
        P(("batch", "seq")),
        P(("batch", "seq"), None),
        P(("batch", "seq"), None),
        P(("batch", "seq"), None),
        P(None, ("batch", "seq")),
        P(("batch", "seq")),
        P(("batch", "seq"), None),
        P(("batch", "seq"), None),
        P(None, ("batch", "seq")),
        P("batch", "seq", None),
    )
    return jax.shard_map(
        body,
        mesh=mesh,
        in_specs=placed,
        out_specs=(
            P("batch", "seq", None),
            P("batch", "seq", None),
            P("batch", "seq"),
            P(("batch", "seq")),
            P(("batch", "seq"), None),
            P(("batch", "seq"), None),
            P(("batch", "seq"), None),
            P(None, ("batch", "seq")),
            P(("batch", "seq")),
            P(("batch", "seq"), None),
            P(("batch", "seq"), None),
            P(None, ("batch", "seq")),
        ),
        check_vma=False,
    )
```

profile of v0, /device:TPU:0, one launch (start us, length us, event | category | flops | bytes accessed | tf_op | source)
XLA Modules:
  0.0 3674.9 jit_solution(39022304064746480)
XLA Ops:
  14.6 42.3 %all-reduce.5 = (bf16[2048]{0:T(1024)(128)(2,1)S(1)}, bf16[2048]{0:T(1024)(128)(2,1)S(1)}) all-reduce(bf16[2048]{0:T(1024)(128)(2,1)S(1)} %dynamic-update-slice, bf16[2048]{0:T(1024)(128)(2,1)S(1)} %dynamic-update-slice.1), channel_id=1, replica_groups=mesh['batch'=4,'seq'=8] {'batch','seq'}, use_global_device_ids=true, to_apply=%add | all-reduce | flops 4096 | bytes 16384
  58.1 33.3 all-gather.11.cloned.1.call-done
  91.4 5.5 convolution_convert_fusion.1
  97.8 73.1 %all-gather.15.cloned.1.call-done = bf16[2048,2048]{1,0:T(8,128)(2,1)} async-done(((bf16[64,2048]{1,0:T(8,128)(2,1)}), bf16[2048,2048]{1,0:T(8,128)(2,1)}) %all-gather.15.cloned.1.call-update) | async-done | bytes 8388624 | tf_op jit(solution)/shard_map/all_gather | solution.py:109
  170.9 12.2 copy.53
  183.2 67.3 %all-gather.13.cloned.1.call-done = bf16[2048,2048]{1,0:T(8,128)(2,1)} async-done(((bf16[64,2048]{1,0:T(8,128)(2,1)}), bf16[2048,2048]{1,0:T(8,128)(2,1)}) %all-gather.13.cloned.1.call-update) | async-done | bytes 8388624 | tf_op jit(solution)/shard_map/all_gather | solution.py:108
  250.4 12.4 copy.52
  262.8 6.0 fusion.53
  280.3 7.7 all-gather.27.cloned.1.call-done
  288.1 5.7 copy.76
  293.8 34.1 all-gather.17.cloned.1.call-done
  327.8 7.8 reshape.353
  335.7 11.2 copy.58
  346.9 6.6 copy.71
  353.5 6.4 fusion.72
  361.9 46.7 %all-gather.19.cloned.1.call-done = bf16[2048,2048]{0,1:T(8,128)(2,1)} async-done(((bf16[2048,64]{0,1:T(8,128)(2,1)}), bf16[2048,2048]{0,1:T(8,128)(2,1)}) %all-gather.19.cloned.1.call-update) | async-done | bytes 8388624 | tf_op jit(solution)/shard_map/all_gather | solution.py:111
  408.6 6.5 multiply_reduce_fusion.2
  415.4 190.1 %all-gather.23.cloned.1.call-done = bf16[2048,8192]{1,0:T(8,128)(2,1)} async-done(((bf16[64,8192]{1,0:T(8,128)(2,1)}), bf16[2048,8192]{1,0:T(8,128)(2,1)}) %all-gather.23.cloned.1.call-update) | async-done | bytes 33554448 | tf_op jit(solution)/shard_map/all_gather | solution.py:142
  605.5 17.6 fusion.74
  623.0 178.9 %all-gather.21.cloned.1.call-done = bf16[2048,8192]{1,0:T(8,128)(2,1)} async-done(((bf16[64,8192]{1,0:T(8,128)(2,1)}), bf16[2048,8192]{1,0:T(8,128)(2,1)}) %all-gather.21.cloned.1.call-update) | async-done | bytes 33554448 | tf_op jit(solution)/shard_map/all_gather | solution.py:141
  801.9 17.9 fusion.73
  819.8 178.5 %all-gather.25.cloned.1.call-done = bf16[8192,2048]{0,1:T(8,128)(2,1)} async-done(((bf16[8192,64]{0,1:T(8,128)(2,1)}), bf16[8192,2048]{0,1:T(8,128)(2,1)}) %all-gather.25.cloned.1.call-update) | async-done | bytes 33554448 | tf_op jit(solution)/shard_map/all_gather | solution.py:143
  998.3 19.4 multiply_convert_fusion
  1017.8 17.4 fusion.75
  1035.2 18.5 multiply_reduce_fusion
  1055.4 5.1 fusion.34
  1060.6 29.5 while.15
  1090.1 7.3 copy.64
  1097.4 7.3 convert_element_type.246
  1106.5 25.8 fusion.78
  1137.0 7.5 convert_element_type.242
  1144.5 23.3 fusion.77
  1167.8 23.1 convolution_bitcast_fusion
  1191.0 132.2 %pad_maximum_fusion = f32[2048,24576]{1,0:T(8,128)} fusion(f32[2048,8192]{1,0:T(8,128)} %convolution_bitcast_fusion, f32[2048,8192]{1,0:T(8,128)} %fusion.78, f32[2048,8192]{1,0:T(8,128)} %fusion.77), kind=kLoop, calls=%fused_computation.23 | loop fusion | flops 100663296 | bytes 402653184 | tf_op jit(solution)/shard_map/concatenate | solution.py:176
  1324.5 11.7 fusion.64
  1337.3 12.8 fusion.47
  1354.5 11.9 fusion.60
  1366.7 11.7 fusion.57
  1380.0 23.1 fusion.24
  1403.1 8.1 fusion.76
  1411.3 8.1 convolution_add_fusion.3
  1422.5 39.4 %all-reduce.4 = (f32[2048]{0:T(1024)S(1)}, f32[2048]{0:T(1024)S(1)}) all-reduce(f32[2048]{0:T(1024)S(1)} %get-tuple-element.137, f32[2048]{0:T(1024)S(1)} %copy-done.38), channel_id=5, replica_groups=mesh['batch'=4,'seq'=8] {'batch','seq'}, use_global_device_ids=true, to_apply=%region_10.11.clone | all-reduce | flops 4096 | bytes 32768
  1464.3 1456.6 %reduce-scatter.20.cloned.1.call-done = f32[64,24576]{1,0:T(8,128)} async-done(((f32[2048,24576]{1,0:T(8,128)}), f32[64,24576]{1,0:T(8,128)}) %reduce-scatter.20.cloned.1.call-update) | async-done | bytes 6291472 | tf_op jit(solution)/shard_map/reduce_scatter | solution.py:175
  2920.9 5.7 slice_bitcast_fusion
  2926.6 179.0 %reduce-scatter.18.cloned.1.call-done = f32[2048,64]{0,1:T(8,128)} async-done(((f32[2048,2048]{0,1:T(8,128)}), f32[2048,64]{0,1:T(8,128)}) %reduce-scatter.18.cloned.1.call-update) | async-done | bytes 524304 | tf_op jit(solution)/shard_map/reduce_scatter | solution.py:286
  3105.6 187.2 %reduce-scatter.16.cloned.1.call-done = f32[64,2048]{1,0:T(8,128)} async-done(((f32[2048,2048]{1,0:T(8,128)}), f32[64,2048]{1,0:T(8,128)}) %reduce-scatter.16.cloned.1.call-update) | async-done | bytes 524304 | tf_op jit(solution)/shard_map/reduce_scatter | solution.py:280
  3292.8 187.3 %reduce-scatter.14.cloned.1.call-done = f32[64,2048]{1,0:T(8,128)} async-done(((f32[2048,2048]{1,0:T(8,128)}), f32[64,2048]{1,0:T(8,128)}) %reduce-scatter.14.cloned.1.call-update) | async-done | bytes 524304 | tf_op jit(solution)/shard_map/reduce_scatter | solution.py:277
  3480.0 187.9 %reduce-scatter.12.cloned.1.call-done = f32[64,2048]{1,0:T(8,128)} async-done(((f32[2048,2048]{1,0:T(8,128)}), f32[64,2048]{1,0:T(8,128)}) %reduce-scatter.12.cloned.1.call-update) | async-done | bytes 524304 | tf_op jit(solution)/shard_map/reduce_scatter | solution.py:271
  (198 shorter events, 74.6 us)
Async XLA Ops:
  7.2 84.2 %copy-start = (bf16[1,128,2048]{2,1,0:T(8,128)(2,1)S(1)}, bf16[1,128,2048]{2,1,0:T(8,128)(2,1)}, u32[]{:S(2)}) copy-start(bf16[1,128,2048]{2,1,0:T(8,128)(2,1)} %param.14) | copy-start | bytes 1572868
  7.2 84.2 %all-gather.11.cloned.1.call-start = ((), (), s32[]{:S(2)}) async-start(), calls=%async_computation.7 | async-start | bytes 8650752 | tf_op jit(solution)/shard_map/all_gather | solution.py:110
  9.1 161.8 %all-gather.15.cloned.1.call-start = ((), (), s32[]{:S(2)}) async-start(), calls=%async_computation.9 | async-start | bytes 8650752 | tf_op jit(solution)/shard_map/all_gather | solution.py:109
  10.9 239.5 %all-gather.13.cloned.1.call-start = ((), (), s32[]{:S(2)}) async-start(), calls=%async_computation.8 | async-start | bytes 8650752 | tf_op jit(solution)/shard_map/all_gather | solution.py:108
  12.8 275.3 %all-gather.27.cloned.1.call-start = ((), (), s32[]{:S(2)}) async-start(), calls=%async_computation.22 | async-start | bytes 4718592 | tf_op jit(solution)/shard_map/all_gather | solution.py:125
  56.9 212.0 %copy-start.29 = (f32[2048]{0:T(1024)}, f32[2048]{0:T(1024)S(1)}, u32[]{:S(2)}) copy-start(f32[2048]{0:T(1024)S(1)} %convert_element_type.208) | copy-start | bytes 24580
  58.1 210.7 %copy-start.36 = (f32[128]{0:T(128)}, f32[128]{0:T(128)S(1)}, u32[]{:S(2)}) copy-start(f32[128]{0:T(128)S(1)} %add_rsqrt_fusion.1) | copy-start | bytes 1540
  58.1 38.9 %copy-start.39 = (s32[1,128]{1,0:T(1,128)S(1)}, s32[1,128]{1,0:T(1,128)}, u32[]{:S(2)}) copy-start(s32[1,128]{1,0:T(1,128)} %param.15) | copy-start | bytes 1540
  96.9 230.9 %all-gather.17.cloned.1.call-start = ((), (), s32[]{:S(2)}) async-start(), calls=%async_computation.10 | async-start | bytes 4718592 | tf_op jit(solution)/shard_map/all_gather | solution.py:124
  97.8 173.6 %copy-start.33 = (f32[128,64]{0,1:T(8,128)}, f32[128,64]{0,1:T(8,128)S(1)}, u32[]{:S(2)}) copy-start(f32[128,64]{0,1:T(8,128)S(1)} %get-tuple-element.183) | copy-start | bytes 98308
  262.8 6.0 copy-start.2
  271.3 3.2 copy-start.27
  271.7 8.3 copy-start.31
  272.5 136.1 %all-gather.19.cloned.1.call-start = ((), (), s32[]{:S(2)}) async-start(), calls=%async_computation.11 | async-start | bytes 8650752 | tf_op jit(solution)/shard_map/all_gather | solution.py:111
  274.5 330.9 %all-gather.23.cloned.1.call-start = ((), (), s32[]{:S(2)}) async-start(), calls=%async_computation.13 | async-start | bytes 34603008 | tf_op jit(solution)/shard_map/all_gather | solution.py:142
  275.7 3.0 copy-start.28
  275.7 526.2 %all-gather.21.cloned.1.call-start = ((), (), s32[]{:S(2)}) async-start(), calls=%async_computation.12 | async-start | bytes 34603008 | tf_op jit(solution)/shard_map/all_gather | solution.py:141
  278.6 719.7 %all-gather.25.cloned.1.call-start = ((), (), s32[]{:S(2)}) async-start(), calls=%async_computation.14 | async-start | bytes 34603008 | tf_op jit(solution)/shard_map/all_gather | solution.py:143
  279.7 1056.6 %reduce-scatter.10.cloned.1.call-start = ((), (), s32[]{:S(2)}) async-start(), calls=%async_computation.16 | async-start | bytes 4718592 | tf_op jit(solution)/shard_map/reduce_scatter | solution.py:249
  346.9 6.6 copy-start.32
  353.5 6.4 copy-start.10
  415.2 638.5 %copy-start.6 = (f32[128,2048]{1,0:T(8,128)}, f32[128,2048]{1,0:T(8,128)S(1)}, u32[]{:S(2)}) copy-start(f32[128,2048]{1,0:T(8,128)S(1)} %get-tuple-element.185) | copy-start | bytes 3145732
  415.3 386.6 %copy-start.11 = (bf16[128,2048]{1,0:T(8,128)(2,1)}, bf16[128,2048]{1,0:T(8,128)(2,1)S(1)}, u32[]{:S(2)}) copy-start(bf16[128,2048]{1,0:T(8,128)(2,1)S(1)} %multiply_convert_fusion.3) | copy-start | bytes 1572868
  1017.8 17.4 copy-start.15
  1055.3 5.1 copy-start.8
  1060.6 3.7 copy-start.3
  1068.7 4.6 copy-start.21
  1068.8 3.7 copy-start.22
  1075.4 3.6 copy-start.3
  1083.5 4.6 copy-start.21
  1083.5 3.7 copy-start.22
  1090.1 7.3 copy-start.4
  1104.7 245.5 %reduce-scatter.8.cloned.1.call-start = ((), (), s32[]{:S(2)}) async-start(), calls=%async_computation.15 | async-start | bytes 4718592 | tf_op jit(solution)/shard_map/reduce_scatter | solution.py:243
  1106.5 25.8 copy-start.24
  1137.0 7.5 copy-start.14
  1144.5 23.3 copy-start.13
  1144.5 23.3 copy-start.25
  1190.9 1730.0 %reduce-scatter.20.cloned.1.call-start = ((), (), s32[]{:S(2)}) async-start(), calls=%async_computation.21 | async-start | bytes 207618048 | tf_op jit(solution)/shard_map/reduce_scatter | solution.py:175
  1323.2 1782.4 %reduce-scatter.18.cloned.1.call-start = ((), (), s32[]{:S(2)}) async-start(), calls=%async_computation.20 | async-start | bytes 17301504 | tf_op jit(solution)/shard_map/reduce_scatter | solution.py:286
  1336.2 1956.5 %reduce-scatter.16.cloned.1.call-start = ((), (), s32[]{:S(2)}) async-start(), calls=%async_computation.19 | async-start | bytes 17301504 | tf_op jit(solution)/shard_map/reduce_scatter | solution.py:280
  1350.2 2129.9 %reduce-scatter.14.cloned.1.call-start = ((), (), s32[]{:S(2)}) async-start(), calls=%async_computation.18 | async-start | bytes 17301504 | tf_op jit(solution)/shard_map/reduce_scatter | solution.py:277
  1354.5 11.9 copy-start.18
  1366.4 2301.5 %reduce-scatter.12.cloned.1.call-start = ((), (), s32[]{:S(2)}) async-start(), calls=%async_computation.17 | async-start | bytes 17301504 | tf_op jit(solution)/shard_map/reduce_scatter | solution.py:271
  1403.1 8.1 copy-start.19
  1403.1 16.2 slice-start
  1411.2 8.2 slice-start.1
  1411.3 8.2 copy-start.26
  1419.4 3.1 copy-start.38
  (16 other events, 27.3 us)
Sparse Core Ops, SparseCore 0:
  11.5 79.8 all-gather.10
  94.8 76.0 all-gather.14
  174.3 76.0 all-gather.12
  252.7 35.2 all-gather.26
  290.4 37.4 all-gather.16
  331.1 77.4 all-gather.18
  412.1 193.3 all-gather.22
  608.9 192.9 all-gather.20
  805.3 192.9 all-gather.24
  1104.8 49.4 reduce-scatter.9
  1191.0 50.0 reduce-scatter.7
  1323.3 1597.5 reduce-scatter.19
  2923.8 181.8 reduce-scatter.17
  3108.3 184.3 reduce-scatter.15
  3295.5 184.5 reduce-scatter.13
  3482.8 185.1 reduce-scatter.11
where the time goes:
time: 3690 us; the launch traced here: 3670 us
  waiting for transfers between devices  3010 us (82%)
  matrix products  298 us (8%)
  other arithmetic  157 us (4%)
  local copies, waits for them, and re-layouts  114 us (3%)
  blocking collectives  81.7 us (2%)
    reduce_scatter x1, waiting for transfers between devices, flat_program(): lax.psum_scatter(jnp.concatenate([transpose_times(normed_ffn, grad_gate),...  1460 us
    all_gather x1, waiting for transfers between devices, flat_program(): lax.all_gather(ffn_parts[1], ('batch', 'seq'), axis=0, tiled=True)  190 us
    reduce_scatter x1, waiting for transfers between devices, flat_program(): lax.psum_scatter(transpose_times(normed, grad_query_raw), ('batch', 'seq'...  188 us
    reduce_scatter x1, waiting for transfers between devices, flat_program(): lax.psum_scatter(transpose_times(normed, grad_key_raw), ('batch', 'seq'),...  187 us
    reduce_scatter x1, waiting for transfers between devices, flat_program(): lax.psum_scatter(transpose_times(normed, grad_value_low), ('batch', 'seq'...  187 us
    reduce_scatter x1, waiting for transfers between devices, flat_program(): lax.psum_scatter(transpose_times(attended, grad_branch), ('batch', 'seq')...  179 us
    all_gather x1, waiting for transfers between devices, flat_program(): lax.all_gather(ffn_parts[0], ('batch', 'seq'), axis=0, tiled=True)  179 us
    all_gather x1, waiting for transfers between devices, flat_program(): lax.all_gather(ffn_parts[2], ('batch', 'seq'), axis=1, tiled=True)  178 us
  transfers between devices with their start and end apart: 16, of which 14 were waited for; matrix products, arithmetic and copies ran while one was open for 12% of the time, Pallas kernels for 0%

commit v1 on v0

v1 whole, which is shorter than its diff:
```python
import math

import jax
import jax.numpy as jnp
from jax import lax
from jax.sharding import PartitionSpec as P

HD = 128
epsilon = 1e-05
rope_base = 10000.0
score_bias = -math.log(4096.0)
score_scale = 1.0 / math.sqrt(HD)
f32 = jnp.float32
bf16 = jnp.bfloat16
PAD = 16
CHUNKS = 4


def dot(left, right):
    return jnp.dot(left, right, preferred_element_type=f32)


def dot_t(left, right):
    return lax.dot_general(left, right, (((1,), (1,)), ((), ())), preferred_element_type=f32)


def t_dot(left, right):
    return lax.dot_general(left, right, (((0,), (0,)), ((), ())), preferred_element_type=f32)


def norm_scale(values):
    return lax.rsqrt(jnp.mean(values * values, axis=-1, keepdims=True) + epsilon)


def norm_back(grad_normed, unit_rows, scale_rows, gain_vec):
    grad_unit = grad_normed * gain_vec
    return scale_rows * (
        grad_unit - unit_rows * jnp.mean(grad_unit * unit_rows, axis=-1, keepdims=True)
    )


def angles_of(seq_pos):
    half_size = HD // 2
    frequency = jnp.exp(
        jnp.arange(half_size).astype(f32) * (-2.0 * math.log(rope_base) / HD)
    )
    angles = seq_pos.astype(f32)[:, None] * frequency[None, :]
    return jnp.cos(angles)[None], jnp.sin(angles)[None]


def rotate(heads, cosine, sine):
    half_size = HD // 2
    first = heads[..., :half_size]
    second = heads[..., half_size:]
    return jnp.concatenate(
        [first * cosine - second * sine, second * cosine + first * sine], axis=-1
    )


def to_heads(rows):
    return rows.reshape(rows.shape[0], -1, HD).transpose(1, 0, 2)


def from_heads(heads):
    return heads.transpose(1, 0, 2).reshape(heads.shape[1], -1)


def body(
    tokens,
    positions,
    gain_attn,
    query_weight,
    key_weight,
    value_weight,
    out_weight,
    gain_ffn,
    gate_weight,
    up_weight,
    down_weight,
    cotangent,
):
    ns = lax.axis_size("seq")
    nb = lax.axis_size("batch")
    rows = query_weight.shape[0]
    width = query_weight.shape[1]
    hidden = gate_weight.shape[1]
    head_cols = width // ns
    ffn_cols = hidden // (ns * CHUNKS)

    def slices(weight, parts=1):
        cut = weight.astype(bf16).reshape(rows, ns, parts, -1)
        return cut.transpose(2, 1, 0, 3)

    def swap(blocks):
        return lax.all_to_all(blocks, "seq", split_axis=0, concat_axis=0, tiled=True)

    def gather_z(block):
        return lax.all_gather(block, "batch", axis=0, tiled=True)

    def gather_s(block):
        return lax.all_gather(block, "seq", axis=0, tiled=True)

    def scatter_z(full):
        return lax.psum_scatter(full, "batch", scatter_dimension=0, tiled=True)

    def scatter_s(full):
        return lax.psum_scatter(full, "seq", scatter_dimension=0, tiled=True)

    qkv_blocks = jnp.concatenate(
        [slices(query_weight)[0], slices(key_weight)[0], slices(value_weight)[0]], axis=2
    )
    gains = jnp.stack([gain_attn.astype(bf16), gain_ffn.astype(bf16)])
    gain_rows = jnp.pad(gains, ((0, PAD - 2), (0, 3 * head_cols - rows)))
    gain_rows = jnp.broadcast_to(gain_rows[None], (ns,) + gain_rows.shape)
    qkv_blocks = swap(jnp.concatenate([qkv_blocks, gain_rows], axis=1))
    full_blocks = gather_z(qkv_blocks)
    w_qkv = full_blocks[:, :rows].reshape(nb * ns * rows, 3 * head_cols)
    gain_one = full_blocks[:, rows, :rows].reshape(-1).astype(f32)
    gain_two = full_blocks[:, rows + 1, :rows].reshape(-1).astype(f32)

    out_blocks = swap(slices(out_weight.T)[0])
    w_out = gather_z(out_blocks.reshape(ns * rows, head_cols))

    ffn_blocks = jnp.concatenate(
        [slices(gate_weight, CHUNKS), slices(up_weight, CHUNKS), slices(down_weight.T, CHUNKS)],
        axis=3,
    )
    w_ffn = [
        gather_z(swap(ffn_blocks[c]).reshape(ns * rows, 3 * ffn_cols)) for c in range(CHUNKS)
    ]

    x_own = tokens[0]
    x_own_f = x_own.astype(f32)
    x_all = gather_s(x_own)
    seq_pos = gather_s(positions[0])
    dy_all = gather_s(cotangent[0])
    length = x_all.shape[0]
    unit_one = x_all.astype(f32)
    unit_one = unit_one * norm_scale(unit_one)
    normed = (unit_one * gain_one).astype(bf16)
    cosine, sine = angles_of(seq_pos)
    qkv = dot(normed, w_qkv)
    queries = rotate(to_heads(qkv[:, :head_cols]), cosine, sine).astype(bf16)
    keys = rotate(to_heads(qkv[:, head_cols : 2 * head_cols]), cosine, sine).astype(bf16)
    values = to_heads(qkv[:, 2 * head_cols :]).astype(bf16)
    index = jnp.arange(length, dtype=jnp.int32)
    visible = (index[None, :] <= index[:, None])[None]
    scores = (
        jnp.einsum("hqd,hkd->hqk", queries, keys, preferred_element_type=f32) * score_scale
        + score_bias
    )
    weights = jnp.where(visible, jax.nn.sigmoid(scores), 0.0)
    weights_low = weights.astype(bf16)
    attended = from_heads(
        jnp.einsum("hqk,hkd->hqd", weights_low, values, preferred_element_type=f32).astype(bf16)
    )
    heads_total = width // HD
    attn_mass = scatter_s(jnp.sum(weights, axis=(0, 2)) * (1.0 / heads_total))

    hidden_own = x_own_f + scatter_s(dot_t(attended, w_out).astype(bf16)).astype(f32)
    scale_two = norm_scale(hidden_own)
    unit_two = hidden_own * scale_two
    normed_ffn = gather_s((unit_two * gain_two).astype(bf16))

    out_part = 0.0
    back_part = 0.0
    ffn_sums = []
    for c in range(CHUNKS):
        w_gate = w_ffn[c][:, :ffn_cols]
        w_up = w_ffn[c][:, ffn_cols : 2 * ffn_cols]
        w_down = w_ffn[c][:, 2 * ffn_cols :]
        gate = dot(normed_ffn, w_gate)
        up = dot(normed_ffn, w_up)
        grad_act = dot(dy_all, w_down)
        sig = jax.nn.sigmoid(gate)
        silu = gate * sig
        act = (silu * up).astype(bf16)
        grad_gate = (grad_act * up * sig * (1.0 + gate * (1.0 - sig))).astype(bf16)
        grad_up = (grad_act * silu).astype(bf16)
        out_part = out_part + dot_t(act, w_down)
        back_part = back_part + dot_t(
            jnp.concatenate([grad_gate, grad_up], axis=1), w_ffn[c][:, : 2 * ffn_cols]
        )
        sums = jnp.concatenate(
            [
                t_dot(normed_ffn, grad_gate).astype(bf16),
                t_dot(normed_ffn, grad_up).astype(bf16),
                t_dot(dy_all, act).astype(bf16),
            ],
            axis=1,
        )
        ffn_sums.append(scatter_z(sums))
    grad_normed_two = scatter_s(back_part.astype(bf16)).astype(f32)
    layer_out = (hidden_own + scatter_s(out_part.astype(bf16)).astype(f32)).astype(bf16)
    grad_hidden = cotangent[0].astype(f32) + norm_back(
        grad_normed_two, unit_two, scale_two, gain_two
    )
    gain_two_part = jnp.sum(grad_normed_two * unit_two, axis=0)

    branch = gather_s(grad_hidden.astype(bf16))
    grad_heads = to_heads(dot(branch, w_out).astype(bf16))
    out_sum = t_dot(branch, attended).astype(bf16)
    grad_weights = jnp.einsum("hqd,hkd->hqk", grad_heads, values, preferred_element_type=f32)
    grad_scores = (grad_weights * weights * (1.0 - weights)).astype(bf16)
    grad_values = jnp.einsum("hqk,hqd->hkd", weights_low, grad_heads, preferred_element_type=f32)
    grad_keys = (
        jnp.einsum("hqk,hqd->hkd", grad_scores, queries, preferred_element_type=f32) * score_scale
    )
    grad_queries = (
        jnp.einsum("hqk,hkd->hqd", grad_scores, keys, preferred_element_type=f32) * score_scale
    )
    grad_qkv = jnp.concatenate(
        [
            from_heads(rotate(grad_queries, cosine, -sine).astype(bf16)),
            from_heads(rotate(grad_keys, cosine, -sine).astype(bf16)),
            from_heads(grad_values.astype(bf16)),
        ],
        axis=1,
    )
    qkv_sum = t_dot(normed, grad_qkv).astype(bf16)
    normed_part = dot_t(grad_qkv, w_qkv)
    gain_one_part = jnp.sum(normed_part * unit_one, axis=0)
    grad_normed = scatter_s(normed_part.astype(bf16)).astype(f32)
    scale_one = norm_scale(x_own_f)
    input_grad = (
        grad_hidden + norm_back(grad_normed, x_own_f * scale_one, scale_one, gain_one)
    ).astype(bf16)

    attn_cols = 3 * head_cols
    gain_parts = jnp.stack([gain_one_part, gain_two_part]).astype(bf16)
    gain_parts = gain_parts.reshape(2, nb, ns, rows).transpose(1, 2, 0, 3)
    gain_parts = jnp.pad(gain_parts, ((0, 0), (0, 0), (0, PAD - 2), (0, attn_cols - rows)))
    attn_sums = jnp.concatenate(
        [qkv_sum.reshape(nb, ns, rows, attn_cols), gain_parts], axis=2
    ).reshape(nb * ns * (rows + PAD), attn_cols)
    attn_sums = swap(scatter_z(attn_sums).reshape(ns, rows + PAD, attn_cols))
    gain_grads = jnp.sum(attn_sums[:, rows : rows + 2, :rows].astype(f32), axis=0)

    def unslice(blocks):
        return blocks.astype(f32).transpose(1, 0, 2).reshape(rows, -1)

    attn_grads = [
        unslice(attn_sums[:, :rows, i * head_cols : (i + 1) * head_cols]) for i in range(3)
    ]
    out_grad = unslice(swap(scatter_z(out_sum).reshape(ns, rows, head_cols))).T
    ffn_back = jnp.stack(
        [swap(part.reshape(ns, rows, 3 * ffn_cols)) for part in ffn_sums], axis=1
    )
    ffn_grads = [
        ffn_back[..., i * ffn_cols : (i + 1) * ffn_cols]
        .astype(f32)
        .transpose(2, 0, 1, 3)
        .reshape(rows, hidden)
        for i in range(3)
    ]
    return (
        layer_out[None],
        input_grad[None],
        attn_mass[None],
        gain_grads[0],
        attn_grads[0],
        attn_grads[1],
        attn_grads[2],
        out_grad,
        gain_grads[1],
        ffn_grads[0],
        ffn_grads[1],
        ffn_grads[2].T,
    )


def solution(mesh):
    both = ("batch", "seq")
    token_spec = P("batch", "seq", None)
    row_spec = P(both, None)
    col_spec = P(None, both)
    return jax.shard_map(
        body,
        mesh=mesh,
        in_specs=(
            token_spec,
            P("batch", "seq"),
            P(both),
            row_spec,
            row_spec,
            row_spec,
            col_spec,
            P(both),
            row_spec,
            row_spec,
            col_spec,
            token_spec,
        ),
        out_specs=(
            token_spec,
            token_spec,
            P("batch", "seq"),
            P(both),
            row_spec,
            row_spec,
            row_spec,
            col_spec,
            P(both),
            row_spec,
            row_spec,
            col_spec,
        ),
        check_vma=False,
    )
```

time: 3690 us -> 1200 us (0.33)
  waiting for transfers between devices: 3010 us -> 746 us
  matrix products: 298 us -> 163 us
  other arithmetic: 157 us -> 53.7 us
  local copies, waits for them, and re-layouts: 114 us -> 63.2 us
  blocking collectives: 81.7 us -> 125 us
    reduce_scatter x7 -> x10, waiting for transfers between devices: 2200 us -> 372 us  [the longest x6 216 us: scatter_z(): return lax.psum_scatter(full, 'batch', scatter_dimension=0, tiled=True)]
    all_gather x9 -> x10, waiting for transfers between devices: 810 us -> 372 us  [the longest x6 268 us: gather_z(): return lax.all_gather(block, 'batch', axis=0, tiled=True)]
    dot_general x33 -> x44, matrix products: 298 us -> 163 us  [the longest x10 62.9 us: dot_t(): lax.dot_general(left, right, (((1,), (1,)), ((), ())), preferred_element_...]
    concatenate x3 -> x7, other arithmetic: 133 us -> 13.2 us  [the longest x4 7.4 us: body(): jnp.concatenate([t_dot(normed_ffn, grad_gate).astype(bf16), t_dot(normed_...]
    all_to_all x0 -> x5, blocking collectives: none -> 97 us  [swap(): lax.all_to_all(blocks, 'seq', split_axis=0, concat_axis=0, tiled=True)]
    unnamed x2 -> x1, blocking collectives: 81.7 us -> 17.7 us
  transfers between devices with their start and end apart: 16 -> 27, of which waited for: 14 -> 17; matrix products, arithmetic and copies ran while one was open for 12% -> 17% of each run, Pallas kernels for 0% -> 0%
where the time goes in v1:
time: 1200 us
  waiting for transfers between devices  746 us (62%)
  matrix products  163 us (14%)
  blocking collectives  125 us (10%)
  local copies, waits for them, and re-layouts  63.2 us (5%)
  other arithmetic  53.7 us (4%)
  starting transfers between devices  28.3 us (2%)
  between operations  16.4 us (1%)
    all_gather x6, waiting for transfers between devices, gather_z(): return lax.all_gather(block, 'batch', axis=0, tiled=True)  268 us
    reduce_scatter x6, waiting for transfers between devices, scatter_z(): return lax.psum_scatter(full, 'batch', scatter_dimension=0, tiled=True)  216 us
    reduce_scatter x4, waiting for transfers between devices, scatter_s(): return lax.psum_scatter(full, 'seq', scatter_dimension=0, tiled=True)  156 us
    all_gather x4, waiting for transfers between devices, gather_s(): return lax.all_gather(block, 'seq', axis=0, tiled=True)  104 us
    all_to_all x5, blocking collectives, swap(): lax.all_to_all(blocks, 'seq', split_axis=0, concat_axis=0, tiled=True)  97 us
    dot_general x10, matrix products, dot_t(): lax.dot_general(left, right, (((1,), (1,)), ((), ())), preferred_element_...  62.9 us
    dot_general x14, matrix products, dot(): return jnp.dot(left, right, preferred_element_type=f32)  45.1 us
    dot_general x14, matrix products, t_dot(): lax.dot_general(left, right, (((0,), (0,)), ((), ())), preferred_element_...  36.3 us
  transfers between devices with their start and end apart: 27, of which 17 were waited for; matrix products, arithmetic and copies ran while one was open for 17% of the time, Pallas kernels for 0%

profile of v1, /device:TPU:0, one launch (start us, length us, event | category | flops | bytes accessed | tf_op | source)
XLA Modules:
  0.0 1195.0 jit_solution(3867566230557798909)
XLA Ops:
  11.7 19.7 %all_to_all.60 = bf16[8,80,768]{2,1,0:T(8,128)(2,1)} all-to-all(bf16[8,80,768]{2,1,0:T(8,128)(2,1)S(1)} %copy.128), channel_id=1, replica_groups=mesh['batch'=4,'seq'=8] {'seq'}, dimensions={0} | all-to-all | bytes 1966080 | tf_op jit(solution)/shard_map/all_to_all | solution.py:95
  36.5 9.8 all-gather.1
  51.6 55.8 %all-gather.14.cloned.1.call-done = bf16[32,80,768]{2,1,0:T(8,128)(2,1)} async-done(((bf16[8,80,768]{2,1,0:T(8,128)(2,1)}), bf16[32,80,768]{2,1,0:T(8,128)(2,1)}) %all-gather.14.cloned.1.call-update) | async-done | bytes 3932176 | tf_op jit(solution)/shard_map/all_gather | solution.py:98
  108.5 3.9 slice.174
  112.4 32.2 %all-gather.30.cloned.1.call-done = bf16[1,1024,2048]{2,1,0:T(8,128)(2,1)} async-done(((bf16[1,128,2048]{2,1,0:T(8,128)(2,1)}), bf16[1,1024,2048]{2,1,0:T(8,128)(2,1)}) %all-gather.30.cloned.1.call-update) | async-done | bytes 4194320 | tf_op jit(solution)/shard_map/all_gather | solution.py:101
  148.0 5.7 fusion.81
  158.9 4.3 fusion.161
  167.2 7.5 all-gather.16.cloned.1.call-done
  174.7 4.7 convolution_convert_fusion
  192.3 5.6 fusion.159
  198.4 24.7 %all_to_all.61 = bf16[8,64,768]{2,1,0:T(8,128)(2,1)} all-to-all(bf16[8,64,768]{2,1,0:T(8,128)(2,1)S(1)} %bitcast.289), channel_id=1, replica_groups=mesh['batch'=4,'seq'=8] {'seq'}, dimensions={0} | all-to-all | bytes 1572864 | tf_op jit(solution)/shard_map/all_to_all | solution.py:95
  225.6 21.3 %all_to_all.62 = bf16[8,64,768]{2,1,0:T(8,128)(2,1)} all-to-all(bf16[8,64,768]{2,1,0:T(8,128)(2,1)S(1)} %bitcast.290), channel_id=1, replica_groups=mesh['batch'=4,'seq'=8] {'seq'}, dimensions={0} | all-to-all | bytes 1572864 | tf_op jit(solution)/shard_map/all_to_all | solution.py:95
  248.9 15.7 %all_to_all.63 = bf16[8,64,768]{2,1,0:T(8,128)(2,1)} all-to-all(bf16[8,64,768]{2,1,0:T(8,128)(2,1)S(1)} %bitcast.291), channel_id=1, replica_groups=mesh['batch'=4,'seq'=8] {'seq'}, dimensions={0} | all-to-all | bytes 1572864 | tf_op jit(solution)/shard_map/all_to_all | solution.py:95
  265.1 15.7 %all_to_all.64 = bf16[8,64,768]{2,1,0:T(8,128)(2,1)} all-to-all(bf16[8,64,768]{2,1,0:T(8,128)(2,1)S(1)} %bitcast.292), channel_id=1, replica_groups=mesh['batch'=4,'seq'=8] {'seq'}, dimensions={0} | all-to-all | bytes 1572864 | tf_op jit(solution)/shard_map/all_to_all | solution.py:95
  284.7 25.8 %all-gather.20.cloned.1.call-done = bf16[2048,768]{1,0:T(8,128)(2,1)} async-done(((bf16[512,768]{1,0:T(8,128)(2,1)}), bf16[2048,768]{1,0:T(8,128)(2,1)}) %all-gather.20.cloned.1.call-update) | async-done | bytes 3145744 | tf_op jit(solution)/shard_map/all_gather | solution.py:98
  310.5 37.3 %all-gather.32.cloned.1.call-done = bf16[1,1024,2048]{2,1,0:T(8,128)(2,1)} async-done(((bf16[1,128,2048]{2,1,0:T(8,128)(2,1)}), bf16[1,1024,2048]{2,1,0:T(8,128)(2,1)}) %all-gather.32.cloned.1.call-update) | async-done | bytes 4194320 | tf_op jit(solution)/shard_map/all_gather | solution.py:101
  347.8 4.8 fusion.58
  352.6 60.4 %all-gather.22.cloned.1.call-done = bf16[2048,768]{1,0:T(8,128)(2,1)} async-done(((bf16[512,768]{1,0:T(8,128)(2,1)}), bf16[2048,768]{1,0:T(8,128)(2,1)}) %all-gather.22.cloned.1.call-update) | async-done | bytes 3145744 | tf_op jit(solution)/shard_map/all_gather | solution.py:98
  413.0 4.8 fusion.61
  417.8 59.0 %all-gather.24.cloned.1.call-done = bf16[2048,768]{1,0:T(8,128)(2,1)} async-done(((bf16[512,768]{1,0:T(8,128)(2,1)}), bf16[2048,768]{1,0:T(8,128)(2,1)}) %all-gather.24.cloned.1.call-update) | async-done | bytes 3145744 | tf_op jit(solution)/shard_map/all_gather | solution.py:98
  476.8 3.8 fusion.64
  480.6 60.0 %all-gather.26.cloned.1.call-done = bf16[2048,768]{1,0:T(8,128)(2,1)} async-done(((bf16[512,768]{1,0:T(8,128)(2,1)}), bf16[2048,768]{1,0:T(8,128)(2,1)}) %all-gather.26.cloned.1.call-update) | async-done | bytes 3145744 | tf_op jit(solution)/shard_map/all_gather | solution.py:98
  540.6 3.8 fusion.67
  544.5 34.0 %all-gather.18.cloned.1.call-done = bf16[1024,2048]{1,0:T(8,128)(2,1)} async-done(((bf16[128,2048]{1,0:T(8,128)(2,1)}), bf16[1024,2048]{1,0:T(8,128)(2,1)}) %all-gather.18.cloned.1.call-update) | async-done | bytes 4194320 | tf_op jit(solution)/shard_map/all_gather | solution.py:101
  578.5 3.9 fusion.105
  602.4 5.6 fusion.52
  608.0 5.6 fusion.48
  613.7 12.1 %add_convert_fusion = bf16[1024,2048]{1,0:T(8,128)(2,1)} fusion(f32[1024,2048]{1,0:T(8,128)} %fusion.48, f32[1024,2048]{1,0:T(8,128)} %fusion.52, f32[1024,2048]{1,0:T(8,128)S(1)} %fusion.50, bf16[2048,768]{1,0:T(8,128)(2,1)} %all-gather.26.cloned.1.call-done, bf16[1024,256]{0,1:T(8,128)(2,1)} %get-tuple-element.33, bf16[1024,256]{0,1:T(8,128)(2,1)} %get-tuple-element.32), kind=kOutput, calls=%fused_computation.8 | convolution fusion | flops 2157969408 | bytes 32505856 | tf_op jit(solution)/shard_map/dot_general | solution.py:24
  625.9 51.4 %reduce-scatter.15.cloned.1.call-done = bf16[128,2048]{1,0:T(8,128)(2,1)} async-done(((bf16[1024,2048]{1,0:T(8,128)(2,1)}), bf16[128,2048]{1,0:T(8,128)(2,1)}) %reduce-scatter.15.cloned.1.call-update) | async-done | bytes 524304 | tf_op jit(solution)/shard_map/reduce_scatter | solution.py:107
  722.4 4.9 multiply_convert_fusion
  734.1 4.5 convolution_convert_fusion.10
  738.7 5.0 fusion.73
  744.0 8.7 fusion.3
  752.8 6.0 convolution_convert_fusion.1
  764.7 5.8 fusion.135
  770.5 5.8 fusion.129
  776.3 9.6 add_convert_fusion.1
  791.8 51.4 %reduce-scatter.25.cloned.1.call-done = bf16[512,768]{0,1:T(8,128)(2,1)} async-done(((bf16[2048,768]{0,1:T(8,128)(2,1)}), bf16[512,768]{0,1:T(8,128)(2,1)}) %reduce-scatter.25.cloned.1.call-update) | async-done | bytes 786448 | tf_op jit(solution)/shard_map/reduce_scatter | solution.py:104
  845.4 3.8 all-to-all-start.9
  849.2 56.4 %reduce-scatter.27.cloned.1.call-done = bf16[512,768]{0,1:T(8,128)(2,1)} async-done(((bf16[2048,768]{0,1:T(8,128)(2,1)}), bf16[512,768]{0,1:T(8,128)(2,1)}) %reduce-scatter.27.cloned.1.call-update) | async-done | bytes 786448 | tf_op jit(solution)/shard_map/reduce_scatter | solution.py:104
  911.6 56.5 %reduce-scatter.29.cloned.1.call-done = bf16[512,768]{0,1:T(8,128)(2,1)} async-done(((bf16[2048,768]{0,1:T(8,128)(2,1)}), bf16[512,768]{0,1:T(8,128)(2,1)}) %reduce-scatter.29.cloned.1.call-update) | async-done | bytes 786448 | tf_op jit(solution)/shard_map/reduce_scatter | solution.py:104
  970.4 4.2 all-to-all-start.11
  975.9 17.7 %all-reduce.2 = f32[1024]{0:T(1024)S(1)} all-reduce(f32[1024]{0:T(1024)S(1)} %broadcast_multiply_fusion), channel_id=9, replica_groups=mesh['batch'=4,'seq'=8] {'seq'}, use_global_device_ids=true, to_apply=%region_10.11.clone | all-reduce | flops 1024 | bytes 8192
  998.0 4.0 all-to-all-start.7
  1002.0 4.8 convert_bitcast_fusion
  1021.1 50.5 %reduce-scatter.19.cloned.1.call-done = bf16[640,768]{1,0:T(8,128)(2,1)} async-done(((bf16[2560,768]{1,0:T(8,128)(2,1)}), bf16[640,768]{1,0:T(8,128)(2,1)}) %reduce-scatter.19.cloned.1.call-update) | async-done | bytes 983056 | tf_op jit(solution)/shard_map/reduce_scatter | solution.py:104
  1075.3 51.8 %reduce-scatter.17.cloned.1.call-done = bf16[128,2048]{1,0:T(8,128)(2,1)} async-done(((bf16[1024,2048]{1,0:T(8,128)(2,1)}), bf16[128,2048]{1,0:T(8,128)(2,1)}) %reduce-scatter.17.cloned.1.call-update) | async-done | bytes 524304 | tf_op jit(solution)/shard_map/reduce_scatter | solution.py:107
  1128.4 53.2 %reduce-scatter.13.cloned.1.call-done = bf16[128,2048]{1,0:T(8,128)(2,1)} async-done(((bf16[1024,2048]{1,0:T(8,128)(2,1)}), bf16[128,2048]{1,0:T(8,128)(2,1)}) %reduce-scatter.13.cloned.1.call-update) | async-done | bytes 524304 | tf_op jit(solution)/shard_map/reduce_scatter | solution.py:107
  (307 shorter events, 175.1 us)
Async XLA Ops:
  7.2 100.2 %all-gather.14.cloned.1.call-start = ((), (), s32[]{:S(2)}) async-start(), calls=%async_computation.22 | async-start | bytes 4915200 | tf_op jit(solution)/shard_map/all_gather | solution.py:98
  10.6 21.6 %copy-start.36 = (f32[2048,64]{0,1:T(8,128)S(1)}, f32[2048,64]{0,1:T(8,128)}, u32[]{:S(2)}) copy-start(f32[2048,64]{0,1:T(8,128)} %param.18) | copy-start | bytes 1572868
  11.5 25.0 %copy-start.47 = (s32[1,128]{1,0:T(1,128)S(1)}, s32[1,128]{1,0:T(1,128)}, u32[]{:S(2)}) copy-start(s32[1,128]{1,0:T(1,128)} %param.13) | copy-start | bytes 1540
  31.4 113.2 %all-gather.30.cloned.1.call-start = ((), (), s32[]{:S(2)}) async-start(), calls=%async_computation.40 | async-start | bytes 4718592 | tf_op jit(solution)/shard_map/all_gather | solution.py:101
  33.0 17.6 %all-to-all-start.1 = ((bf16[8,64,256]{2,1,0:T(8,128)(2,1)}), bf16[8,64,256]{2,1,0:T(8,128)(2,1)S(1)}, u32[]{:S(2)}, u32[]{:S(2)}) async-start(bf16[8,64,256]{2,1,0:T(8,128)(2,1)} %copy.132), calls=%async_computation.1 | async-start | bytes 524288 | tf_op jit(solution)/shard_map/all_to_all | solution.py:95
  36.5 138.2 %all-gather.16.cloned.1.call-start = ((), (), s32[]{:S(2)}) async-start(), calls=%async_computation.23 | async-start | bytes 1310720 | tf_op jit(solution)/shard_map/all_gather | solution.py:98
  50.7 106.3 %copy-start.3 = (f32[1024,64]{1,0:T(8,128)}, f32[1024,64]{1,0:T(8,128)S(1)}, u32[]{:S(2)}) copy-start(f32[1024,64]{1,0:T(8,128)S(1)} %get-tuple-element.59) | copy-start | bytes 786436
  51.4 229.5 %reduce-scatter.11.cloned.1.call-start = ((), (), s32[]{:S(2)}) async-start(), calls=%async_computation.24 | async-start | bytes 4718592 | tf_op jit(solution)/shard_map/reduce_scatter | solution.py:107
  108.5 39.4 %copy-start.42 = (f32[2048]{0:T(1024)}, f32[2048]{0:T(1024)S(1)}, u32[]{:S(2)}) copy-start(f32[2048]{0:T(1024)S(1)} %reshape.336) | copy-start | bytes 24580
  147.8 6.0 copy-start.45
  167.2 12.2 %copy-start.9 = (bf16[2,1024,128]{1,2,0:T(8,128)(2,1)}, bf16[2,1024,128]{1,2,0:T(8,128)(2,1)S(1)}, u32[]{:S(2)}) copy-start(bf16[2,1024,128]{1,2,0:T(8,128)(2,1)S(1)} %fusion.70) | copy-start | bytes 1572868
  179.5 131.0 %all-gather.20.cloned.1.call-start = ((), (), s32[]{:S(2)}) async-start(), calls=%async_computation.26 | async-start | bytes 3932160 | tf_op jit(solution)/shard_map/all_gather | solution.py:98
  223.1 124.7 %all-gather.32.cloned.1.call-start = ((), (), s32[]{:S(2)}) async-start(), calls=%async_computation.41 | async-start | bytes 4718592 | tf_op jit(solution)/shard_map/all_gather | solution.py:101
  223.7 189.3 %all-gather.22.cloned.1.call-start = ((), (), s32[]{:S(2)}) async-start(), calls=%async_computation.27 | async-start | bytes 3932160 | tf_op jit(solution)/shard_map/all_gather | solution.py:98
  246.9 229.9 %all-gather.24.cloned.1.call-start = ((), (), s32[]{:S(2)}) async-start(), calls=%async_computation.28 | async-start | bytes 3932160 | tf_op jit(solution)/shard_map/all_gather | solution.py:98
  247.0 33.9 %copy-start.1 = (bf16[1,128,2048]{2,1,0:T(8,128)(2,1)S(1)}, bf16[1,128,2048]{2,1,0:T(8,128)(2,1)}, u32[]{:S(2)}) copy-start(bf16[1,128,2048]{2,1,0:T(8,128)(2,1)} %param.12) | copy-start | bytes 1572868
  264.6 276.1 %all-gather.26.cloned.1.call-start = ((), (), s32[]{:S(2)}) async-start(), calls=%async_computation.29 | async-start | bytes 3932160 | tf_op jit(solution)/shard_map/all_gather | solution.py:98
  280.8 297.8 %all-gather.18.cloned.1.call-start = ((), (), s32[]{:S(2)}) async-start(), calls=%async_computation.25 | async-start | bytes 4718592 | tf_op jit(solution)/shard_map/all_gather | solution.py:101
  284.3 393.0 %reduce-scatter.15.cloned.1.call-start = ((), (), s32[]{:S(2)}) async-start(), calls=%async_computation.31 | async-start | bytes 4718592 | tf_op jit(solution)/shard_map/reduce_scatter | solution.py:107
  591.8 10.6 copy-start.66
  591.8 10.6 copy-start.67
  597.1 10.9 copy-start.58
  597.1 10.9 copy-start.60
  625.8 51.5 %copy-start.2 = (bf16[128,2048]{1,0:T(8,128)(2,1)S(1)}, bf16[128,2048]{1,0:T(8,128)(2,1)}, u32[]{:S(2)}) copy-start(bf16[128,2048]{1,0:T(8,128)(2,1)} %reduce-scatter.11.cloned.1.call-done) | copy-start | bytes 1572868
  625.8 53.1 %copy-start.6 = (bf16[1,128,2048]{2,1,0:T(8,128)(2,1)S(1)}, bf16[1,128,2048]{2,1,0:T(8,128)(2,1)}, u32[]{:S(2)}) copy-start(bf16[1,128,2048]{2,1,0:T(8,128)(2,1)} %param.23) | copy-start | bytes 1572868
  625.8 55.5 %copy-start.68 = (bf16[1024,256]{0,1:T(8,128)(2,1)S(1)}, bf16[1024,256]{0,1:T(8,128)(2,1)}, u32[]{:S(2)}) copy-start(bf16[1024,256]{0,1:T(8,128)(2,1)} %copy-done.67) | copy-start | bytes 1572868
  625.8 93.1 %all-gather.28.cloned.1.call-start = ((), (), s32[]{:S(2)}) async-start(), calls=%async_computation.32 | async-start | bytes 4718592 | tf_op jit(solution)/shard_map/all_gather | solution.py:101
  681.2 104.7 %reduce-scatter.23.cloned.1.call-start = ((), (), s32[]{:S(2)}) async-start(), calls=%async_computation.36 | async-start | bytes 3932160 | tf_op jit(solution)/shard_map/reduce_scatter | solution.py:104
  690.6 152.6 %reduce-scatter.25.cloned.1.call-start = ((), (), s32[]{:S(2)}) async-start(), calls=%async_computation.37 | async-start | bytes 3932160 | tf_op jit(solution)/shard_map/reduce_scatter | solution.py:104
  699.8 205.8 %reduce-scatter.27.cloned.1.call-start = ((), (), s32[]{:S(2)}) async-start(), calls=%async_computation.38 | async-start | bytes 3932160 | tf_op jit(solution)/shard_map/reduce_scatter | solution.py:104
  709.3 258.8 %reduce-scatter.29.cloned.1.call-start = ((), (), s32[]{:S(2)}) async-start(), calls=%async_computation.39 | async-start | bytes 3932160 | tf_op jit(solution)/shard_map/reduce_scatter | solution.py:104
  718.6 279.4 %reduce-scatter.21.cloned.1.call-start = ((), (), s32[]{:S(2)}) async-start(), calls=%async_computation.35 | async-start | bytes 1310720 | tf_op jit(solution)/shard_map/reduce_scatter | solution.py:104
  743.7 327.9 %reduce-scatter.19.cloned.1.call-start = ((), (), s32[]{:S(2)}) async-start(), calls=%async_computation.34 | async-start | bytes 4915200 | tf_op jit(solution)/shard_map/reduce_scatter | solution.py:104
  744.0 8.8 copy-start.43
  761.0 366.0 %reduce-scatter.17.cloned.1.call-start = ((), (), s32[]{:S(2)}) async-start(), calls=%async_computation.33 | async-start | bytes 4718592 | tf_op jit(solution)/shard_map/reduce_scatter | solution.py:107
  761.8 419.8 %reduce-scatter.13.cloned.1.call-start = ((), (), s32[]{:S(2)}) async-start(), calls=%async_computation.30 | async-start | bytes 4718592 | tf_op jit(solution)/shard_map/reduce_scatter | solution.py:107
  764.6 5.8 copy-start.31
  770.5 5.8 copy-start.33
  788.2 57.2 %all-to-all-start.8 = ((bf16[8,64,768]{2,1,0:T(8,128)(2,1)}), bf16[8,64,768]{2,1,0:T(8,128)(2,1)S(1)}, u32[]{:S(2)}, u32[]{:S(2)}) async-start(bf16[8,64,768]{2,1,0:T(8,128)(2,1)} %bitcast.71), calls=%async_computation.15 | async-start | bytes 1572864 | tf_op jit(solution)/shard_map/all_to_all | solution.py:95
  845.4 129.2 %copy-start.57 = (u32[32]{0:T(128)S(1)}, u32[32]{0:T(128)}, u32[]{:S(2)}) copy-start(u32[32]{0:T(128)} %constant.37) | copy-start | bytes 388
  845.4 130.4 %copy-start.44 = (f32[1024]{0:T(1024)S(1)}, f32[1024]{0:T(1024)}, u32[]{:S(2)}) copy-start(f32[1024]{0:T(1024)} %get-tuple-element.63) | copy-start | bytes 12292
  845.4 62.5 %all-to-all-start.9 = ((bf16[8,64,768]{2,1,0:T(8,128)(2,1)}), bf16[8,64,768]{2,1,0:T(8,128)(2,1)S(1)}, u32[]{:S(2)}, u32[]{:S(2)}) async-start(bf16[8,64,768]{2,1,0:T(8,128)(2,1)} %bitcast.74), calls=%async_computation.17 | async-start | bytes 1572864 | tf_op jit(solution)/shard_map/all_to_all | solution.py:95
  907.9 62.5 %all-to-all-start.10 = ((bf16[8,64,768]{2,1,0:T(8,128)(2,1)}), bf16[8,64,768]{2,1,0:T(8,128)(2,1)S(1)}, u32[]{:S(2)}, u32[]{:S(2)}) async-start(bf16[8,64,768]{2,1,0:T(8,128)(2,1)} %bitcast.288), calls=%async_computation.19 | async-start | bytes 1572864 | tf_op jit(solution)/shard_map/all_to_all | solution.py:95
  970.4 23.8 %all-to-all-start.11 = ((bf16[8,64,768]{2,1,0:T(8,128)(2,1)}), bf16[8,64,768]{2,1,0:T(8,128)(2,1)}, u32[]{:S(2)}, u32[]{:S(2)}) async-start(bf16[8,64,768]{2,1,0:T(8,128)(2,1)} %bitcast.287), calls=%async_computation.21 | async-start | bytes 1572864 | tf_op jit(solution)/shard_map/all_to_all | solution.py:95
  998.0 22.3 %all-to-all-start.7 = ((bf16[8,64,256]{2,1,0:T(8,128)(2,1)}), bf16[8,64,256]{2,1,0:T(8,128)(2,1)S(1)}, u32[]{:S(2)}, u32[]{:S(2)}) async-start(bf16[8,64,256]{2,1,0:T(8,128)(2,1)} %bitcast.316), calls=%async_computation.13 | async-start | bytes 524288 | tf_op jit(solution)/shard_map/all_to_all | solution.py:95
  1020.3 161.3 %copy-start.5 = (bf16[128,2048]{1,0:T(8,128)(2,1)S(1)}, bf16[128,2048]{1,0:T(8,128)(2,1)}, u32[]{:S(2)}) copy-start(bf16[128,2048]{1,0:T(8,128)(2,1)} %reduce-scatter.15.cloned.1.call-done) | copy-start | bytes 1572868
  1020.3 161.3 %copy-start.7 = (bf16[1,128,2048]{2,1,0:T(8,128)(2,1)S(1)}, bf16[1,128,2048]{2,1,0:T(8,128)(2,1)}, u32[]{:S(2)}) copy-start(bf16[1,128,2048]{2,1,0:T(8,128)(2,1)} %param.23) | copy-start | bytes 1572868
  1071.6 113.0 %all-to-all-start.6 = ((bf16[8,80,768]{2,1,0:T(8,128)(2,1)}), bf16[8,80,768]{2,1,0:T(8,128)(2,1)S(1)}, u32[]{:S(2)}, u32[]{:S(2)}) async-start(bf16[8,80,768]{2,1,0:T(8,128)(2,1)} %bitcast.305), calls=%async_computation.11 | async-start | bytes 1966080 | tf_op jit(solution)/shard_map/all_to_all | solution.py:95
  (50 other events, 156.1 us)
Sparse Core Ops, SparseCore 0:
  31.6 75.7 all-gather.13
  109.3 35.2 all-gather.29
  146.7 27.9 all-gather.15
  179.6 66.0 reduce-scatter.10
  247.2 63.2 all-gather.19
  312.4 35.3 all-gather.31
  349.4 63.4 all-gather.21
  414.6 62.1 all-gather.23
  478.5 62.1 all-gather.25
  543.1 35.3 all-gather.17
  625.9 51.3 reduce-scatter.14
  681.3 36.7 all-gather.27
  720.4 60.2 reduce-scatter.22
  782.8 60.2 reduce-scatter.24
  845.3 60.2 reduce-scatter.26
  907.8 60.2 reduce-scatter.28
  970.8 27.1 reduce-scatter.20
  1000.3 71.3 reduce-scatter.18
  1075.3 51.6 reduce-scatter.16
  1130.3 51.2 reduce-scatter.12

commit v2 on v1

v2 whole, which is shorter than its diff:
```python
import functools
import math

import jax
import jax.numpy as jnp
from jax import lax
from jax.experimental import pallas as pl
from jax.experimental.pallas import tpu as pltpu
from jax.sharding import PartitionSpec as P

HD = 128
LANES = 128
epsilon = 1e-05
rope_base = 10000.0
score_bias = -math.log(4096.0)
score_scale = 1.0 / math.sqrt(HD)
f32 = jnp.float32
bf16 = jnp.bfloat16
CHUNKS = 2
TILE = 256
MIB = 1 << 20


def dot(left, right):
    return jnp.dot(left, right, preferred_element_type=f32)


def dot_t(left, right):
    return lax.dot_general(left, right, (((1,), (1,)), ((), ())), preferred_element_type=f32)


def t_dot(left, right):
    return lax.dot_general(left, right, (((0,), (0,)), ((), ())), preferred_element_type=f32)


def norm_scale(values):
    return lax.rsqrt(jnp.mean(values * values, axis=-1, keepdims=True) + epsilon)


def norm_back(grad_normed, unit_rows, scale_rows, gain_vec):
    grad_unit = grad_normed * gain_vec
    return scale_rows * (
        grad_unit - unit_rows * jnp.mean(grad_unit * unit_rows, axis=-1, keepdims=True)
    )


def columns(array, at, cols):
    return pl.BlockSpec((array.shape[0], cols), lambda *_: (0, at), pipeline_mode=pl.Buffered(1))


def whole(shape):
    zeros = (0,) * len(shape)
    return pl.BlockSpec(shape, lambda *_: zeros, pipeline_mode=pl.Buffered(1))


def rows_of(tile, cols):
    return pl.BlockSpec((tile, cols), lambda i, *_: (i, 0))


def call(kernel, steps, ins, in_specs, outs, out_specs, flops, vmem=60, scalars=0):
    size = sum(math.prod(a.shape) * a.dtype.itemsize for a in (*ins, *outs))
    result = pl.pallas_call(
        kernel,
        grid_spec=pltpu.PrefetchScalarGridSpec(
            num_scalar_prefetch=scalars,
            grid=(steps,),
            in_specs=in_specs,
            out_specs=out_specs,
        ),
        out_shape=outs,
        compiler_params=pltpu.CompilerParams(
            dimension_semantics=("arbitrary",), vmem_limit_bytes=vmem * MIB
        ),
        cost_estimate=pl.CostEstimate(flops=flops, bytes_accessed=size, transcendentals=0),
    )(*ins)
    return result[0] if len(outs) == 1 else result


def pack_kernel(plans, *refs):
    ins, outs = refs[: -len(plans)], refs[-len(plans) :]
    for plan, out_ref in zip(plans, outs):
        at = 0
        for m, part, parts in plan:
            cols = ins[m].shape[1] // parts
            value = ins[m][:, part * cols : (part + 1) * cols]
            out_ref[0, :, at : at + cols] = value.astype(bf16)
            at += cols


def pack(arrays, plans, ns, marks=None):
    rows = arrays[0].shape[0]
    specs = [pl.BlockSpec((rows, a.shape[1] // ns), lambda i: (0, i)) for a in arrays]
    widths = [a.shape[1] // ns for a in arrays]
    if marks is not None:
        plans = [plan + [(len(arrays), 0, 1)] for plan in plans]
        arrays = arrays + (marks,)
        specs.append(whole(marks.shape))
        widths.append(marks.shape[1])
    cols = [sum(widths[m] // parts for m, _, parts in plan) for plan in plans]
    return call(
        functools.partial(pack_kernel, plans),
        ns,
        arrays,
        specs,
        [jax.ShapeDtypeStruct((ns, rows, n), bf16) for n in cols],
        [pl.BlockSpec((1, rows, n), lambda i: (i, 0, 0)) for n in cols],
        0,
    )


def turn(values, cosine, sine):
    return values * cosine + pltpu.roll(values, HD // 2, 1) * sine


def attend_kernel(
    heads_all, q_ref, k_ref, v_ref, cos_ref, sin_ref, col_ref, row_ref, qo, ko, vo, oo, mo
):
    length = q_ref.shape[0]
    tile = min(TILE, length)
    cosine, sine = cos_ref[...], sin_ref[...]
    queries = turn(q_ref[...], cosine, sine).astype(bf16)
    keys = turn(k_ref[...], cosine, sine).astype(bf16)
    values = v_ref[...].astype(bf16)
    qo[...] = queries
    ko[...] = keys
    vo[...] = values
    first = pl.program_id(0) == 0
    for i in range(length // tile):
        at = slice(i * tile, (i + 1) * tile)
        scores = dot_t(queries[at], keys) * score_scale + score_bias
        visible = row_ref[...] <= col_ref[at, :]
        weights = jnp.where(visible, jax.nn.sigmoid(scores), 0.0)
        oo[at, :] = dot(weights.astype(bf16), values).astype(bf16)
        mass = jnp.sum(weights, axis=1, keepdims=True) * (1.0 / heads_all)
        mass = jnp.broadcast_to(mass, (tile, LANES))
        mo[at, :] = jnp.where(first, mass, mo[at, :] + mass)


def attend(qkv, cosine, sine, pos_col, pos_row, heads, heads_all):
    length = qkv.shape[0]
    part = lambda j: pl.BlockSpec((length, HD), lambda i, j=j: (0, i + j * heads))
    out = jax.ShapeDtypeStruct((length, heads * HD), bf16)
    return call(
        functools.partial(attend_kernel, heads_all),
        heads,
        (qkv, qkv, qkv, cosine, sine, pos_col, pos_row),
        [part(0), part(1), part(2)]
        + [whole(a.shape) for a in (cosine, sine, pos_col, pos_row)],
        [out] * 4 + [jax.ShapeDtypeStruct((length, LANES), f32)],
        [part(0)] * 4 + [pl.BlockSpec((length, LANES), lambda i: (0, 0))],
        4 * heads * length * length * HD,
    )


def halves(length, cols):
    tile = min(TILE, length // 2)
    count = length // 2 // tile
    shape = jax.ShapeDtypeStruct((length // 2, cols), bf16)
    return tile, 2 * count, [shape] * 2, pair_specs(length, cols, tile)


def pair_specs(length, cols, tile):
    count = length // 2 // tile
    return [
        pl.BlockSpec((tile, cols), lambda i, *_: (jnp.minimum(i, count - 1), 0)),
        pl.BlockSpec((tile, cols), lambda i, *_: (jnp.maximum(i - count, 0), 0)),
    ]


def either(pair):
    first = pl.program_id(0) < pl.num_programs(0) // 2
    return jnp.where(first, pair[0][...], pair[1][...])


def store_half(value, outs):
    first = pl.program_id(0) < pl.num_programs(0) // 2

    @pl.when(first)
    def _():
        outs[0][...] = value

    @pl.when(jnp.logical_not(first))
    def _():
        outs[1][...] = value


def project_kernel(o_ref, m_ref, w_ref, *outs):
    value = dot_t(o_ref[...], w_ref[...]).astype(bf16)
    store_half(jnp.concatenate([value, m_ref[...].astype(bf16)], axis=1), outs)


def project(attended, mass, w_qko):
    length, cols = attended.shape
    width = w_qko.shape[0]
    tile, steps, outs, specs = halves(length, width + LANES)
    return call(
        project_kernel,
        steps,
        (attended, mass, w_qko),
        [rows_of(tile, cols), rows_of(tile, LANES), columns(w_qko, 2, cols)],
        outs,
        specs,
        2 * length * cols * width,
    )


def enter_kernel(a_ref, b_ref, gain_ref, wq_ref, wk_ref, wv_ref, qkv_ref, n_ref):
    rows = either((a_ref, b_ref)).astype(f32)
    normed = (rows * norm_scale(rows) * gain_ref[...]).astype(bf16)
    n_ref[...] = normed
    cols = wq_ref.shape[1]
    for i, ref in enumerate((wq_ref, wk_ref, wv_ref)):
        qkv_ref[:, i * cols : (i + 1) * cols] = dot(normed, ref[...])


def enter(x_pair, gain, w_qko, w_v):
    length, width = 2 * x_pair[0].shape[0], x_pair[0].shape[1]
    one = w_v.shape[1]
    cols = 3 * one
    tile = min(TILE, length // 2)
    return call(
        enter_kernel,
        length // tile,
        (*x_pair, gain, w_qko, w_qko, w_v),
        pair_specs(length, width, tile)
        + [whole(gain.shape), columns(w_qko, 0, one), columns(w_qko, 1, one), whole(w_v.shape)],
        [
            jax.ShapeDtypeStruct((length, cols), f32),
            jax.ShapeDtypeStruct((length, width), bf16),
        ],
        [rows_of(tile, cols), rows_of(tile, width)],
        2 * length * width * cols,
    )


def ffn_kernel(na_ref, nb_ref, da_ref, db_ref, w_ref, act_ref, back_ref):
    cols = act_ref.shape[1]
    gated = dot(either((na_ref, nb_ref)), w_ref[:, : 2 * cols])
    grad_act = dot(either((da_ref, db_ref)), w_ref[:, 2 * cols :])
    gate, up = gated[:, :cols], gated[:, cols:]
    sig = jax.nn.sigmoid(gate)
    silu = gate * sig
    act_ref[...] = (silu * up).astype(bf16)
    back_ref[:, :cols] = (grad_act * up * sig * (1.0 + gate * (1.0 - sig))).astype(bf16)
    back_ref[:, cols:] = (grad_act * silu).astype(bf16)


def ffn(n_pair, d_pair, w):
    length, width = 2 * n_pair[0].shape[0], n_pair[0].shape[1]
    cols = w.shape[1] // 3
    tile = min(2 * TILE, length // 2)
    return call(
        ffn_kernel,
        length // tile,
        (*n_pair, *d_pair, w),
        pair_specs(length, width, tile) * 2 + [whole(w.shape)],
        [
            jax.ShapeDtypeStruct((length, cols), bf16),
            jax.ShapeDtypeStruct((length, 2 * cols), bf16),
        ],
        [rows_of(tile, cols), rows_of(tile, 2 * cols)],
        6 * length * width * cols,
    )


def cols_of(length, tile):
    return pl.BlockSpec((length, tile), lambda i, *_: (0, i))


def t_dot_pair(pair, right):
    half = pair[0].shape[0]
    return t_dot(pair[0][...], right[:half, :]) + t_dot(pair[1][...], right[half:, :])


def ffn_sums_kernel(na_ref, nb_ref, da_ref, db_ref, act_ref, back_ref, w_ref, sum_ref, gain_ref):
    cols = act_ref.shape[1]
    gated = t_dot_pair((na_ref, nb_ref), back_ref)
    sum_ref[:, : 2 * cols] = gated.astype(bf16)
    sum_ref[:, 2 * cols :] = t_dot_pair((da_ref, db_ref), act_ref).astype(bf16)
    gain = jnp.sum(gated * w_ref[:, : 2 * cols].astype(f32), axis=1, keepdims=True)
    gain_ref[...] = jnp.broadcast_to(gain, gain_ref.shape)


def ffn_sums(n_pair, d_pair, act, back, w):
    half, width = n_pair[0].shape
    cols = act.shape[1]
    tile = min(2 * TILE, width)
    return call(
        ffn_sums_kernel,
        width // tile,
        (*n_pair, *d_pair, act, back, w),
        [cols_of(half, tile)] * 4
        + [whole(act.shape), whole(back.shape), rows_of(tile, 3 * cols)],
        [
            jax.ShapeDtypeStruct((width, 3 * cols), bf16),
            jax.ShapeDtypeStruct((width, LANES), f32),
        ],
        [rows_of(tile, 3 * cols), rows_of(tile, LANES)],
        12 * half * width * cols,
    )


def branch_kernel(a_ref, b_ref, w_ref, out_ref):
    out_ref[...] = dot(either((a_ref, b_ref)), w_ref[...]).astype(bf16)


def branch_back(pair, w_qko):
    length, width = 2 * pair[0].shape[0], pair[0].shape[1]
    cols = w_qko.shape[1] // 3
    tile = min(TILE, length // 2)
    return call(
        branch_kernel,
        length // tile,
        (*pair, w_qko),
        pair_specs(length, width, tile) + [columns(w_qko, 2, cols)],
        [jax.ShapeDtypeStruct((length, cols), bf16)],
        [rows_of(tile, cols)],
        2 * length * width * cols,
    )


def branch_sums_kernel(a_ref, b_ref, o_ref, sum_ref):
    sum_ref[...] = t_dot_pair((a_ref, b_ref), o_ref).astype(bf16)


def branch_sums(pair, attended):
    half, width = pair[0].shape
    cols = attended.shape[1]
    tile = min(2 * TILE, width)
    return call(
        branch_sums_kernel,
        width // tile,
        (*pair, attended),
        [cols_of(half, tile)] * 2 + [whole(attended.shape)],
        [jax.ShapeDtypeStruct((width, cols), bf16)],
        [rows_of(tile, cols)],
        4 * half * width * cols,
    )


def back_kernel(count, first, *refs):
    lefts, rights, outs = refs[:count], refs[count : 2 * count], refs[2 * count :]
    total = 0.0
    for left, right in zip(lefts, rights):
        cols = left.shape[1]
        total = total + dot_t(left[...], right[:, first : first + cols])
    store_half(total.astype(bf16), outs)


def enter_back(lefts, w_qko, w_v):
    length, cols = lefts[0].shape
    width = w_v.shape[0]
    tile, steps, outs, specs = halves(length, width)
    return call(
        functools.partial(back_kernel, 3, 0),
        steps,
        (*lefts, w_qko, w_qko, w_v),
        [rows_of(tile, cols)] * 3
        + [columns(w_qko, 0, cols), columns(w_qko, 1, cols), whole(w_v.shape)],
        outs,
        specs,
        6 * length * width * cols,
    )


def back(lefts, rights, first=0):
    length = lefts[0].shape[0]
    width = rights[0].shape[0]
    tile, steps, outs, specs = halves(length, width)
    return call(
        functools.partial(back_kernel, len(lefts), first),
        steps,
        (*lefts, *rights),
        [rows_of(tile, a.shape[1]) for a in lefts] + [whole(a.shape) for a in rights],
        outs,
        specs,
        2 * length * width * sum(a.shape[1] for a in lefts),
    )


def attend_back_kernel(q_ref, k_ref, v_ref, g_ref, cos_ref, sin_ref, col_ref, row_ref, dq, dk, dv):
    length = q_ref.shape[0]
    tile = min(TILE, length)
    cosine, sine = cos_ref[...], -sin_ref[...]
    queries, keys, values, grads = q_ref[...], k_ref[...], v_ref[...], g_ref[...]
    grad_keys = grad_values = 0.0
    for i in range(length // tile):
        at = slice(i * tile, (i + 1) * tile)
        scores = dot_t(keys, queries[at]) * score_scale + score_bias
        visible = col_ref[...] <= row_ref[:, at]
        weights = jnp.where(visible, jax.nn.sigmoid(scores), 0.0)
        grad_weights = dot_t(values, grads[at])
        grad_scores = (grad_weights * weights * (1.0 - weights)).astype(bf16)
        grad_values = grad_values + dot(weights.astype(bf16), grads[at])
        grad_keys = grad_keys + dot(grad_scores, queries[at])
        grad_query = t_dot(grad_scores, keys) * score_scale
        dq[at, :] = turn(grad_query, cosine[at], sine[at]).astype(bf16)
    dk[...] = turn(grad_keys * score_scale, cosine, sine).astype(bf16)
    dv[...] = grad_values.astype(bf16)


def attend_back(queries, keys, values, grads, cosine, sine, pos_col, pos_row):
    length, cols = queries.shape
    heads = cols // HD
    part = pl.BlockSpec((length, HD), lambda i: (0, i))
    out = jax.ShapeDtypeStruct((length, cols), bf16)
    return call(
        attend_back_kernel,
        heads,
        (queries, keys, values, grads, cosine, sine, pos_col, pos_row),
        [part] * 4 + [whole(a.shape) for a in (cosine, sine, pos_col, pos_row)],
        [out] * 3,
        [part] * 3,
        10 * heads * length * length * HD,
    )


def qkv_sums_kernel(n_ref, dq, dk, dv, wq_ref, wk_ref, wv_ref, other_ref, out_ref):
    cols = dq.shape[1]
    gain = 0.0
    for i, (ref, w) in enumerate(((dq, wq_ref), (dk, wk_ref), (dv, wv_ref))):
        part = t_dot(n_ref[...], ref[...])
        out_ref[:, i * cols : (i + 1) * cols] = part.astype(bf16)
        gain = gain + jnp.sum(part * w[...].astype(f32), axis=1, keepdims=True)
    lane = lax.broadcasted_iota(jnp.int32, other_ref.shape, 1)
    gains = jnp.where(lane == 0, gain, other_ref[...])
    out_ref[:, 3 * cols :] = gains.astype(bf16)


def qkv_sums(normed, dq, dk, dv, w_qko, w_v, other):
    length, width = normed.shape
    cols = dq.shape[1]
    tile = min(2 * TILE, width)
    return call(
        qkv_sums_kernel,
        width // tile,
        (normed, dq, dk, dv, w_qko, w_qko, w_v, other),
        [cols_of(length, tile)]
        + [whole(a.shape) for a in (dq, dk, dv)]
        + [pl.BlockSpec((tile, cols), lambda i, at=at: (i, at)) for at in (0, 1, 0)]
        + [rows_of(tile, LANES)],
        [jax.ShapeDtypeStruct((width, 3 * cols + LANES), bf16)],
        [rows_of(tile, 3 * cols + LANES)],
        6 * length * width * cols,
    )


def unpack_kernel(count, parts, *refs):
    ins, outs = refs[:count], refs[count:]
    cols = outs[0].shape[1] // count
    for c, ref in enumerate(ins):
        for i in range(parts):
            outs[i][:, c * cols : (c + 1) * cols] = ref[0, :, i * cols : (i + 1) * cols].astype(f32)
    for i, out in enumerate(outs[parts:]):
        step = pl.program_id(0)
        part = ref[0, :, parts * cols :].astype(f32)
        out[...] = jnp.where(step == 0, part, out[...] + part)


def unpack(blocks, parts, extra=False):
    ns, rows, cols = blocks[0].shape
    cols = (cols - LANES * extra) // parts
    outs = [jax.ShapeDtypeStruct((rows, ns * len(blocks) * cols), f32)] * parts
    specs = [pl.BlockSpec((rows, len(blocks) * cols), lambda i: (0, i))] * parts
    if extra:
        outs = outs + [jax.ShapeDtypeStruct((rows, LANES), f32)]
        specs = specs + [pl.BlockSpec((rows, LANES), lambda i: (0, 0))]
    return call(
        functools.partial(unpack_kernel, len(blocks), parts),
        ns,
        tuple(blocks),
        [pl.BlockSpec((1,) + a.shape[1:], lambda i: (i, 0, 0)) for a in blocks],
        outs,
        specs,
        0,
    )


def swap_bit(block, bit, size):
    return lax.ppermute(block, "seq", [(i, i ^ bit) for i in range(size)])


def link_bits(size):
    bits = []
    bit = 2
    while bit < size:
        bits.append(bit)
        bit *= 2
    return bits


def orders(size):
    bits = link_bits(size)
    found = []
    for run in (bits, bits[::-1]):
        order = [0]
        for bit in run:
            order += [k ^ bit for k in order]
        found.append(order)
    return found


def swap_side(block):
    return lax.ppermute(block, "side", [(0, 1), (1, 0)])


def exchange(moves, waits=()):
    blocks = lax.optimization_barrier([b for b, _ in moves])
    got = [f(b) for (_, f), b in zip(moves, blocks)]
    got, values = lax.optimization_barrier((got, [box[i] for box, i in waits]))
    for (box, i), value in zip(waits, values):
        box[i] = value
    return got


def along(bit):
    return functools.partial(swap_bit, bit=bit, size=lax.axis_size("seq"))


def gather_steps(held):
    bits = link_bits(lax.axis_size("seq"))
    for pair in zip(bits, bits[::-1]):
        got = yield [(block, along(bit)) for block, bit in zip(held, pair)]
        held = [jnp.concatenate(pieces, axis=0) for pieces in zip(held, got)]
    side = jnp.concatenate(held, axis=0)
    (got,) = yield [(side, along(1))]
    return side, got


def scatter_steps(keep, away):
    bits = link_bits(lax.axis_size("seq"))
    (got,) = yield [(away, along(1))]
    length = keep.shape[0] // 2
    terms = [[t[i * length : (i + 1) * length] for t in (keep, got)] for i in range(2)]

    def total(parts, start, stop):
        return sum(t[start:stop].astype(f32) for t in parts)

    for pair in zip(bits[::-1], bits):
        sent = [total(parts, length // 2, length).astype(bf16) for parts in terms]
        got = yield [(block, along(bit)) for block, bit in zip(sent, pair)]
        length //= 2
        for parts, block in zip(terms, got):
            parts.append(block)
    return [total(parts, 0, length) for parts in terms]


def gather_one(own):
    half = own.shape[0] // 2
    return (yield from gather_steps([own[:half], own[half:]]))


def scatter_one(pair):
    blocks = yield from scatter_steps(*pair)
    return jnp.concatenate(blocks, axis=0)


def gather_two(own):
    (got,) = yield [(own, swap_side)]
    return (yield from gather_steps([own, got]))


def scatter_two(pair):
    mine, other = yield from scatter_steps(*pair)
    (got,) = yield [(other.astype(bf16), swap_side)]
    return mine + got.astype(f32)


class Ride:
    def __init__(self, steps):
        self.steps = steps
        self.result = None
        self.feed(None)

    def feed(self, got):
        try:
            self.moves = self.steps.send(got)
        except StopIteration as end:
            self.moves, self.result = None, end.value


def run(steps, riders=(), waits=()):
    main = Ride(steps)
    waits = list(waits)
    while main.moves is not None:
        active = [main] + [rider for rider in riders if rider.moves is not None]
        got = exchange(
            [move for ride in active for move in ride.moves], waits.pop(0) if waits else ()
        )
        for ride in active:
            part, got = got[: len(ride.moves)], got[len(ride.moves) :]
            ride.feed(part)
    return main.result


def body(
    tokens,
    positions,
    gain_attn,
    query_weight,
    key_weight,
    value_weight,
    out_weight,
    gain_ffn,
    gate_weight,
    up_weight,
    down_weight,
    cotangent,
):
    ns = lax.axis_size("seq")
    nb = lax.axis_size("pair") * lax.axis_size("side")
    batch = ("pair", "side")
    near = ("side", "seq")
    rows, width = query_weight.shape
    hidden = gate_weight.shape[1]
    head_cols = width // ns
    heads = head_cols // HD
    ffn_cols = hidden // (2 * ns * CHUNKS)
    own = tokens.shape[1]

    def swap(blocks, axes="seq"):
        return lax.all_to_all(blocks, axes, split_axis=0, concat_axis=0, tiled=True)

    def gather_z(block, axes=batch):
        return lax.all_gather(block, axes, axis=0, tiled=True)

    def scatter_z(full, axes=batch):
        return lax.psum_scatter(full, axes, scatter_dimension=0, tiled=True)

    low_gains = [gain_attn.astype(bf16), gain_ffn.astype(bf16)]
    gain_cols = jnp.pad(jnp.stack(low_gains, axis=1), ((0, 0), (0, LANES - 2)))
    w_v = gather_z(jnp.concatenate([value_weight.astype(bf16), gain_cols], axis=1))

    place = positions[0]
    marks = jnp.stack([place // 128, place % 128]).astype(bf16)
    marks = jnp.pad(marks.reshape(2, -1, LANES)[:, 0], ((0, rows - 2), (0, 0)))
    attn_blocks = pack(
        (query_weight, key_weight, out_weight.T.astype(bf16)),
        [[(m, 0, 1) for m in range(3)]],
        ns,
        marks,
    )
    attn_blocks = swap(attn_blocks)
    plans = [[(m, c, CHUNKS) for m in range(3)] for c in range(CHUNKS)]
    ffn_blocks = list(pack((gate_weight, up_weight, down_weight.T.astype(bf16)), plans, 2 * ns))
    x_own, attn_blocks = lax.optimization_barrier((tokens[0], attn_blocks))
    x_all = run(gather_one(x_own))
    w_v = w_v.reshape(nb, rows, -1)
    spread = jnp.broadcast_to(w_v[None, :, :, width:], (ns, nb, rows, LANES))
    w_v = w_v[:, :, :width].reshape(nb, rows, ns, head_cols).transpose(2, 0, 1, 3)
    w_v = swap(jnp.concatenate([w_v, spread], axis=3))
    w_v = w_v.transpose(1, 0, 2, 3).reshape(width, -1)
    gain_one = w_v[:, head_cols].astype(f32)
    gain_two = w_v[:, head_cols + 1].astype(f32)
    w_v = w_v[:, :head_cols]

    around = jnp.array([[[k ^ core for k in order] for order in orders(ns)] for core in range(2)])
    around = lax.axis_index("seq") ^ around.astype(jnp.int32)
    place = attn_blocks[:, :2, -LANES:].astype(f32).astype(jnp.int32)
    place = (place[:, 0] * 128 + place[:, 1]).reshape(ns, 2, own // 2)
    place = jnp.stack([jnp.take(place[:, i], around[:, i], axis=0) for i in range(2)], axis=1)
    place = place.reshape(-1)
    half_size = HD // 2
    frequency = jnp.exp(jnp.arange(half_size).astype(f32) * (-2.0 * math.log(rope_base) / HD))
    angles = place.astype(f32)[:, None] * frequency[None, :]
    cosine, sine = jnp.cos(angles), jnp.sin(angles)
    cosine = jnp.concatenate([cosine, cosine], axis=1)
    sine = jnp.concatenate([-sine, sine], axis=1)
    pos_col, pos_row = place[:, None], place[None, :]

    attn_blocks = attn_blocks.reshape(ns * rows, -1)
    w_qko = gather_z(attn_blocks[:, : 3 * head_cols])
    (w_qko, w_v, gain_one, x_all, cosine, sine, pos_col, pos_row, ffn_blocks[0]) = (
        lax.optimization_barrier(
            (w_qko, w_v, gain_one, x_all, cosine, sine, pos_col, pos_row, ffn_blocks[0])
        )
    )
    ffn_blocks[0] = swap(ffn_blocks[0], near).reshape(2 * ns * rows, -1)

    qkv, normed = enter(x_all, gain_one[None], w_qko, w_v)
    queries, keys, values, attended, mass = attend(
        qkv, cosine, sine, pos_col, pos_row, heads, width // HD
    )
    attended, ffn_blocks = lax.optimization_barrier((attended, ffn_blocks))
    ffn_blocks[0], ffn_blocks[1] = lax.optimization_barrier((ffn_blocks[0], ffn_blocks[1]))
    ffn_blocks[1] = swap(ffn_blocks[1], near).reshape(2 * ns * rows, -1)
    w_ffn = [gather_z(block, "pair") for block in ffn_blocks]
    dy_ride = Ride(gather_two(cotangent[0]))
    attn_own = run(
        scatter_one(project(attended, mass, w_qko)), [dy_ride], [[], [(w_ffn, 0)]]
    )
    attn_mass = attn_own[:, width]
    x_own_f = x_own.astype(f32)
    hidden_own = x_own_f + attn_own[:, :width]
    scale_two = norm_scale(hidden_own)
    unit_two = hidden_own * scale_two
    normed_ffn = run(
        gather_two((unit_two * gain_two).astype(bf16)),
        [dy_ride],
        [[], [], [(w_ffn, 1)]],
    )
    dy_all = dy_ride.result

    acts, backs, sums, gain_sums = [], [], [], []
    for c in range(CHUNKS):
        act, grads = ffn(normed_ffn, dy_all, w_ffn[c])
        if c + 1 == CHUNKS:
            grads_pair = back(backs + [grads], w_ffn)
            act, grads_pair = lax.optimization_barrier((act, grads_pair))
        part, gains = ffn_sums(normed_ffn, dy_all, act, grads, w_ffn[c])
        if c + 1 < CHUNKS:
            act, grads, part, w_ffn[c + 1] = lax.optimization_barrier(
                (act, grads, part, w_ffn[c + 1])
            )
        acts.append(act)
        backs.append(grads)
        sums.append(scatter_z(part, "pair"))
        gain_sums.append(gains)
    gain_sums = sum(gain_sums)
    grad_normed_two = run(scatter_two(grads_pair), (), [[], [], [(sums, 0)]])
    grad_hidden = cotangent[0].astype(f32) + norm_back(
        grad_normed_two, unit_two, scale_two, gain_two
    )

    def home(part, axes="seq"):
        return swap(part.reshape(lax.axis_size(axes), rows, -1), axes)

    branch = run(gather_one(grad_hidden.astype(bf16)), (), [[], [(sums, 1)]])
    out_sum = branch_sums(branch, attended)
    branch, out_sum = lax.optimization_barrier((branch, out_sum))
    out_sum = scatter_z(out_sum)
    grad_heads = branch_back(branch, w_qko)
    dq, dk, dv = attend_back(queries, keys, values, grad_heads, cosine, sine, pos_col, pos_row)
    ffn_sum = [home(sums[0], near)]
    dq, ffn_sum = lax.optimization_barrier((dq, ffn_sum))
    qkv_local = qkv_sums(normed, dq, dk, dv, w_qko, w_v, gain_sums)
    dq, dk, dv, qkv_local = lax.optimization_barrier((dq, dk, dv, qkv_local))
    qkv_sum = scatter_z(qkv_local)
    part = enter_back([dq, dk, dv], w_qko, w_v)
    part, acts = lax.optimization_barrier((part, acts))
    out_ride = Ride(scatter_two(back(acts, w_ffn, 2 * ffn_cols)))
    grad_normed = run(scatter_one(part), [out_ride])
    (got,) = exchange(out_ride.moves)
    out_ride.feed([got])
    layer_out = (hidden_own + out_ride.result).astype(bf16)
    ffn_sum.append(home(sums[1], near))
    scale_one = norm_scale(x_own_f)
    input_grad = (
        grad_hidden + norm_back(grad_normed, x_own_f * scale_one, scale_one, gain_one)
    ).astype(bf16)

    gate_grad, up_grad, down_grad = unpack(ffn_sum, 3)
    out_grad = unpack([home(out_sum)], 1).T
    down_grad = down_grad.T
    gate_grad, up_grad, down_grad, out_grad, qkv_sum = lax.optimization_barrier(
        (gate_grad, up_grad, down_grad, out_grad, qkv_sum)
    )
    query_grad, key_grad, value_grad, gains = unpack([home(qkv_sum)], 3, True)
    return (
        layer_out[None],
        input_grad[None],
        attn_mass[None],
        gains[:, 0] / low_gains[0].astype(f32),
        query_grad,
        key_grad,
        value_grad,
        out_grad,
        gains[:, 1] / low_gains[1].astype(f32),
        gate_grad,
        up_grad,
        down_grad,
    )


def solution(mesh):
    nb, ns = mesh.shape["batch"], mesh.shape["seq"]
    mesh = jax.sharding.Mesh(mesh.devices.reshape(nb // 2, 2, ns), ("pair", "side", "seq"))
    batch = ("pair", "side")
    both = ("pair", "side", "seq")
    token_spec = P(batch, "seq", None)
    row_spec = P(both, None)
    col_spec = P(None, both)
    return jax.shard_map(
        body,
        mesh=mesh,
        in_specs=(
            token_spec,
            P(batch, "seq"),
            P(both),
            row_spec,
            row_spec,
            row_spec,
            col_spec,
            P(both),
            row_spec,
            row_spec,
            col_spec,
            token_spec,
        ),
        out_specs=(
            token_spec,
            token_spec,
            P(batch, "seq"),
            P(both),
            row_spec,
            row_spec,
            row_spec,
            col_spec,
            P(both),
            row_spec,
            row_spec,
            col_spec,
        ),
        check_vma=False,
    )
```

time: 1200 us -> 761 us (0.63)
  waiting for transfers between devices: 746 us -> 369 us
  Pallas kernels: 0 us -> 178 us
  matrix products: 163 us -> 0 us
  blocking collectives: 125 us -> 25.1 us
  starting transfers between devices: 28.3 us -> 64.2 us
  local copies, waits for them, and re-layouts: 63.2 us -> 36.6 us
    reduce_scatter x10 -> x4, waiting for transfers between devices: 372 us -> 19.3 us  [scatter_z(): return lax.psum_scatter(full, axes, scatter_dimension=0, tiled=True)]
    all_gather x10 -> x4, waiting for transfers between devices: 372 us -> 79.5 us  [gather_z(): return lax.all_gather(block, axes, axis=0, tiled=True)]
    ppermute x0 -> x44, waiting for transfers between devices: none -> 231 us  [the longest x40 168 us: swap_bit(): return lax.ppermute(block, 'seq', [(i, i ^ bit) for i in range(size)])]
    pallas_call x0 -> x19, Pallas kernels: none -> 178 us  [call(): pl.pallas_call(kernel, grid_spec=pltpu.PrefetchScalarGridSpec(num_scalar_...]
    dot_general x44 -> x0, matrix products: 163 us -> none  [the longest x10 62.9 us: dot_t(): lax.dot_general(left, right, (((1,), (1,)), ((), ())), preferred_element_...]
    all_to_all x5 -> x1, blocking collectives: 97 us -> 25.1 us  [swap(): return lax.all_to_all(blocks, axes, split_axis=0, concat_axis=0, tiled=True)]
    all_to_all x7, waiting for transfers between devices: 0.02 us -> 38.6 us  [swap(): return lax.all_to_all(blocks, axes, split_axis=0, concat_axis=0, tiled=True)]
    ppermute x0 -> x44, starting transfers between devices: none -> 34.1 us  [the longest x40 32.8 us: swap_bit(): return lax.ppermute(block, 'seq', [(i, i ^ bit) for i in range(size)])]
  transfers between devices with their start and end apart: 27 -> 59, of which waited for: 17 -> 30; matrix products, arithmetic and copies ran while one was open for 17% -> 10% of each run, Pallas kernels for 0% -> 16%
where the time goes in v2:
time: 761 us; the launch traced here: 750 us
  waiting for transfers between devices  369 us (48%)
  Pallas kernels  178 us (23%)
  starting transfers between devices  64.2 us (8%)
  other arithmetic  62 us (8%)
  local copies, waits for them, and re-layouts  36.6 us (5%)
  blocking collectives  25.1 us (3%)
  between operations  15.2 us (2%)
    pallas_call x19, Pallas kernels, call(): pl.pallas_call(kernel, grid_spec=pltpu.PrefetchScalarGridSpec(num_scalar_...  178 us
    ppermute x40, waiting for transfers between devices, swap_bit(): return lax.ppermute(block, 'seq', [(i, i ^ bit) for i in range(size)])  168 us
    all_gather x4, waiting for transfers between devices, gather_z(): return lax.all_gather(block, axes, axis=0, tiled=True)  79.5 us
    ppermute x4, waiting for transfers between devices, swap_side(): return lax.ppermute(block, 'side', [(0, 1), (1, 0)])  63.8 us
    all_to_all x7, waiting for transfers between devices, swap(): return lax.all_to_all(blocks, axes, split_axis=0, concat_axis=0, tiled=True)  38.6 us
    ppermute x40, starting transfers between devices, swap_bit(): return lax.ppermute(block, 'seq', [(i, i ^ bit) for i in range(size)])  32.8 us
    all_to_all x7, starting transfers between devices, swap(): return lax.all_to_all(blocks, axes, split_axis=0, concat_axis=0, tiled=True)  29.1 us
    all_to_all x1, blocking collectives, swap(): return lax.all_to_all(blocks, axes, split_axis=0, concat_axis=0, tiled=True)  25.1 us
  transfers between devices with their start and end apart: 59, of which 30 were waited for; matrix products, arithmetic and copies ran while one was open for 10% of the time, Pallas kernels for 16%

profile of v2, /device:TPU:0, one launch (start us, length us, event | category | flops | bytes accessed | tf_op | source)
XLA Modules:
  0.0 750.2 jit_solution(4627593687649180156)
XLA Ops:
  12.9 5.0 shard_map.220
  17.9 5.3 all-to-all-start
  26.0 11.2 %all-to-all-done = bf16[8,64,896]{2,1,0:T(8,128)(2,1)S(1)} async-done(((bf16[8,64,896]{2,1,0:T(8,128)(2,1)}), bf16[8,64,896]{2,1,0:T(8,128)(2,1)S(1)}, u32[]{:S(2)}, u32[]{:S(2)}) %all-to-all-start) | async-done | bytes 917536 | tf_op jit(solution)/shard_map/all_to_all | solution.py:622
  40.3 10.2 %shard_map.221 = (bf16[16,64,768]{2,1,0:T(8,128)(2,1)}, bf16[16,64,768]{2,1,0:T(8,128)(2,1)}) custom-call(f32[64,8192]{1,0:T(8,128)} %refs_0_.3, f32[64,8192]{1,0:T(8,128)} %refs_1_.3, bf16[64,8192]{1,0:T(8,128)(2,1)} %convert_bitcast_fusion.refs_2_), custom_call_target="tpu_custom_call" | custom-call | bytes 8388608 | tf_op jit(solution)/shard_map/pallas_call | solution.py:62
  54.4 9.5 %collective-permute-done.2 = bf16[128,2048]{1,0:T(8,128)(2,1)S(1)} collective-permute-done((bf16[128,2048]{1,0:T(8,128)(2,1)S(1)}, bf16[128,2048]{1,0:T(8,128)(2,1)S(1)}, u32[]{:S(2)}, u32[]{:S(2)}) %collective-permute-start.2) | collective-permute-done | bytes 524320 | tf_op jit(solution)/shard_map/ppermute | solution.py:480
  72.6 3.6 all-to-all-start.1
  82.4 14.8 %all-to-all-done.1 = bf16[8,4,64,384]{3,2,1,0:T(8,128)(2,1)S(1)} async-done(((bf16[8,4,64,384]{3,2,1,0:T(8,128)(2,1)}), bf16[8,4,64,384]{3,2,1,0:T(8,128)(2,1)S(1)}, u32[]{:S(2)}, u32[]{:S(2)}) %all-to-all-start.1) | async-done | bytes 1572896 | tf_op jit(solution)/shard_map/all_to_all | solution.py:622
  99.5 7.0 all-gather.5.cloned.1.call-done.wq_ref.wk_ref.w_ref.refs_3_.refs_4_
  106.5 3.8 all-to-all-start.2
  111.3 9.0 %shard_map.222 = (f32[1024,768]{1,0:T(8,128)}, bf16[1024,2048]{1,0:T(8,128)(2,1)}) custom-call(bf16[512,2048]{1,0:T(8,128)(2,1)} %constant_dynamic-update-slice_fusion.a_ref, bf16[512,2048]{1,0:T(8,128)(2,1)} %collective-permute-done.4.b_ref, f32[1,2048]{1,0:T(1,128)} %bitcast.88, ...), custom_call_target="tpu_custom_call" | custom-call | flops 3221225472 | bytes 18882560 | tf_op jit(solution)/shard_map/pallas_call | solution.py:62
  120.3 7.0 shard_map.223
  127.4 5.7 all-to-all-done.2
  133.0 6.5 shard_map.224
  140.4 17.9 %collective-permute-done.6 = bf16[128,2048]{1,0:T(8,128)(2,1)S(1)} collective-permute-done((bf16[128,2048]{1,0:T(8,128)(2,1)S(1)}, bf16[128,2048]{1,0:T(8,128)(2,1)S(1)}, u32[]{:S(2)}, u32[]{:S(2)}) %collective-permute-start.6) | collective-permute-done | bytes 524320 | tf_op jit(solution)/shard_map/ppermute | solution.py:504
  164.2 21.9 %collective-permute-done.9 = bf16[128,2048]{1,0:T(8,128)(2,1)S(1)} collective-permute-done((bf16[128,2048]{1,0:T(8,128)(2,1)S(1)}, bf16[128,2048]{1,0:T(8,128)(2,1)S(1)}, u32[]{:S(2)}, u32[]{:S(2)}) %collective-permute-start.9) | collective-permute-done | bytes 524320 | tf_op jit(solution)/shard_map/ppermute | solution.py:480
  186.2 32.2 %all-gather.9.cloned.1.call-done.w_ref.refs_2_ = bf16[2048,768]{1,0:T(8,128)(2,1)} async-done(((bf16[1024,768]{1,0:T(8,128)(2,1)}), bf16[2048,768]{1,0:T(8,128)(2,1)}) %all-gather.9.cloned.1.call-update) | async-done | bytes 3145744 | tf_op jit(solution)/shard_map/all_gather | solution.py:625
  225.8 26.3 %collective-permute-done.11 = bf16[64,2176]{1,0:T(8,128)(2,1)S(1)} collective-permute-done((bf16[64,2176]{1,0:T(8,128)(2,1)S(1)}, bf16[64,2176]{1,0:T(8,128)(2,1)S(1)}, u32[]{:S(2)}, u32[]{:S(2)}) %collective-permute-start.11) | collective-permute-done | bytes 278560 | tf_op jit(solution)/shard_map/ppermute | solution.py:480
  258.9 25.1 %all_to_all.40 = bf16[16,64,768]{2,1,0:T(8,128)(2,1)} all-to-all(bf16[16,64,768]{2,1,0:T(8,128)(2,1)S(1)} %copy-done.10), channel_id=1, replica_groups=mesh['pair'=2,'side'=2,'seq'=8] {'side','seq'}, dimensions={0} | all-to-all | bytes 3145728 | tf_op jit(solution)/shard_map/all_to_all | solution.py:622
  284.7 17.8 %collective-permute-done.15 = bf16[128,2048]{1,0:T(8,128)(2,1)S(1)} collective-permute-done((bf16[128,2048]{1,0:T(8,128)(2,1)S(1)}, bf16[128,2048]{1,0:T(8,128)(2,1)S(1)}, u32[]{:S(2)}, u32[]{:S(2)}) %collective-permute-start.15) | collective-permute-done | bytes 524320 | tf_op jit(solution)/shard_map/ppermute | solution.py:504
  303.1 10.0 %collective-permute-done.17 = bf16[128,2048]{1,0:T(8,128)(2,1)S(1)} collective-permute-done((bf16[128,2048]{1,0:T(8,128)(2,1)S(1)}, bf16[128,2048]{1,0:T(8,128)(2,1)S(1)}, u32[]{:S(2)}, u32[]{:S(2)}) %collective-permute-start.17) | collective-permute-done | bytes 524320 | tf_op jit(solution)/shard_map/ppermute | solution.py:480
  320.3 40.3 %all-gather.11.cloned.1.call-done.w_ref.refs_3_ = bf16[2048,768]{1,0:T(8,128)(2,1)} async-done(((bf16[1024,768]{1,0:T(8,128)(2,1)}), bf16[2048,768]{1,0:T(8,128)(2,1)}) %all-gather.11.cloned.1.call-update) | async-done | bytes 3145744 | tf_op jit(solution)/shard_map/all_gather | solution.py:625
  366.9 7.5 collective-permute-done.21.nb_ref
  374.4 13.4 %shard_map.225 = (bf16[2048,256]{1,0:T(8,128)(2,1)}, bf16[2048,512]{1,0:T(8,128)(2,1)}) custom-call(bf16[1024,2048]{1,0:T(8,128)(2,1)} %constant_dynamic-update-slice_fusion.12.na_ref, bf16[1024,2048]{1,0:T(8,128)(2,1)} %collective-permute-done.21.nb_ref, bf16[1024,2048]{1,0:T(8,128)(2,1)} %constant_dynamic-update-slice_fusion.6.da_ref, ...), custom_call_target="tpu_custom_call" | custom-call | flops 6442450944 | bytes 23068672 | tf_op jit(solution)/shard_map/pallas_call | solution.py:62
  387.8 14.0 %shard_map.226 = (bf16[2048,768]{1,0:T(8,128)(2,1)}, f32[2048,128]{1,0:T(8,128)}) custom-call(bf16[1024,2048]{1,0:T(8,128)(2,1)} %constant_dynamic-update-slice_fusion.12.na_ref, bf16[1024,2048]{1,0:T(8,128)(2,1)} %collective-permute-done.21.nb_ref, bf16[1024,2048]{1,0:T(8,128)(2,1)} %constant_dynamic-update-slice_fusion.6.da_ref, ...), custom_call_target="tpu_custom_call" | custom-call | flops 6442450944 | bytes 27262976 | tf_op jit(solution)/shard_map/pallas_call | solution.py:62
  402.1 13.5 %shard_map.227 = (bf16[2048,256]{1,0:T(8,128)(2,1)}, bf16[2048,512]{1,0:T(8,128)(2,1)}) custom-call(bf16[1024,2048]{1,0:T(8,128)(2,1)} %constant_dynamic-update-slice_fusion.12.na_ref, bf16[1024,2048]{1,0:T(8,128)(2,1)} %collective-permute-done.21.nb_ref, bf16[1024,2048]{1,0:T(8,128)(2,1)} %constant_dynamic-update-slice_fusion.6.da_ref, ...), custom_call_target="tpu_custom_call" | custom-call | flops 6442450944 | bytes 23068672 | tf_op jit(solution)/shard_map/pallas_call | solution.py:62
  415.6 15.8 %shard_map.228 = (bf16[1024,2048]{1,0:T(8,128)(2,1)}, bf16[1024,2048]{1,0:T(8,128)(2,1)}) custom-call(bf16[2048,512]{1,0:T(8,128)(2,1)} %get-tuple-element.244.back_ref.refs_0_, bf16[2048,512]{1,0:T(8,128)(2,1)} %get-tuple-element.245.refs_1_.back_ref, bf16[2048,768]{1,0:T(8,128)(2,1)} %all-gather.9.cloned.1.call-done.w_ref.refs_2_, ...), custom_call_target="tpu_custom_call" | custom-call | flops 8589934592 | bytes 18874368 | tf_op jit(solution)/shard_map/pallas_call | solution.py:62
  431.4 13.9 %shard_map.229 = (bf16[2048,768]{1,0:T(8,128)(2,1)}, f32[2048,128]{1,0:T(8,128)}) custom-call(bf16[1024,2048]{1,0:T(8,128)(2,1)} %constant_dynamic-update-slice_fusion.12.na_ref, bf16[1024,2048]{1,0:T(8,128)(2,1)} %collective-permute-done.21.nb_ref, bf16[1024,2048]{1,0:T(8,128)(2,1)} %constant_dynamic-update-slice_fusion.6.da_ref, ...), custom_call_target="tpu_custom_call" | custom-call | flops 6442450944 | bytes 27262976 | tf_op jit(solution)/shard_map/pallas_call | solution.py:62
  451.5 22.5 %collective-permute-done.23 = bf16[256,2048]{1,0:T(8,128)(2,1)S(1)} collective-permute-done((bf16[256,2048]{1,0:T(8,128)(2,1)S(1)}, bf16[256,2048]{1,0:T(8,128)(2,1)S(1)}, u32[]{:S(2)}, u32[]{:S(2)}) %collective-permute-start.23) | collective-permute-done | bytes 1048608 | tf_op jit(solution)/shard_map/ppermute | solution.py:480
  479.7 11.2 %collective-permute-done.25 = bf16[128,2048]{1,0:T(8,128)(2,1)S(1)} collective-permute-done((bf16[128,2048]{1,0:T(8,128)(2,1)S(1)}, bf16[128,2048]{1,0:T(8,128)(2,1)S(1)}, u32[]{:S(2)}, u32[]{:S(2)}) %collective-permute-start.25) | collective-permute-done | bytes 524320 | tf_op jit(solution)/shard_map/ppermute | solution.py:480
  494.1 22.7 %collective-permute-done.27 = bf16[128,2048]{1,0:T(8,128)(2,1)S(1)} collective-permute-done((bf16[128,2048]{1,0:T(8,128)(2,1)S(1)}, bf16[128,2048]{1,0:T(8,128)(2,1)S(1)}, u32[]{:S(2)}, u32[]{:S(2)}) %collective-permute-start.27) | collective-permute-done | bytes 524320 | tf_op jit(solution)/shard_map/ppermute | solution.py:504
  523.7 5.0 collective-permute-done.28
  533.1 4.8 all-to-all-start.4
  538.9 19.3 %reduce-scatter.7.cloned.1.call-done = bf16[1024,768]{1,0:T(8,128)(2,1)} async-done(((bf16[2048,768]{1,0:T(8,128)(2,1)}), bf16[1024,768]{1,0:T(8,128)(2,1)}) %reduce-scatter.7.cloned.1.call-update) | async-done | bytes 1572880 | tf_op jit(solution)/shard_map/reduce_scatter | solution.py:628
  568.1 5.0 shard_map.230
  573.1 5.3 shard_map.231.g_ref
  578.4 9.7 %shard_map.232 = (bf16[1024,256]{1,0:T(8,128)(2,1)}, bf16[1024,256]{1,0:T(8,128)(2,1)}, bf16[1024,256]{1,0:T(8,128)(2,1)}) custom-call(bf16[1024,256]{1,0:T(8,128)(2,1)} %get-tuple-element.219.q_ref, bf16[1024,256]{1,0:T(8,128)(2,1)} %get-tuple-element.220.k_ref, bf16[1024,256]{1,0:T(8,128)(2,1)} %get-tuple-element.221.v_ref, ...), custom_call_target="tpu_custom_call" | custom-call | flops 2684354560 | bytes 4726784 | tf_op jit(solution)/shard_map/pallas_call | solution.py:62
  588.1 8.7 %shard_map.233 = bf16[2048,896]{1,0:T(8,128)(2,1)} custom-call(bf16[1024,2048]{1,0:T(8,128)(2,1)} %get-tuple-element.276.n_ref, bf16[1024,256]{1,0:T(8,128)(2,1)} %get-tuple-element.279.dq.refs_0_, bf16[1024,256]{1,0:T(8,128)(2,1)} %get-tuple-element.280.dk.refs_1_, bf16[1024,256]{1,0:T(8,128)(2,1)} %get-tuple-element.281.dv.refs_2_, ...), custom_call_target="tpu_custom_call" | custom-call | flops 3221225472 | bytes 17825792 | tf_op jit(solution)/shard_map/pallas_call | solution.py:62
  596.8 8.3 %shard_map.234 = (bf16[512,2048]{1,0:T(8,128)(2,1)}, bf16[512,2048]{1,0:T(8,128)(2,1)}) custom-call(bf16[1024,256]{1,0:T(8,128)(2,1)} %get-tuple-element.279.dq.refs_0_, bf16[1024,256]{1,0:T(8,128)(2,1)} %get-tuple-element.280.dk.refs_1_, bf16[1024,256]{1,0:T(8,128)(2,1)} %get-tuple-element.281.dv.refs_2_, ...), custom_call_target="tpu_custom_call" | custom-call | flops 3221225472 | bytes 13107200 | tf_op jit(solution)/shard_map/pallas_call | solution.py:62
  605.2 12.6 %shard_map.235 = (bf16[1024,2048]{1,0:T(8,128)(2,1)}, bf16[1024,2048]{1,0:T(8,128)(2,1)}) custom-call(bf16[2048,256]{1,0:T(8,128)(2,1)} %get-tuple-element.285.act_ref.refs_0_, bf16[2048,256]{1,0:T(8,128)(2,1)} %get-tuple-element.286.act_ref.refs_1_, bf16[2048,768]{1,0:T(8,128)(2,1)} %all-gather.9.cloned.1.call-done.w_ref.refs_2_, ...), custom_call_target="tpu_custom_call" | custom-call | flops 4294967296 | bytes 16777216 | tf_op jit(solution)/shard_map/pallas_call | solution.py:62
  618.4 3.7 all-to-all-start.5
  622.1 6.3 collective-permute-done.33
  637.7 38.8 %collective-permute-done.35 = bf16[128,2048]{1,0:T(8,128)(2,1)S(1)} collective-permute-done((bf16[128,2048]{1,0:T(8,128)(2,1)S(1)}, bf16[128,2048]{1,0:T(8,128)(2,1)S(1)}, u32[]{:S(2)}, u32[]{:S(2)}) %collective-permute-start.35) | collective-permute-done | bytes 524320 | tf_op jit(solution)/shard_map/ppermute | solution.py:480
  687.4 4.4 all-to-all-start.6
  693.2 10.4 %shard_map.236 = (f32[64,8192]{1,0:T(8,128)}, f32[64,8192]{1,0:T(8,128)}, f32[64,8192]{1,0:T(8,128)}) custom-call(bf16[16,64,768]{2,1,0:T(8,128)(2,1)} %all-to-all-done.4.refs_0_, bf16[16,64,768]{2,1,0:T(8,128)(2,1)} %copy-done.2), custom_call_target="tpu_custom_call" | custom-call | bytes 9437184 | tf_op jit(solution)/shard_map/pallas_call | solution.py:62
  703.6 3.7 all-to-all-done.6.refs_0_
  708.0 4.4 shard_map.237
  723.1 5.5 collective-permute-done.43
  735.5 5.3 shard_map.238
  (247 shorter events, 149.5 us)
Async XLA Ops:
  7.2 61.2 %all-gather.7.cloned.1.call-start = ((), (), s32[]{:S(2)}) async-start(), calls=%async_computation.13 | async-start | bytes 1392640 | tf_op jit(solution)/shard_map/all_gather | solution.py:625
  17.9 19.3 %all-to-all-start = ((bf16[8,64,896]{2,1,0:T(8,128)(2,1)}), bf16[8,64,896]{2,1,0:T(8,128)(2,1)S(1)}, u32[]{:S(2)}, u32[]{:S(2)}) async-start(bf16[8,64,896]{2,1,0:T(8,128)(2,1)} %shard_map.220), calls=%async_computation | async-start | bytes 1835008 | tf_op jit(solution)/shard_map/all_to_all | solution.py:622
  23.2 83.2 %all-gather.5.cloned.1.call-start = ((), (), s32[]{:S(2)}) async-start(), calls=%async_computation.12 | async-start | bytes 3932160 | tf_op jit(solution)/shard_map/all_gather | solution.py:625
  50.7 13.2 %collective-permute-start.2 = (bf16[128,2048]{1,0:T(8,128)(2,1)S(1)}, bf16[128,2048]{1,0:T(8,128)(2,1)S(1)}, u32[]{:S(2)}, u32[]{:S(2)}) collective-permute-start(bf16[128,2048]{1,0:T(8,128)(2,1)S(1)} %get-tuple-element.176), channel_id=1, source_target_pairs={{0,4},{1,5},{2,6},{3,7},{4,0},{5,1},{6,2},{7,3},{8,12},{9,13},{10,... | collective-permute-start | bytes 1572872 | tf_op jit(solution)/shard_map/ppermute | solution.py:480
  52.1 13.1 %collective-permute-start.3 = (bf16[128,2048]{1,0:T(8,128)(2,1)S(1)}, bf16[128,2048]{1,0:T(8,128)(2,1)S(1)}, u32[]{:S(2)}, u32[]{:S(2)}) collective-permute-start(bf16[128,2048]{1,0:T(8,128)(2,1)S(1)} %get-tuple-element.177), channel_id=1, source_target_pairs={{0,2},{1,3},{2,0},{3,1},{4,6},{5,7},{6,4},{7,5},{8,10},{9,11},{10,... | collective-permute-start | bytes 1572872 | tf_op jit(solution)/shard_map/ppermute | solution.py:480
  68.3 31.2 %collective-permute-start.4 = (bf16[512,2048]{1,0:T(8,128)(2,1)}, bf16[512,2048]{1,0:T(8,128)(2,1)}, u32[]{:S(2)}, u32[]{:S(2)}) collective-permute-start(bf16[512,2048]{1,0:T(8,128)(2,1)} %constant_dynamic-update-slice_fusion.a_ref), channel_id=1, source_target_pairs={{0,1},{1,0},{2,3},{3,2},{4,5},{5,4},{6,7},{7,6},{8,9},{9,8},{10,11... | collective-permute-start | bytes 6291464 | tf_op jit(solution)/shard_map/ppermute | solution.py:480
  72.6 24.5 %all-to-all-start.1 = ((bf16[8,4,64,384]{3,2,1,0:T(8,128)(2,1)}), bf16[8,4,64,384]{3,2,1,0:T(8,128)(2,1)S(1)}, u32[]{:S(2)}, u32[]{:S(2)}) async-start(bf16[8,4,64,384]{3,2,1,0:T(8,128)(2,1)} %copy.35), calls=%async_computation.1 | async-start | bytes 3145728 | tf_op jit(solution)/shard_map/all_to_all | solution.py:622
  106.5 26.5 %all-to-all-start.2 = ((bf16[16,64,768]{2,1,0:T(8,128)(2,1)}), bf16[16,64,768]{2,1,0:T(8,128)(2,1)S(1)}, u32[]{:S(2)}, u32[]{:S(2)}) async-start(bf16[16,64,768]{2,1,0:T(8,128)(2,1)} %get-tuple-element.192), calls=%async_computation.2 | async-start | bytes 3145728 | tf_op jit(solution)/shard_map/all_to_all | solution.py:622
  110.2 108.1 %all-gather.9.cloned.1.call-start = ((), (), s32[]{:S(2)}) async-start(), calls=%async_computation.14 | async-start | bytes 4718592 | tf_op jit(solution)/shard_map/all_gather | solution.py:625
  139.6 18.7 %collective-permute-start.5 = (bf16[512,2176]{1,0:T(8,128)(2,1)}, bf16[512,2176]{1,0:T(8,128)(2,1)}, u32[]{:S(2)}, u32[]{:S(2)}) collective-permute-start(bf16[512,2176]{1,0:T(8,128)(2,1)} %get-tuple-element.198), channel_id=1, source_target_pairs={{0,1},{1,0},{2,3},{3,2},{4,5},{5,4},{6,7},{7,6},{8,9},{9,8},{10,11... | collective-permute-start | bytes 6684680 | tf_op jit(solution)/shard_map/ppermute | solution.py:480
  139.6 221.0 %all-gather.11.cloned.1.call-start = ((), (), s32[]{:S(2)}) async-start(), calls=%async_computation.15 | async-start | bytes 4718592 | tf_op jit(solution)/shard_map/all_gather | solution.py:625
  139.8 18.5 %collective-permute-start.6 = (bf16[128,2048]{1,0:T(8,128)(2,1)S(1)}, bf16[128,2048]{1,0:T(8,128)(2,1)S(1)}, u32[]{:S(2)}, u32[]{:S(2)}) collective-permute-start(bf16[128,2048]{1,0:T(8,128)(2,1)S(1)} %bitcast.73), channel_id=1, source_target_pairs={{0,8},{8,0},{1,9},{9,1},{2,10},{10,2},{3,11},{11,3},{4,12},{12,4},... | collective-permute-start | bytes 1572872 | tf_op jit(solution)/shard_map/ppermute | solution.py:504
  160.1 26.0 %collective-permute-start.7 = (bf16[128,2176]{1,0:T(8,128)(2,1)S(1)}, bf16[128,2176]{1,0:T(8,128)(2,1)S(1)}, u32[]{:S(2)}, u32[]{:S(2)}) collective-permute-start(bf16[128,2176]{1,0:T(8,128)(2,1)S(1)} %get-tuple-element.202), channel_id=1, source_target_pairs={{0,4},{1,5},{2,6},{3,7},{4,0},{5,1},{6,2},{7,3},{8,12},{9,13},{10,... | collective-permute-start | bytes 1671176 | tf_op jit(solution)/shard_map/ppermute | solution.py:480
  161.0 25.2 %collective-permute-start.8 = (bf16[128,2176]{1,0:T(8,128)(2,1)S(1)}, bf16[128,2176]{1,0:T(8,128)(2,1)}, u32[]{:S(2)}, u32[]{:S(2)}) collective-permute-start(bf16[128,2176]{1,0:T(8,128)(2,1)S(1)} %get-tuple-element.203), channel_id=1, source_target_pairs={{0,2},{1,3},{2,0},{3,1},{4,6},{5,7},{6,4},{7,5},{8,10},{9,11},{10,... | collective-permute-start | bytes 1671176 | tf_op jit(solution)/shard_map/ppermute | solution.py:480
  162.3 23.9 %collective-permute-start.9 = (bf16[128,2048]{1,0:T(8,128)(2,1)S(1)}, bf16[128,2048]{1,0:T(8,128)(2,1)S(1)}, u32[]{:S(2)}, u32[]{:S(2)}) collective-permute-start(bf16[128,2048]{1,0:T(8,128)(2,1)S(1)} %bitcast.74), channel_id=1, source_target_pairs={{0,2},{1,3},{2,0},{3,1},{4,6},{5,7},{6,4},{7,5},{8,10},{9,11},{10,... | collective-permute-start | bytes 1572872 | tf_op jit(solution)/shard_map/ppermute | solution.py:480
  163.0 23.1 %collective-permute-start.10 = (bf16[128,2048]{1,0:T(8,128)(2,1)S(1)}, bf16[128,2048]{1,0:T(8,128)(2,1)S(1)}, u32[]{:S(2)}, u32[]{:S(2)}) collective-permute-start(bf16[128,2048]{1,0:T(8,128)(2,1)S(1)} %collective-permute-done.6), channel_id=1, source_target_pairs={{0,4},{1,5},{2,6},{3,7},{4,0},{5,1},{6,2},{7,3},{8,12},{9,13},{10,... | collective-permute-start | bytes 1572872 | tf_op jit(solution)/shard_map/ppermute | solution.py:480
  220.0 32.1 %collective-permute-start.13 = (bf16[256,2048]{1,0:T(8,128)(2,1)S(1)}, bf16[256,2048]{1,0:T(8,128)(2,1)S(1)}, u32[]{:S(2)}, u32[]{:S(2)}) collective-permute-start(bf16[256,2048]{1,0:T(8,128)(2,1)S(1)} %pad_maximum_fusion.1), channel_id=1, source_target_pairs={{0,4},{1,5},{2,6},{3,7},{4,0},{5,1},{6,2},{7,3},{8,12},{9,13},{10,... | collective-permute-start | bytes 3145736 | tf_op jit(solution)/shard_map/ppermute | solution.py:480
  221.6 30.6 %collective-permute-start.14 = (bf16[256,2048]{1,0:T(8,128)(2,1)S(1)}, bf16[256,2048]{1,0:T(8,128)(2,1)S(1)}, u32[]{:S(2)}, u32[]{:S(2)}) collective-permute-start(bf16[256,2048]{1,0:T(8,128)(2,1)S(1)} %pad_maximum_fusion.2), channel_id=1, source_target_pairs={{0,2},{1,3},{2,0},{3,1},{4,6},{5,7},{6,4},{7,5},{8,10},{9,11},{10,... | collective-permute-start | bytes 3145736 | tf_op jit(solution)/shard_map/ppermute | solution.py:480
  223.0 29.1 %collective-permute-start.11 = (bf16[64,2176]{1,0:T(8,128)(2,1)S(1)}, bf16[64,2176]{1,0:T(8,128)(2,1)S(1)}, u32[]{:S(2)}, u32[]{:S(2)}) collective-permute-start(bf16[64,2176]{1,0:T(8,128)(2,1)S(1)} %get-tuple-element.213), channel_id=1, source_target_pairs={{0,2},{1,3},{2,0},{3,1},{4,6},{5,7},{6,4},{7,5},{8,10},{9,11},{10,... | collective-permute-start | bytes 835592 | tf_op jit(solution)/shard_map/ppermute | solution.py:480
  223.6 28.6 %collective-permute-start.12 = (bf16[64,2176]{1,0:T(8,128)(2,1)S(1)}, bf16[64,2176]{1,0:T(8,128)(2,1)S(1)}, u32[]{:S(2)}, u32[]{:S(2)}) collective-permute-start(bf16[64,2176]{1,0:T(8,128)(2,1)S(1)} %get-tuple-element.214), channel_id=1, source_target_pairs={{0,4},{1,5},{2,6},{3,7},{4,0},{5,1},{6,2},{7,3},{8,12},{9,13},{10,... | collective-permute-start | bytes 835592 | tf_op jit(solution)/shard_map/ppermute | solution.py:480
  258.9 43.6 %collective-permute-start.16 = (bf16[1024,2048]{1,0:T(8,128)(2,1)}, bf16[1024,2048]{1,0:T(8,128)(2,1)}, u32[]{:S(2)}, u32[]{:S(2)}) collective-permute-start(bf16[1024,2048]{1,0:T(8,128)(2,1)} %constant_dynamic-update-slice_fusion.6.da_ref), channel_id=1, source_target_pairs={{0,1},{1,0},{2,3},{3,2},{4,5},{5,4},{6,7},{7,6},{8,9},{9,8},{10,11... | collective-permute-start | bytes 12582920 | tf_op jit(solution)/shard_map/ppermute | solution.py:480
  284.0 208.2 %reduce-scatter.5.cloned.1.call-start = ((), (), s32[]{:S(2)}) async-start(), calls=%async_computation.16 | async-start | bytes 4718592 | tf_op jit(solution)/shard_map/reduce_scatter | solution.py:628
  284.0 18.4 %collective-permute-start.15 = (bf16[128,2048]{1,0:T(8,128)(2,1)S(1)}, bf16[128,2048]{1,0:T(8,128)(2,1)S(1)}, u32[]{:S(2)}, u32[]{:S(2)}) collective-permute-start(bf16[128,2048]{1,0:T(8,128)(2,1)S(1)} %get-tuple-element.227), channel_id=1, source_target_pairs={{0,8},{8,0},{1,9},{9,1},{2,10},{10,2},{3,11},{11,3},{4,12},{12,4},... | collective-permute-start | bytes 1572872 | tf_op jit(solution)/shard_map/ppermute | solution.py:504
  316.9 43.7 %collective-permute-start.19 = (bf16[256,2048]{1,0:T(8,128)(2,1)}, bf16[256,2048]{1,0:T(8,128)(2,1)}, u32[]{:S(2)}, u32[]{:S(2)}) collective-permute-start(bf16[256,2048]{1,0:T(8,128)(2,1)} %pad_maximum_fusion.3), channel_id=1, source_target_pairs={{0,4},{1,5},{2,6},{3,7},{4,0},{5,1},{6,2},{7,3},{8,12},{9,13},{10,... | collective-permute-start | bytes 3145736 | tf_op jit(solution)/shard_map/ppermute | solution.py:480
  318.6 42.0 %collective-permute-start.20 = (bf16[256,2048]{1,0:T(8,128)(2,1)}, bf16[256,2048]{1,0:T(8,128)(2,1)}, u32[]{:S(2)}, u32[]{:S(2)}) collective-permute-start(bf16[256,2048]{1,0:T(8,128)(2,1)} %pad_maximum_fusion.4), channel_id=1, source_target_pairs={{0,2},{1,3},{2,0},{3,1},{4,6},{5,7},{6,4},{7,5},{8,10},{9,11},{10,... | collective-permute-start | bytes 3145736 | tf_op jit(solution)/shard_map/ppermute | solution.py:480
  401.8 156.4 %reduce-scatter.7.cloned.1.call-start = ((), (), s32[]{:S(2)}) async-start(), calls=%async_computation.17 | async-start | bytes 4718592 | tf_op jit(solution)/shard_map/reduce_scatter | solution.py:628
  431.4 14.0 %collective-permute-start.22 = (bf16[1024,2048]{1,0:T(8,128)(2,1)}, bf16[1024,2048]{1,0:T(8,128)(2,1)}, u32[]{:S(2)}, u32[]{:S(2)}) collective-permute-start(bf16[1024,2048]{1,0:T(8,128)(2,1)} %get-tuple-element.249), channel_id=1, source_target_pairs={{0,1},{1,0},{2,3},{3,2},{4,5},{5,4},{6,7},{7,6},{8,9},{9,8},{10,11... | collective-permute-start | bytes 12582920 | tf_op jit(solution)/shard_map/ppermute | solution.py:480
  448.5 25.6 %collective-permute-start.23 = (bf16[256,2048]{1,0:T(8,128)(2,1)S(1)}, bf16[256,2048]{1,0:T(8,128)(2,1)S(1)}, u32[]{:S(2)}, u32[]{:S(2)}) collective-permute-start(bf16[256,2048]{1,0:T(8,128)(2,1)S(1)} %get-tuple-element.250), channel_id=1, source_target_pairs={{0,4},{1,5},{2,6},{3,7},{4,0},{5,1},{6,2},{7,3},{8,12},{9,13},{10,... | collective-permute-start | bytes 3145736 | tf_op jit(solution)/shard_map/ppermute | solution.py:480
  450.0 25.1 %collective-permute-start.24 = (bf16[256,2048]{1,0:T(8,128)(2,1)S(1)}, bf16[256,2048]{1,0:T(8,128)(2,1)S(1)}, u32[]{:S(2)}, u32[]{:S(2)}) collective-permute-start(bf16[256,2048]{1,0:T(8,128)(2,1)S(1)} %get-tuple-element.251), channel_id=1, source_target_pairs={{0,2},{1,3},{2,0},{3,1},{4,6},{5,7},{6,4},{7,5},{8,10},{9,11},{10,... | collective-permute-start | bytes 3145736 | tf_op jit(solution)/shard_map/ppermute | solution.py:480
  477.6 13.2 %collective-permute-start.25 = (bf16[128,2048]{1,0:T(8,128)(2,1)S(1)}, bf16[128,2048]{1,0:T(8,128)(2,1)S(1)}, u32[]{:S(2)}, u32[]{:S(2)}) collective-permute-start(bf16[128,2048]{1,0:T(8,128)(2,1)S(1)} %get-tuple-element.254), channel_id=1, source_target_pairs={{0,2},{1,3},{2,0},{3,1},{4,6},{5,7},{6,4},{7,5},{8,10},{9,11},{10,... | collective-permute-start | bytes 1572872 | tf_op jit(solution)/shard_map/ppermute | solution.py:480
  494.0 22.7 %collective-permute-start.27 = (bf16[128,2048]{1,0:T(8,128)(2,1)S(1)}, bf16[128,2048]{1,0:T(8,128)(2,1)S(1)}, u32[]{:S(2)}, u32[]{:S(2)}) collective-permute-start(bf16[128,2048]{1,0:T(8,128)(2,1)S(1)} %add_convert_fusion.12), channel_id=1, source_target_pairs={{0,8},{8,0},{1,9},{9,1},{2,10},{10,2},{3,11},{11,3},{4,12},{12,4},... | collective-permute-start | bytes 1572872 | tf_op jit(solution)/shard_map/ppermute | solution.py:504
  531.0 27.2 %collective-permute-start.30 = (bf16[128,2048]{1,0:T(8,128)(2,1)}, bf16[128,2048]{1,0:T(8,128)(2,1)}, u32[]{:S(2)}, u32[]{:S(2)}) collective-permute-start(bf16[128,2048]{1,0:T(8,128)(2,1)} %pad_maximum_fusion.9), channel_id=1, source_target_pairs={{0,4},{1,5},{2,6},{3,7},{4,0},{5,1},{6,2},{7,3},{8,12},{9,13},{10,... | collective-permute-start | bytes 1572872 | tf_op jit(solution)/shard_map/ppermute | solution.py:480
  531.7 26.5 %collective-permute-start.31 = (bf16[128,2048]{1,0:T(8,128)(2,1)}, bf16[128,2048]{1,0:T(8,128)(2,1)S(1)}, u32[]{:S(2)}, u32[]{:S(2)}) collective-permute-start(bf16[128,2048]{1,0:T(8,128)(2,1)} %pad_maximum_fusion.10), channel_id=1, source_target_pairs={{0,2},{1,3},{2,0},{3,1},{4,6},{5,7},{6,4},{7,5},{8,10},{9,11},{10,... | collective-permute-start | bytes 1572872 | tf_op jit(solution)/shard_map/ppermute | solution.py:480
  533.1 55.0 %all-to-all-start.4 = ((bf16[16,64,768]{2,1,0:T(8,128)(2,1)}), bf16[16,64,768]{2,1,0:T(8,128)(2,1)}, u32[]{:S(2)}, u32[]{:S(2)}) async-start(bf16[16,64,768]{2,1,0:T(8,128)(2,1)} %bitcast.80), calls=%async_computation.6 | async-start | bytes 3145728 | tf_op jit(solution)/shard_map/all_to_all | solution.py:622
  537.9 149.5 %reduce-scatter.9.cloned.1.call-start = ((), (), s32[]{:S(2)}) async-start(), calls=%async_computation.18 | async-start | bytes 1310720 | tf_op jit(solution)/shard_map/reduce_scatter | solution.py:628
  605.1 112.0 %reduce-scatter.11.cloned.1.call-start = ((), (), s32[]{:S(2)}) async-start(), calls=%async_computation.19 | async-start | bytes 4587520 | tf_op jit(solution)/shard_map/reduce_scatter | solution.py:628
  618.4 69.0 %all-to-all-start.5 = ((bf16[16,64,768]{2,1,0:T(8,128)(2,1)}), bf16[16,64,768]{2,1,0:T(8,128)(2,1)S(1)}, u32[]{:S(2)}, u32[]{:S(2)}) async-start(bf16[16,64,768]{2,1,0:T(8,128)(2,1)} %bitcast.79), calls=%async_computation.7 | async-start | bytes 3145728 | tf_op jit(solution)/shard_map/all_to_all | solution.py:622
  633.5 43.7 %collective-permute-start.37 = (bf16[256,2048]{1,0:T(8,128)(2,1)S(1)}, bf16[256,2048]{1,0:T(8,128)(2,1)S(1)}, u32[]{:S(2)}, u32[]{:S(2)}) collective-permute-start(bf16[256,2048]{1,0:T(8,128)(2,1)S(1)} %get-tuple-element.297), channel_id=1, source_target_pairs={{0,4},{1,5},{2,6},{3,7},{4,0},{5,1},{6,2},{7,3},{8,12},{9,13},{10,... | collective-permute-start | bytes 3145736 | tf_op jit(solution)/shard_map/ppermute | solution.py:480
  635.1 42.1 %collective-permute-start.38 = (bf16[256,2048]{1,0:T(8,128)(2,1)S(1)}, bf16[256,2048]{1,0:T(8,128)(2,1)S(1)}, u32[]{:S(2)}, u32[]{:S(2)}) collective-permute-start(bf16[256,2048]{1,0:T(8,128)(2,1)S(1)} %get-tuple-element.298), channel_id=1, source_target_pairs={{0,2},{1,3},{2,0},{3,1},{4,6},{5,7},{6,4},{7,5},{8,10},{9,11},{10,... | collective-permute-start | bytes 3145736 | tf_op jit(solution)/shard_map/ppermute | solution.py:480
  636.5 39.9 %collective-permute-start.35 = (bf16[128,2048]{1,0:T(8,128)(2,1)S(1)}, bf16[128,2048]{1,0:T(8,128)(2,1)S(1)}, u32[]{:S(2)}, u32[]{:S(2)}) collective-permute-start(bf16[128,2048]{1,0:T(8,128)(2,1)S(1)} %get-tuple-element.295), channel_id=1, source_target_pairs={{0,4},{1,5},{2,6},{3,7},{4,0},{5,1},{6,2},{7,3},{8,12},{9,13},{10,... | collective-permute-start | bytes 1572872 | tf_op jit(solution)/shard_map/ppermute | solution.py:480
  637.1 40.1 %collective-permute-start.36 = (bf16[128,2048]{1,0:T(8,128)(2,1)S(1)}, bf16[128,2048]{1,0:T(8,128)(2,1)S(1)}, u32[]{:S(2)}, u32[]{:S(2)}) collective-permute-start(bf16[128,2048]{1,0:T(8,128)(2,1)S(1)} %get-tuple-element.296), channel_id=1, source_target_pairs={{0,2},{1,3},{2,0},{3,1},{4,6},{5,7},{6,4},{7,5},{8,10},{9,11},{10,... | collective-permute-start | bytes 1572872 | tf_op jit(solution)/shard_map/ppermute | solution.py:480
  683.3 29.1 %collective-permute-start.41 = (bf16[128,2048]{1,0:T(8,128)(2,1)}, bf16[128,2048]{1,0:T(8,128)(2,1)}, u32[]{:S(2)}, u32[]{:S(2)}) collective-permute-start(bf16[128,2048]{1,0:T(8,128)(2,1)} %get-tuple-element.305), channel_id=1, source_target_pairs={{0,2},{1,3},{2,0},{3,1},{4,6},{5,7},{6,4},{7,5},{8,10},{9,11},{10,... | collective-permute-start | bytes 1572872 | tf_op jit(solution)/shard_map/ppermute | solution.py:480
  684.2 28.1 %collective-permute-start.42 = (bf16[128,2048]{1,0:T(8,128)(2,1)}, bf16[128,2048]{1,0:T(8,128)(2,1)}, u32[]{:S(2)}, u32[]{:S(2)}) collective-permute-start(bf16[128,2048]{1,0:T(8,128)(2,1)} %get-tuple-element.306), channel_id=1, source_target_pairs={{0,4},{1,5},{2,6},{3,7},{4,0},{5,1},{6,2},{7,3},{8,12},{9,13},{10,... | collective-permute-start | bytes 1572872 | tf_op jit(solution)/shard_map/ppermute | solution.py:480
  686.7 25.7 %collective-permute-start.39 = (bf16[64,2048]{1,0:T(8,128)(2,1)}, bf16[64,2048]{1,0:T(8,128)(2,1)}, u32[]{:S(2)}, u32[]{:S(2)}) collective-permute-start(bf16[64,2048]{1,0:T(8,128)(2,1)} %get-tuple-element.303), channel_id=1, source_target_pairs={{0,2},{1,3},{2,0},{3,1},{4,6},{5,7},{6,4},{7,5},{8,10},{9,11},{10,... | collective-permute-start | bytes 786440 | tf_op jit(solution)/shard_map/ppermute | solution.py:480
  686.9 25.5 %collective-permute-start.40 = (bf16[64,2048]{1,0:T(8,128)(2,1)}, bf16[64,2048]{1,0:T(8,128)(2,1)}, u32[]{:S(2)}, u32[]{:S(2)}) collective-permute-start(bf16[64,2048]{1,0:T(8,128)(2,1)} %get-tuple-element.304), channel_id=1, source_target_pairs={{0,4},{1,5},{2,6},{3,7},{4,0},{5,1},{6,2},{7,3},{8,12},{9,13},{10,... | collective-permute-start | bytes 786440 | tf_op jit(solution)/shard_map/ppermute | solution.py:480
  687.4 19.9 %all-to-all-start.6 = ((bf16[8,64,256]{2,1,0:T(8,128)(2,1)}), bf16[8,64,256]{2,1,0:T(8,128)(2,1)S(1)}, u32[]{:S(2)}, u32[]{:S(2)}) async-start(bf16[8,64,256]{2,1,0:T(8,128)(2,1)} %bitcast.87), calls=%async_computation.9 | async-start | bytes 524288 | tf_op jit(solution)/shard_map/all_to_all | solution.py:622
  715.0 13.6 %collective-permute-start.43 = (bf16[128,2048]{1,0:T(8,128)(2,1)}, bf16[128,2048]{1,0:T(8,128)(2,1)}, u32[]{:S(2)}, u32[]{:S(2)}) collective-permute-start(bf16[128,2048]{1,0:T(8,128)(2,1)} %add_convert_fusion.7), channel_id=1, source_target_pairs={{0,8},{8,0},{1,9},{9,1},{2,10},{10,2},{3,11},{11,3},{4,12},{12,4},... | collective-permute-start | bytes 1572872 | tf_op jit(solution)/shard_map/ppermute | solution.py:504
  717.1 17.5 %all-to-all-start.7 = ((bf16[8,64,896]{2,1,0:T(8,128)(2,1)}), bf16[8,64,896]{2,1,0:T(8,128)(2,1)S(1)}, u32[]{:S(2)}, u32[]{:S(2)}) async-start(bf16[8,64,896]{2,1,0:T(8,128)(2,1)} %bitcast.83), calls=%async_computation.11 | async-start | bytes 1835008 | tf_op jit(solution)/shard_map/all_to_all | solution.py:622
  (35 other events, 300.1 us)
Sparse Core Ops, SparseCore 0:
  10.2 31.6 all-gather.6
  43.5 62.9 all-gather.4
  139.7 78.5 all-gather.8
  284.1 76.4 all-gather.10
  401.9 76.9 reduce-scatter.4
  481.1 77.0 reduce-scatter.6
  605.2 30.1 reduce-scatter.8
  637.8 69.2 reduce-scatter.10

commit v3 on v2

--- a/solution.py
+++ b/solution.py
@@ -112,46 +112,6 @@
     return values * cosine + pltpu.roll(values, HD // 2, 1) * sine
 
 
-def attend_kernel(
-    heads_all, q_ref, k_ref, v_ref, cos_ref, sin_ref, col_ref, row_ref, qo, ko, vo, oo, mo
-):
-    length = q_ref.shape[0]
-    tile = min(TILE, length)
-    cosine, sine = cos_ref[...], sin_ref[...]
-    queries = turn(q_ref[...], cosine, sine).astype(bf16)
-    keys = turn(k_ref[...], cosine, sine).astype(bf16)
-    values = v_ref[...].astype(bf16)
-    qo[...] = queries
-    ko[...] = keys
-    vo[...] = values
-    first = pl.program_id(0) == 0
-    for i in range(length // tile):
-        at = slice(i * tile, (i + 1) * tile)
-        scores = dot_t(queries[at], keys) * score_scale + score_bias
-        visible = row_ref[...] <= col_ref[at, :]
-        weights = jnp.where(visible, jax.nn.sigmoid(scores), 0.0)
-        oo[at, :] = dot(weights.astype(bf16), values).astype(bf16)
-        mass = jnp.sum(weights, axis=1, keepdims=True) * (1.0 / heads_all)
-        mass = jnp.broadcast_to(mass, (tile, LANES))
-        mo[at, :] = jnp.where(first, mass, mo[at, :] + mass)
-
-
-def attend(qkv, cosine, sine, pos_col, pos_row, heads, heads_all):
-    length = qkv.shape[0]
-    part = lambda j: pl.BlockSpec((length, HD), lambda i, j=j: (0, i + j * heads))
-    out = jax.ShapeDtypeStruct((length, heads * HD), bf16)
-    return call(
-        functools.partial(attend_kernel, heads_all),
-        heads,
-        (qkv, qkv, qkv, cosine, sine, pos_col, pos_row),
-        [part(0), part(1), part(2)]
-        + [whole(a.shape) for a in (cosine, sine, pos_col, pos_row)],
-        [out] * 4 + [jax.ShapeDtypeStruct((length, LANES), f32)],
-        [part(0)] * 4 + [pl.BlockSpec((length, LANES), lambda i: (0, 0))],
-        4 * heads * length * length * HD,
-    )
-
-
 def halves(length, cols):
     tile = min(TILE, length // 2)
     count = length // 2 // tile
@@ -184,53 +144,100 @@
         outs[1][...] = value
 
 
-def project_kernel(o_ref, m_ref, w_ref, *outs):
-    value = dot_t(o_ref[...], w_ref[...]).astype(bf16)
-    store_half(jnp.concatenate([value, m_ref[...].astype(bf16)], axis=1), outs)
-
-
-def project(attended, mass, w_qko):
-    length, cols = attended.shape
-    width = w_qko.shape[0]
-    tile, steps, outs, specs = halves(length, width + LANES)
-    return call(
-        project_kernel,
-        steps,
-        (attended, mass, w_qko),
-        [rows_of(tile, cols), rows_of(tile, LANES), columns(w_qko, 2, cols)],
-        outs,
-        specs,
-        2 * length * cols * width,
-    )
-
-
-def enter_kernel(a_ref, b_ref, gain_ref, wq_ref, wk_ref, wv_ref, qkv_ref, n_ref):
-    rows = either((a_ref, b_ref)).astype(f32)
-    normed = (rows * norm_scale(rows) * gain_ref[...]).astype(bf16)
-    n_ref[...] = normed
-    cols = wq_ref.shape[1]
-    for i, ref in enumerate((wq_ref, wk_ref, wv_ref)):
-        qkv_ref[:, i * cols : (i + 1) * cols] = dot(normed, ref[...])
-
-
-def enter(x_pair, gain, w_qko, w_v):
+def later(i, first, count):
+    return jnp.clip(i - first, 0, count - 1)
+
+
+def front_kernel(
+    heads_all, steps, xa, xb, gain_ref, wq, wk, wv, wo, cos, sin, col, row, *refs
+):
+    n_ref, qo, ko, vo, oo, keep, away, qkv, mass = refs
+    i = pl.program_id(0)
+    tile = n_ref.shape[0]
+    cols = wq.shape[1]
+
+    @pl.when(i < steps)
+    def _():
+        rows = jnp.where(i < steps // 2, xa[...], xb[...]).astype(f32)
+        normed = (rows * norm_scale(rows) * gain_ref[...]).astype(bf16)
+        n_ref[...] = normed
+        at = pl.ds(pl.multiple_of(i * tile, tile), tile)
+        for j, w in enumerate((wq, wk, wv)):
+            qkv[at, j * cols : (j + 1) * cols] = dot(normed, w[...])
+
+    @pl.when(i == steps - 1)
+    def _():
+        cosine, sine = cos[...], sin[...]
+        for h in range(cols // HD):
+            head = slice(h * HD, (h + 1) * HD)
+            queries = turn(qkv[:, h * HD : (h + 1) * HD], cosine, sine).astype(bf16)
+            keys = turn(qkv[:, cols + h * HD : cols + (h + 1) * HD], cosine, sine).astype(bf16)
+            values = qkv[:, 2 * cols + h * HD : 2 * cols + (h + 1) * HD].astype(bf16)
+            qo[:, head] = queries
+            ko[:, head] = keys
+            vo[:, head] = values
+            for j in range(steps):
+                at = slice(j * tile, (j + 1) * tile)
+                scores = dot_t(queries[at], keys) * score_scale + score_bias
+                weights = jnp.where(row[...] <= col[at, :], jax.nn.sigmoid(scores), 0.0)
+                oo[at, head] = dot(weights.astype(bf16), values).astype(bf16)
+                part = jnp.sum(weights, axis=1, keepdims=True) * (1.0 / heads_all)
+                part = jnp.broadcast_to(part, (tile, LANES))
+                mass[at, :] = part if h == 0 else mass[at, :] + part
+
+    def projected():
+        at = pl.ds(pl.multiple_of((i - steps) * tile, tile), tile)
+        value = dot_t(oo[at, :], wo[...]).astype(bf16)
+        return jnp.concatenate([value, mass[at, :].astype(bf16)], axis=1)
+
+    @pl.when((i >= steps) & (i < steps + steps // 2))
+    def _():
+        keep[...] = projected()
+
+    @pl.when(i >= steps + steps // 2)
+    def _():
+        away[...] = projected()
+
+
+def front(x_pair, gain, w_qko, w_v, cosine, sine, pos_col, pos_row, heads_all):
     length, width = 2 * x_pair[0].shape[0], x_pair[0].shape[1]
-    one = w_v.shape[1]
-    cols = 3 * one
+    cols = w_v.shape[1]
     tile = min(TILE, length // 2)
-    return call(
-        enter_kernel,
-        length // tile,
-        (*x_pair, gain, w_qko, w_qko, w_v),
-        pair_specs(length, width, tile)
-        + [whole(gain.shape), columns(w_qko, 0, one), columns(w_qko, 1, one), whole(w_v.shape)],
-        [
-            jax.ShapeDtypeStruct((length, cols), f32),
-            jax.ShapeDtypeStruct((length, width), bf16),
+    steps = length // tile
+    half = steps // 2
+    constants = (cosine, sine, pos_col, pos_row)
+    rows = jax.ShapeDtypeStruct((length, cols), bf16)
+    sides = jax.ShapeDtypeStruct((length // 2, width + LANES), bf16)
+    return pl.pallas_call(
+        functools.partial(front_kernel, heads_all, steps),
+        grid=(2 * steps,),
+        in_specs=[
+            pl.BlockSpec((tile, width), lambda i: (later(i, 0, half), 0)),
+            pl.BlockSpec((tile, width), lambda i: (later(i, half, half), 0)),
+            whole(gain.shape),
+            columns(w_qko, 0, cols),
+            columns(w_qko, 1, cols),
+            whole(w_v.shape),
+            columns(w_qko, 2, cols),
+        ]
+        + [whole(a.shape) for a in constants],
+        out_specs=[pl.BlockSpec((tile, width), lambda i: (later(i, 0, steps), 0))]
+        + [pl.BlockSpec((length, cols), lambda i: (0, 0))] * 4
+        + [
+            pl.BlockSpec((tile, width + LANES), lambda i: (later(i, steps, half), 0)),
+            pl.BlockSpec((tile, width + LANES), lambda i: (later(i, steps + half, half), 0)),
         ],
-        [rows_of(tile, cols), rows_of(tile, width)],
-        2 * length * width * cols,
-    )
+        out_shape=[jax.ShapeDtypeStruct((length, width), bf16)] + [rows] * 4 + [sides] * 2,
+        scratch_shapes=[pltpu.VMEM((length, 3 * cols), f32), pltpu.VMEM((length, LANES), f32)],
+        compiler_params=pltpu.CompilerParams(
+            dimension_semantics=("arbitrary",), vmem_limit_bytes=60 * MIB
+        ),
+        cost_estimate=pl.CostEstimate(
+            flops=8 * length * width * cols,
+            bytes_accessed=12 * length * width,
+            transcendentals=0,
+        ),
+    )(*x_pair, gain, w_qko, w_qko, w_v, w_qko, *constants)
 
 
 def ffn_kernel(na_ref, nb_ref, da_ref, db_ref, w_ref, act_ref, back_ref):
@@ -300,25 +307,6 @@
     )
 
 
-def branch_kernel(a_ref, b_ref, w_ref, out_ref):
-    out_ref[...] = dot(either((a_ref, b_ref)), w_ref[...]).astype(bf16)
-
-
-def branch_back(pair, w_qko):
-    length, width = 2 * pair[0].shape[0], pair[0].shape[1]
-    cols = w_qko.shape[1] // 3
-    tile = min(TILE, length // 2)
-    return call(
-        branch_kernel,
-        length // tile,
-        (*pair, w_qko),
-        pair_specs(length, width, tile) + [columns(w_qko, 2, cols)],
-        [jax.ShapeDtypeStruct((length, cols), bf16)],
-        [rows_of(tile, cols)],
-        2 * length * width * cols,
-    )
-
-
 def branch_sums_kernel(a_ref, b_ref, o_ref, sum_ref):
     sum_ref[...] = t_dot_pair((a_ref, b_ref), o_ref).astype(bf16)
 
@@ -378,71 +366,88 @@
     )
 
 
-def attend_back_kernel(q_ref, k_ref, v_ref, g_ref, cos_ref, sin_ref, col_ref, row_ref, dq, dk, dv):
-    length = q_ref.shape[0]
-    tile = min(TILE, length)
-    cosine, sine = cos_ref[...], -sin_ref[...]
-    queries, keys, values, grads = q_ref[...], k_ref[...], v_ref[...], g_ref[...]
-    grad_keys = grad_values = 0.0
-    for i in range(length // tile):
-        at = slice(i * tile, (i + 1) * tile)
-        scores = dot_t(keys, queries[at]) * score_scale + score_bias
-        visible = col_ref[...] <= row_ref[:, at]
-        weights = jnp.where(visible, jax.nn.sigmoid(scores), 0.0)
-        grad_weights = dot_t(values, grads[at])
-        grad_scores = (grad_weights * weights * (1.0 - weights)).astype(bf16)
-        grad_values = grad_values + dot(weights.astype(bf16), grads[at])
-        grad_keys = grad_keys + dot(grad_scores, queries[at])
-        grad_query = t_dot(grad_scores, keys) * score_scale
-        dq[at, :] = turn(grad_query, cosine[at], sine[at]).astype(bf16)
-    dk[...] = turn(grad_keys * score_scale, cosine, sine).astype(bf16)
-    dv[...] = grad_values.astype(bf16)
-
-
-def attend_back(queries, keys, values, grads, cosine, sine, pos_col, pos_row):
-    length, cols = queries.shape
-    heads = cols // HD
-    part = pl.BlockSpec((length, HD), lambda i: (0, i))
-    out = jax.ShapeDtypeStruct((length, cols), bf16)
-    return call(
-        attend_back_kernel,
-        heads,
-        (queries, keys, values, grads, cosine, sine, pos_col, pos_row),
-        [part] * 4 + [whole(a.shape) for a in (cosine, sine, pos_col, pos_row)],
-        [out] * 3,
-        [part] * 3,
-        10 * heads * length * length * HD,
-    )
-
-
-def qkv_sums_kernel(n_ref, dq, dk, dv, wq_ref, wk_ref, wv_ref, other_ref, out_ref):
-    cols = dq.shape[1]
-    gain = 0.0
-    for i, (ref, w) in enumerate(((dq, wq_ref), (dk, wk_ref), (dv, wv_ref))):
-        part = t_dot(n_ref[...], ref[...])
-        out_ref[:, i * cols : (i + 1) * cols] = part.astype(bf16)
-        gain = gain + jnp.sum(part * w[...].astype(f32), axis=1, keepdims=True)
-    lane = lax.broadcasted_iota(jnp.int32, other_ref.shape, 1)
-    gains = jnp.where(lane == 0, gain, other_ref[...])
-    out_ref[:, 3 * cols :] = gains.astype(bf16)
-
-
-def qkv_sums(normed, dq, dk, dv, w_qko, w_v, other):
+def rear_kernel(
+    steps, ba, bb, wo, q_ref, k_ref, v_ref, cos, sin, col, row, n_ref, wq, wk, wv, g0, g1, *refs
+):
+    dq, dk, dv, out_ref, grads = refs
+    i = pl.program_id(0)
+    tile = ba.shape[0]
+    cols = wo.shape[1]
+
+    @pl.when(i < steps)
+    def _():
+        at = pl.ds(pl.multiple_of(i * tile, tile), tile)
+        rows = jnp.where(i < steps // 2, ba[...], bb[...])
+        grads[at, :] = dot(rows, wo[...]).astype(bf16)
+
+    @pl.when(i == steps - 1)
+    def _():
+        cosine, sine = cos[...], -sin[...]
+        for h in range(cols // HD):
+            head = slice(h * HD, (h + 1) * HD)
+            queries, keys, values = q_ref[:, head], k_ref[:, head], v_ref[:, head]
+            gradient = grads[:, head]
+            grad_keys = grad_values = 0.0
+            for j in range(steps):
+                at = slice(j * tile, (j + 1) * tile)
+                scores = dot_t(keys, queries[at]) * score_scale + score_bias
+                weights = jnp.where(col[...] <= row[:, at], jax.nn.sigmoid(scores), 0.0)
+                grad_weights = dot_t(values, gradient[at])
+                grad_scores = (grad_weights * weights * (1.0 - weights)).astype(bf16)
+                grad_values = grad_values + dot(weights.astype(bf16), gradient[at])
+                grad_keys = grad_keys + dot(grad_scores, queries[at])
+                grad_query = t_dot(grad_scores, keys) * score_scale
+                dq[at, head] = turn(grad_query, cosine[at], sine[at]).astype(bf16)
+            dk[:, head] = turn(grad_keys * score_scale, cosine, sine).astype(bf16)
+            dv[:, head] = grad_values.astype(bf16)
+
+    @pl.when(i >= steps)
+    def _():
+        gain = 0.0
+        for j, (ref, w) in enumerate(((dq, wq), (dk, wk), (dv, wv))):
+            part = t_dot(n_ref[...], ref[...])
+            out_ref[:, j * cols : (j + 1) * cols] = part.astype(bf16)
+            gain = gain + jnp.sum(part * w[...].astype(f32), axis=1, keepdims=True)
+        lane = lax.broadcasted_iota(jnp.int32, g0.shape, 1)
+        gains = jnp.where(lane == 0, gain, g0[...] + g1[...])
+        out_ref[:, 3 * cols :] = gains.astype(bf16)
+
+
+def rear(pair, queries, keys, values, constants, normed, w_qko, w_v, gain_sums):
     length, width = normed.shape
-    cols = dq.shape[1]
-    tile = min(2 * TILE, width)
-    return call(
-        qkv_sums_kernel,
-        width // tile,
-        (normed, dq, dk, dv, w_qko, w_qko, w_v, other),
-        [cols_of(length, tile)]
-        + [whole(a.shape) for a in (dq, dk, dv)]
-        + [pl.BlockSpec((tile, cols), lambda i, at=at: (i, at)) for at in (0, 1, 0)]
-        + [rows_of(tile, LANES)],
-        [jax.ShapeDtypeStruct((width, 3 * cols + LANES), bf16)],
-        [rows_of(tile, 3 * cols + LANES)],
-        6 * length * width * cols,
-    )
+    cols = w_v.shape[1]
+    tile = min(TILE, length // 2)
+    steps = length // tile
+    half = steps // 2
+    block = min(2 * TILE, width)
+    blocks = width // block
+    rows = jax.ShapeDtypeStruct((length, cols), bf16)
+    place = lambda at: pl.BlockSpec((block, cols), lambda i: (later(i, steps, blocks), at))
+    return pl.pallas_call(
+        functools.partial(rear_kernel, steps),
+        grid=(steps + blocks,),
+        in_specs=[
+            pl.BlockSpec((tile, width), lambda i: (later(i, 0, half), 0)),
+            pl.BlockSpec((tile, width), lambda i: (later(i, half, half), 0)),
+            columns(w_qko, 2, cols),
+        ]
+        + [whole(a.shape) for a in (queries, keys, values, *constants)]
+        + [pl.BlockSpec((length, block), lambda i: (0, later(i, steps, blocks)))]
+        + [place(0), place(1), place(0)]
+        + [pl.BlockSpec((block, LANES), lambda i: (later(i, steps, blocks), 0))] * 2,
+        out_specs=[pl.BlockSpec((length, cols), lambda i: (0, 0))] * 3
+        + [pl.BlockSpec((block, 3 * cols + LANES), lambda i: (later(i, steps, blocks), 0))],
+        out_shape=[rows] * 3 + [jax.ShapeDtypeStruct((width, 3 * cols + LANES), bf16)],
+        scratch_shapes=[pltpu.VMEM((length, cols), bf16)],
+        compiler_params=pltpu.CompilerParams(
+            dimension_semantics=("arbitrary",), vmem_limit_bytes=60 * MIB
+        ),
+        cost_estimate=pl.CostEstimate(
+            flops=8 * length * width * cols,
+            bytes_accessed=8 * length * width,
+            transcendentals=0,
+        ),
+    )(*pair, w_qko, queries, keys, values, *constants, normed, w_qko, w_qko, w_v, *gain_sums)
 
 
 def unpack_kernel(count, parts, *refs):
@@ -579,17 +584,20 @@
             self.moves, self.result = None, end.value
 
 
-def run(steps, riders=(), waits=()):
-    main = Ride(steps)
-    waits = list(waits)
+def run(steps, riders=(), waits=(), then=(), late=0):
+    main = steps if isinstance(steps, Ride) else Ride(steps)
+    waits, then = list(waits), list(then)
     while main.moves is not None:
-        active = [main] + [rider for rider in riders if rider.moves is not None]
+        active = [main] + [rider for rider in riders if rider.moves is not None and late <= 0]
+        late -= 1
         got = exchange(
             [move for ride in active for move in ride.moves], waits.pop(0) if waits else ()
         )
         for ride in active:
             part, got = got[: len(ride.moves)], got[len(ride.moves) :]
             ride.feed(part)
+        if then:
+            then.pop(0)()
     return main.result
 
 
@@ -644,7 +652,11 @@
     plans = [[(m, c, CHUNKS) for m in range(3)] for c in range(CHUNKS)]
     ffn_blocks = list(pack((gate_weight, up_weight, down_weight.T.astype(bf16)), plans, 2 * ns))
     x_own, attn_blocks = lax.optimization_barrier((tokens[0], attn_blocks))
-    x_all = run(gather_one(x_own))
+    x_ride, dy_ride = Ride(gather_one(x_own)), Ride(gather_two(cotangent[0]))
+    got = exchange(x_ride.moves + dy_ride.moves)
+    x_ride.feed(got[:-1])
+    dy_ride.feed(got[-1:])
+    x_all = run(x_ride)
     w_v = w_v.reshape(nb, rows, -1)
     spread = jnp.broadcast_to(w_v[None, :, :, width:], (ns, nb, rows, LANES))
     w_v = w_v[:, :, :width].reshape(nb, rows, ns, head_cols).transpose(2, 0, 1, 3)
@@ -677,18 +689,22 @@
     )
     ffn_blocks[0] = swap(ffn_blocks[0], near).reshape(2 * ns * rows, -1)
 
-    qkv, normed = enter(x_all, gain_one[None], w_qko, w_v)
-    queries, keys, values, attended, mass = attend(
-        qkv, cosine, sine, pos_col, pos_row, heads, width // HD
-    )
-    attended, ffn_blocks = lax.optimization_barrier((attended, ffn_blocks))
-    ffn_blocks[0], ffn_blocks[1] = lax.optimization_barrier((ffn_blocks[0], ffn_blocks[1]))
-    ffn_blocks[1] = swap(ffn_blocks[1], near).reshape(2 * ns * rows, -1)
-    w_ffn = [gather_z(block, "pair") for block in ffn_blocks]
-    dy_ride = Ride(gather_two(cotangent[0]))
+    constants = (cosine, sine, pos_col, pos_row)
+    normed, queries, keys, values, attended, kept, away = front(
+        x_all, gain_one[None], w_qko, w_v, *constants, width // HD
+    )
+    w_ffn = [gather_z(ffn_blocks[0], "pair")]
+
+    def second():
+        ffn_blocks[1] = swap(ffn_blocks[1], near).reshape(2 * ns * rows, -1)
+
     attn_own = run(
-        scatter_one(project(attended, mass, w_qko)), [dy_ride], [[], [(w_ffn, 0)]]
-    )
+        scatter_one((kept, away)),
+        [dy_ride],
+        [[(ffn_blocks, 1)], [(w_ffn, 0), (ffn_blocks, 1)]],
+        [second],
+    )
+    w_ffn.append(gather_z(ffn_blocks[1], "pair"))
     attn_mass = attn_own[:, width]
     x_own_f = x_own.astype(f32)
     hidden_own = x_own_f + attn_own[:, :width]
@@ -697,65 +713,83 @@
     normed_ffn = run(
         gather_two((unit_two * gain_two).astype(bf16)),
         [dy_ride],
-        [[], [], [(w_ffn, 1)]],
+        [[], [(w_ffn, 1)]],
     )
     dy_all = dy_ride.result
 
     acts, backs, sums, gain_sums = [], [], [], []
     for c in range(CHUNKS):
         act, grads = ffn(normed_ffn, dy_all, w_ffn[c])
-        if c + 1 == CHUNKS:
-            grads_pair = back(backs + [grads], w_ffn)
-            act, grads_pair = lax.optimization_barrier((act, grads_pair))
-        part, gains = ffn_sums(normed_ffn, dy_all, act, grads, w_ffn[c])
-        if c + 1 < CHUNKS:
-            act, grads, part, w_ffn[c + 1] = lax.optimization_barrier(
-                (act, grads, part, w_ffn[c + 1])
-            )
         acts.append(act)
         backs.append(grads)
+        if c + 1 == CHUNKS:
+            break
+        part, gains = ffn_sums(normed_ffn, dy_all, act, grads, w_ffn[c])
+        gain_sums.append(gains)
+        acts[c], backs[c], part, w_ffn[c + 1] = lax.optimization_barrier(
+            (act, grads, part, w_ffn[c + 1])
+        )
         sums.append(scatter_z(part, "pair"))
+    grads_pair = back(backs, w_ffn)
+
+    def home(part, axes="seq"):
+        return swap(part.reshape(lax.axis_size(axes), rows, -1), axes)
+
+    made = []
+
+    def last_sums():
+        part, gains = ffn_sums(normed_ffn, dy_all, acts[-1], backs[-1], w_ffn[-1])
         gain_sums.append(gains)
-    gain_sums = sum(gain_sums)
-    grad_normed_two = run(scatter_two(grads_pair), (), [[], [], [(sums, 0)]])
+        made.append(part)
+
+    def leave():
+        sums.append(scatter_z(made[0], "pair"))
+
+    def output():
+        made.append(back(acts, w_ffn, 2 * ffn_cols))
+
+    grad_normed_two = run(
+        scatter_two(grads_pair),
+        (),
+        [[(acts, 1), (backs, 1)], [(made, 0)], [(sums, 0), (acts, 0)], [(made, 1)]],
+        [last_sums, leave, output],
+    )
     grad_hidden = cotangent[0].astype(f32) + norm_back(
         grad_normed_two, unit_two, scale_two, gain_two
     )
 
-    def home(part, axes="seq"):
-        return swap(part.reshape(lax.axis_size(axes), rows, -1), axes)
-
-    branch = run(gather_one(grad_hidden.astype(bf16)), (), [[], [(sums, 1)]])
+    ffn_sum = [home(sums[0], near)]
+    out_ride = Ride(scatter_two(made[1]))
+    waits = [[], [(ffn_sum, 0), (sums, 1)]]
+    branch = run(gather_one(grad_hidden.astype(bf16)), [out_ride], waits, late=2)
     out_sum = branch_sums(branch, attended)
-    branch, out_sum = lax.optimization_barrier((branch, out_sum))
+    moves = out_ride.moves
+    branch, out_sum, sent = lax.optimization_barrier((branch, out_sum, [b for b, _ in moves]))
+    flying = [f(b) for (_, f), b in zip(moves, sent)]
     out_sum = scatter_z(out_sum)
-    grad_heads = branch_back(branch, w_qko)
-    dq, dk, dv = attend_back(queries, keys, values, grad_heads, cosine, sine, pos_col, pos_row)
-    ffn_sum = [home(sums[0], near)]
-    dq, ffn_sum = lax.optimization_barrier((dq, ffn_sum))
-    qkv_local = qkv_sums(normed, dq, dk, dv, w_qko, w_v, gain_sums)
-    dq, dk, dv, qkv_local = lax.optimization_barrier((dq, dk, dv, qkv_local))
+    dq, dk, dv, qkv_local = rear(
+        branch, queries, keys, values, constants, normed, w_qko, w_v, gain_sums
+    )
+    ffn_sum.append(home(sums[1], near))
+    dq, dk, dv, qkv_local, ffn_sum, flying, out_sum = lax.optimization_barrier(
+        (dq, dk, dv, qkv_local, ffn_sum, flying, out_sum)
+    )
+    out_ride.feed(flying)
     qkv_sum = scatter_z(qkv_local)
     part = enter_back([dq, dk, dv], w_qko, w_v)
-    part, acts = lax.optimization_barrier((part, acts))
-    out_ride = Ride(scatter_two(back(acts, w_ffn, 2 * ffn_cols)))
     grad_normed = run(scatter_one(part), [out_ride])
-    (got,) = exchange(out_ride.moves)
-    out_ride.feed([got])
+    while out_ride.moves is not None:
+        out_ride.feed(exchange(out_ride.moves))
     layer_out = (hidden_own + out_ride.result).astype(bf16)
-    ffn_sum.append(home(sums[1], near))
     scale_one = norm_scale(x_own_f)
     input_grad = (
         grad_hidden + norm_back(grad_normed, x_own_f * scale_one, scale_one, gain_one)
     ).astype(bf16)
 
     gate_grad, up_grad, down_grad = unpack(ffn_sum, 3)
-    out_grad = unpack([home(out_sum)], 1).T
-    down_grad = down_grad.T
-    gate_grad, up_grad, down_grad, out_grad, qkv_sum = lax.optimization_barrier(
-        (gate_grad, up_grad, down_grad, out_grad, qkv_sum)
-    )
-    query_grad, key_grad, value_grad, gains = unpack([home(qkv_sum)], 3, True)
+    attn_sums = home(jnp.concatenate([out_sum, qkv_sum], axis=1))
+    out_grad, query_grad, key_grad, value_grad, gains = unpack([attn_sums], 4, True)
+    out_grad, down_grad = out_grad.T, down_grad.T
     return (
         layer_out[None],
         input_grad[None],

time: 761 us -> 705 us (0.926)
  waiting for transfers between devices: 369 us -> 337 us
  blocking collectives: 25.1 us -> 0 us
  Pallas kernels: 178 us -> 167 us
    pallas_call x19 -> x12, Pallas kernels: 178 us -> 128 us  [call(): pl.pallas_call(kernel, grid_spec=pltpu.PrefetchScalarGridSpec(num_scalar_...]
    pallas_call x0 -> x2, Pallas kernels: none -> 38.7 us  [the longest x1 20.7 us: rear(): pl.pallas_call(functools.partial(rear_kernel, steps), grid=(steps + block...]
    all_gather x4, waiting for transfers between devices: 79.5 us -> 51.6 us  [gather_z(): return lax.all_gather(block, axes, axis=0, tiled=True)]
    all_to_all x1 -> x0, blocking collectives: 25.1 us -> none  [swap(): return lax.all_to_all(blocks, axes, split_axis=0, concat_axis=0, tiled=True)]
    reduce_scatter x4, waiting for transfers between devices: 19.3 us -> 11.1 us  [scatter_z(): return lax.psum_scatter(full, axes, scatter_dimension=0, tiled=True)]
    ppermute x40, waiting for transfers between devices: 168 us -> 176 us  [swap_bit(): return lax.ppermute(block, 'seq', [(i, i ^ bit) for i in range(size)])]
    unnamed x67 -> x107, local copies, waits for them, and re-layouts: 19.9 us -> 25.4 us
  transfers between devices with their start and end apart: 59 -> 59, of which waited for: 30 -> 38; matrix products, arithmetic and copies ran while one was open for 10% -> 11% of each run, Pallas kernels for 16% -> 19%
where the time goes in v3:
time: 705 us; the launch traced here: 696 us
  waiting for transfers between devices  337 us (48%)
  Pallas kernels  167 us (24%)
  starting transfers between devices  71.5 us (10%)
  other arithmetic  62.4 us (9%)
  local copies, waits for them, and re-layouts  42.8 us (6%)
  between operations  15.1 us (2%)
    ppermute x40, waiting for transfers between devices, swap_bit(): return lax.ppermute(block, 'seq', [(i, i ^ bit) for i in range(size)])  176 us
    pallas_call x12, Pallas kernels, call(): pl.pallas_call(kernel, grid_spec=pltpu.PrefetchScalarGridSpec(num_scalar_...  128 us
    ppermute x4, waiting for transfers between devices, swap_side(): return lax.ppermute(block, 'side', [(0, 1), (1, 0)])  59.5 us
    all_gather x4, waiting for transfers between devices, gather_z(): return lax.all_gather(block, axes, axis=0, tiled=True)  51.6 us
    all_to_all x7, waiting for transfers between devices, swap(): return lax.all_to_all(blocks, axes, split_axis=0, concat_axis=0, tiled=True)  39.5 us
    ppermute x40, starting transfers between devices, swap_bit(): return lax.ppermute(block, 'seq', [(i, i ^ bit) for i in range(size)])  38.9 us
    all_to_all x7, starting transfers between devices, swap(): return lax.all_to_all(blocks, axes, split_axis=0, concat_axis=0, tiled=True)  28.8 us
    unnamed x107, local copies, waits for them, and re-layouts  25.4 us
  transfers between devices with their start and end apart: 59, of which 38 were waited for; matrix products, arithmetic and copies ran while one was open for 11% of the time, Pallas kernels for 19%

profile of v3, /device:TPU:0, one launch (start us, length us, event | category | flops | bytes accessed | tf_op | source)
XLA Modules:
  0.0 696.4 jit_solution(16205209083311813111)
XLA Ops:
  12.9 5.0 shard_map.220
  17.9 5.2 all-to-all-start
  25.9 11.2 %all-to-all-done = bf16[8,64,896]{2,1,0:T(8,128)(2,1)S(1)} async-done(((bf16[8,64,896]{2,1,0:T(8,128)(2,1)}), bf16[8,64,896]{2,1,0:T(8,128)(2,1)S(1)}, u32[]{:S(2)}, u32[]{:S(2)}) %all-to-all-start) | async-done | bytes 917536 | tf_op jit(solution)/shard_map/all_to_all | solution.py:630
  42.4 10.3 %shard_map.221 = (bf16[16,64,768]{2,1,0:T(8,128)(2,1)}, bf16[16,64,768]{2,1,0:T(8,128)(2,1)}) custom-call(f32[64,8192]{1,0:T(8,128)} %refs_0_.3, f32[64,8192]{1,0:T(8,128)} %refs_1_.3, bf16[64,8192]{1,0:T(8,128)(2,1)} %convert_bitcast_fusion.refs_2_), custom_call_target="tpu_custom_call" | custom-call | bytes 8388608 | tf_op jit(solution)/shard_map/pallas_call | solution.py:62
  57.5 8.2 %collective-permute-done.3 = bf16[128,2048]{1,0:T(8,128)(2,1)S(1)} collective-permute-done((bf16[128,2048]{1,0:T(8,128)(2,1)S(1)}, bf16[128,2048]{1,0:T(8,128)(2,1)S(1)}, u32[]{:S(2)}, u32[]{:S(2)}) %collective-permute-start.3) | collective-permute-done | bytes 524320 | tf_op jit(solution)/shard_map/ppermute | solution.py:485
  74.4 3.7 all-to-all-start.1
  84.3 14.8 %all-to-all-done.1 = bf16[8,4,64,384]{3,2,1,0:T(8,128)(2,1)S(1)} async-done(((bf16[8,4,64,384]{3,2,1,0:T(8,128)(2,1)}), bf16[8,4,64,384]{3,2,1,0:T(8,128)(2,1)S(1)}, u32[]{:S(2)}, u32[]{:S(2)}) %all-to-all-start.1) | async-done | bytes 1572896 | tf_op jit(solution)/shard_map/all_to_all | solution.py:630
  101.4 6.2 all-gather.5.cloned.1.call-done.wq.wk.wo.refs_3_.refs_4_
  107.6 3.8 all-to-all-start.2
  112.7 18.0 %shard_map.222 = (bf16[1024,2048]{1,0:T(8,128)(2,1)}, bf16[1024,256]{1,0:T(8,128)(2,1)}, bf16[1024,256]{1,0:T(8,128)(2,1)}, bf16[1024,256]{1,0:T(8,128)(2,1)}, b...) custom-call(bf16[512,2048]{1,0:T(8,128)(2,1)} %constant_dynamic-update-slice_fusion.xa, ...), custom_call_target="tpu_custom_call" | custom-call | flops 4294967296 | bytes 25165824 | tf_op jit(solution)/shard_map/pallas_call | solution.py:211
  135.5 9.9 %collective-permute-done.7 = bf16[128,2048]{1,0:T(8,128)(2,1)} collective-permute-done((bf16[128,2048]{1,0:T(8,128)(2,1)S(1)}, bf16[128,2048]{1,0:T(8,128)(2,1)}, u32[]{:S(2)}, u32[]{:S(2)}) %collective-permute-start.7) | collective-permute-done | bytes 524320 | tf_op jit(solution)/shard_map/ppermute | solution.py:485
  146.8 3.8 all-to-all-start.3
  161.5 43.4 %collective-permute-done.9 = bf16[128,2176]{1,0:T(8,128)(2,1)S(1)} collective-permute-done((bf16[128,2176]{1,0:T(8,128)(2,1)S(1)}, bf16[128,2176]{1,0:T(8,128)(2,1)S(1)}, u32[]{:S(2)}, u32[]{:S(2)}) %collective-permute-start.9) | collective-permute-done | bytes 557088 | tf_op jit(solution)/shard_map/ppermute | solution.py:485
  207.8 6.1 all-gather.9.cloned.1.call-done.w_ref.refs_2_
  226.2 6.1 collective-permute-done.13
  236.3 24.1 %collective-permute-done.16 = bf16[128,2048]{1,0:T(8,128)(2,1)S(1)} collective-permute-done((bf16[128,2048]{1,0:T(8,128)(2,1)S(1)}, bf16[128,2048]{1,0:T(8,128)(2,1)S(1)}, u32[]{:S(2)}, u32[]{:S(2)}) %collective-permute-start.16) | collective-permute-done | bytes 524320 | tf_op jit(solution)/shard_map/ppermute | solution.py:509
  262.6 39.2 %all-gather.11.cloned.1.call-done.w_ref.refs_3_ = bf16[2048,768]{1,0:T(8,128)(2,1)} async-done(((bf16[1024,768]{1,0:T(8,128)(2,1)}), bf16[2048,768]{1,0:T(8,128)(2,1)}) %all-gather.11.cloned.1.call-update) | async-done | bytes 3145744 | tf_op jit(solution)/shard_map/all_gather | solution.py:633
  307.3 20.9 %collective-permute-done.19 = bf16[256,2048]{1,0:T(8,128)(2,1)S(1)} collective-permute-done((bf16[256,2048]{1,0:T(8,128)(2,1)S(1)}, bf16[256,2048]{1,0:T(8,128)(2,1)S(1)}, u32[]{:S(2)}, u32[]{:S(2)}) %collective-permute-start.19) | collective-permute-done | bytes 1048608 | tf_op jit(solution)/shard_map/ppermute | solution.py:485
  331.7 7.3 %collective-permute-done.21.nb_ref = bf16[1024,2048]{1,0:T(8,128)(2,1)} collective-permute-done((bf16[1024,2048]{1,0:T(8,128)(2,1)S(1)}, bf16[1024,2048]{1,0:T(8,128)(2,1)}, u32[]{:S(2)}, u32[]{:S(2)}) %collective-permute-start.21) | collective-permute-done | bytes 4194336 | tf_op jit(solution)/shard_map/ppermute | solution.py:485
  339.0 13.4 %shard_map.223 = (bf16[2048,256]{1,0:T(8,128)(2,1)}, bf16[2048,512]{1,0:T(8,128)(2,1)}) custom-call(bf16[1024,2048]{1,0:T(8,128)(2,1)} %copy-done.36, bf16[1024,2048]{1,0:T(8,128)(2,1)} %collective-permute-done.21.nb_ref, bf16[1024,2048]{1,0:T(8,128)(2,1)} %constant_dynamic-update-slice_fusion.6.da_ref, bf16[1024,2048]{1,0:T(8,128)(2,1)} %collective-permute-done.15.db_ref, ...), custom_call_target="tpu_custom_call" | custom-call | flops 6442450944 | bytes 23068672 | tf_op jit(solution)/shard_map/pallas_call | solution.py:62
  352.4 13.9 %shard_map.224 = (bf16[2048,768]{1,0:T(8,128)(2,1)}, f32[2048,128]{1,0:T(8,128)}) custom-call(bf16[1024,2048]{1,0:T(8,128)(2,1)} %copy-done.36, bf16[1024,2048]{1,0:T(8,128)(2,1)} %collective-permute-done.21.nb_ref, bf16[1024,2048]{1,0:T(8,128)(2,1)} %constant_dynamic-update-slice_fusion.6.da_ref, bf16[1024,2048]{1,0:T(8,128)(2,1)} %collective-permute-done.15.db_ref, ...), custom_call_target="tpu_custom_call" | custom-call | flops 6442450944 | bytes 27262976 | tf_op jit(solution)/shard_map/pallas_call | solution.py:62
  366.8 13.9 %shard_map.225 = (bf16[2048,256]{1,0:T(8,128)(2,1)}, bf16[2048,512]{1,0:T(8,128)(2,1)}) custom-call(bf16[1024,2048]{1,0:T(8,128)(2,1)} %copy-done.36, bf16[1024,2048]{1,0:T(8,128)(2,1)} %collective-permute-done.21.nb_ref, bf16[1024,2048]{1,0:T(8,128)(2,1)} %constant_dynamic-update-slice_fusion.6.da_ref, bf16[1024,2048]{1,0:T(8,128)(2,1)} %collective-permute-done.15.db_ref, ...), custom_call_target="tpu_custom_call" | custom-call | flops 6442450944 | bytes 23068672 | tf_op jit(solution)/shard_map/pallas_call | solution.py:62
  380.7 15.8 %shard_map.226 = (bf16[1024,2048]{1,0:T(8,128)(2,1)}, bf16[1024,2048]{1,0:T(8,128)(2,1)}) custom-call(bf16[2048,512]{1,0:T(8,128)(2,1)} %get-tuple-element.228.back_ref.refs_0_, bf16[2048,512]{1,0:T(8,128)(2,1)} %get-tuple-element.238.refs_1_.back_ref, bf16[2048,768]{1,0:T(8,128)(2,1)} %all-gather.9.cloned.1.call-done.w_ref.refs_2_, ...), custom_call_target="tpu_custom_call" | custom-call | flops 8589934592 | bytes 18874368 | tf_op jit(solution)/shard_map/pallas_call | solution.py:62
  396.5 7.4 %collective-permute-done.22 = bf16[1024,2048]{1,0:T(8,128)(2,1)S(1)} collective-permute-done((bf16[1024,2048]{1,0:T(8,128)(2,1)}, bf16[1024,2048]{1,0:T(8,128)(2,1)S(1)}, u32[]{:S(2)}, u32[]{:S(2)}) %collective-permute-start.22) | collective-permute-done | bytes 4194336 | tf_op jit(solution)/shard_map/ppermute | solution.py:485
  403.9 5.2 add_convert_fusion.2
  410.7 14.1 %shard_map.227 = (bf16[2048,768]{1,0:T(8,128)(2,1)}, f32[2048,128]{1,0:T(8,128)}) custom-call(bf16[1024,2048]{1,0:T(8,128)(2,1)} %copy-done.36, bf16[1024,2048]{1,0:T(8,128)(2,1)} %collective-permute-done.21.nb_ref, bf16[1024,2048]{1,0:T(8,128)(2,1)} %constant_dynamic-update-slice_fusion.6.da_ref, bf16[1024,2048]{1,0:T(8,128)(2,1)} %collective-permute-done.15.db_ref, ...), custom_call_target="tpu_custom_call" | custom-call | flops 6442450944 | bytes 27262976 | tf_op jit(solution)/shard_map/pallas_call | solution.py:62
  424.7 9.8 %collective-permute-done.23 = bf16[256,2048]{1,0:T(8,128)(2,1)S(1)} collective-permute-done((bf16[256,2048]{1,0:T(8,128)(2,1)}, bf16[256,2048]{1,0:T(8,128)(2,1)S(1)}, u32[]{:S(2)}, u32[]{:S(2)}) %collective-permute-start.23) | collective-permute-done | bytes 1048608 | tf_op jit(solution)/shard_map/ppermute | solution.py:485
  440.0 10.5 %collective-permute-done.25 = bf16[128,2048]{1,0:T(8,128)(2,1)} collective-permute-done((bf16[128,2048]{1,0:T(8,128)(2,1)S(1)}, bf16[128,2048]{1,0:T(8,128)(2,1)}, u32[]{:S(2)}, u32[]{:S(2)}) %collective-permute-start.25) | collective-permute-done | bytes 524320 | tf_op jit(solution)/shard_map/ppermute | solution.py:485
  454.0 4.4 all-to-all-start.4
  458.4 12.7 %shard_map.228 = (bf16[1024,2048]{1,0:T(8,128)(2,1)}, bf16[1024,2048]{1,0:T(8,128)(2,1)}) custom-call(bf16[2048,256]{1,0:T(8,128)(2,1)} %get-tuple-element.247.act_ref.refs_0_, bf16[2048,256]{1,0:T(8,128)(2,1)} %get-tuple-element.237.act_ref.refs_1_, bf16[2048,768]{1,0:T(8,128)(2,1)} %all-gather.9.cloned.1.call-done.w_ref.refs_2_, ...), custom_call_target="tpu_custom_call" | custom-call | flops 4294967296 | bytes 16777216 | tf_op jit(solution)/shard_map/pallas_call | solution.py:62
  471.0 9.4 %collective-permute-done.27 = bf16[128,2048]{1,0:T(8,128)(2,1)} collective-permute-done((bf16[128,2048]{1,0:T(8,128)(2,1)}, bf16[128,2048]{1,0:T(8,128)(2,1)}, u32[]{:S(2)}, u32[]{:S(2)}) %collective-permute-start.27) | collective-permute-done | bytes 524320 | tf_op jit(solution)/shard_map/ppermute | solution.py:509
  488.9 8.1 %collective-permute-done.28 = bf16[64,2048]{1,0:T(8,128)(2,1)S(1)} collective-permute-done((bf16[64,2048]{1,0:T(8,128)(2,1)S(1)}, bf16[64,2048]{1,0:T(8,128)(2,1)S(1)}, u32[]{:S(2)}, u32[]{:S(2)}) %collective-permute-start.28) | collective-permute-done | bytes 262176 | tf_op jit(solution)/shard_map/ppermute | solution.py:485
  502.3 7.2 %collective-permute-done.30 = bf16[128,2048]{1,0:T(8,128)(2,1)S(1)} collective-permute-done((bf16[128,2048]{1,0:T(8,128)(2,1)S(1)}, bf16[128,2048]{1,0:T(8,128)(2,1)S(1)}, u32[]{:S(2)}, u32[]{:S(2)}) %collective-permute-start.30) | collective-permute-done | bytes 524320 | tf_op jit(solution)/shard_map/ppermute | solution.py:485
  510.9 11.1 %reduce-scatter.7.cloned.1.call-done = bf16[1024,768]{1,0:T(8,128)(2,1)} async-done(((bf16[2048,768]{1,0:T(8,128)(2,1)}), bf16[1024,768]{1,0:T(8,128)(2,1)}) %reduce-scatter.7.cloned.1.call-update) | async-done | bytes 1572880 | tf_op jit(solution)/shard_map/reduce_scatter | solution.py:636
  528.7 4.4 all-to-all-start.5
  533.1 5.5 collective-permute-done.32.b_ref.bb
  538.6 5.0 shard_map.229
  543.7 4.4 add_convert_fusion
  551.3 20.7 %shard_map.230 = (bf16[1024,256]{1,0:T(8,128)(2,1)}, bf16[1024,256]{1,0:T(8,128)(2,1)}, bf16[1024,256]{1,0:T(8,128)(2,1)}, bf16[2048,896]{1,0:T(8,128)(2,1)}) custom-call(bf16[512,2048]{1,0:T(8,128)(2,1)} %constant_dynamic-update-slice_fusion.18.a_ref.ba, bf16[512,2048]{1,0:T(8,128)(2,1)} %collective-permute-done.32.b_ref.bb, ...), custom_call_target="tpu_custom_call" | custom-call | flops 4294967296 | bytes 16777216 | tf_op jit(solution)/shard_map/pallas_call | solution.py:426
  572.1 4.9 collective-permute-done.34
  578.9 8.3 %shard_map.231 = (bf16[512,2048]{1,0:T(8,128)(2,1)}, bf16[512,2048]{1,0:T(8,128)(2,1)}) custom-call(bf16[1024,256]{1,0:T(8,128)(2,1)} %get-tuple-element.287.refs_0_, bf16[1024,256]{1,0:T(8,128)(2,1)} %get-tuple-element.288.refs_1_, bf16[1024,256]{1,0:T(8,128)(2,1)} %get-tuple-element.289.refs_2_, ...), custom_call_target="tpu_custom_call" | custom-call | flops 3221225472 | bytes 13107200 | tf_op jit(solution)/shard_map/pallas_call | solution.py:62
  592.7 11.5 %collective-permute-done.37 = bf16[128,2048]{1,0:T(8,128)(2,1)S(1)} collective-permute-done((bf16[128,2048]{1,0:T(8,128)(2,1)S(1)}, bf16[128,2048]{1,0:T(8,128)(2,1)S(1)}, u32[]{:S(2)}, u32[]{:S(2)}) %collective-permute-start.37) | collective-permute-done | bytes 524320 | tf_op jit(solution)/shard_map/ppermute | solution.py:485
  613.5 10.5 %shard_map.233 = (f32[64,8192]{1,0:T(8,128)}, f32[64,8192]{1,0:T(8,128)}, f32[64,8192]{1,0:T(8,128)}) custom-call(bf16[16,64,768]{2,1,0:T(8,128)(2,1)} %copy-done.1, bf16[16,64,768]{2,1,0:T(8,128)(2,1)} %all-to-all-done.5.refs_1_), custom_call_target="tpu_custom_call" | custom-call | bytes 9437184 | tf_op jit(solution)/shard_map/pallas_call | solution.py:62
  624.2 26.0 %collective-permute-done.41 = bf16[128,2048]{1,0:T(8,128)(2,1)} collective-permute-done((bf16[128,2048]{1,0:T(8,128)(2,1)}, bf16[128,2048]{1,0:T(8,128)(2,1)}, u32[]{:S(2)}, u32[]{:S(2)}) %collective-permute-start.41) | collective-permute-done | bytes 524320 | tf_op jit(solution)/shard_map/ppermute | solution.py:509
  654.6 3.5 collective-permute-done.42
  660.5 3.6 all-to-all-start.6
  667.4 13.4 %all-to-all-done.6.refs_0_ = bf16[8,64,1152]{2,1,0:T(8,128)(2,1)S(1)} async-done(((bf16[8,64,1152]{2,1,0:T(8,128)(2,1)}), bf16[8,64,1152]{2,1,0:T(8,128)(2,1)S(1)}, u32[]{:S(2)}, u32[]{:S(2)}) %all-to-all-start.6) | async-done | bytes 1179680 | tf_op jit(solution)/shard_map/all_to_all | solution.py:630
  681.8 5.5 shard_map.232
  (281 shorter events, 150.1 us)
Async XLA Ops:
  7.2 63.0 %all-gather.7.cloned.1.call-start = ((), (), s32[]{:S(2)}) async-start(), calls=%async_computation.12 | async-start | bytes 1392640 | tf_op jit(solution)/shard_map/all_gather | solution.py:633
  17.9 19.2 %all-to-all-start = ((bf16[8,64,896]{2,1,0:T(8,128)(2,1)}), bf16[8,64,896]{2,1,0:T(8,128)(2,1)S(1)}, u32[]{:S(2)}, u32[]{:S(2)}) async-start(bf16[8,64,896]{2,1,0:T(8,128)(2,1)} %shard_map.220), calls=%async_computation | async-start | bytes 1835008 | tf_op jit(solution)/shard_map/all_to_all | solution.py:630
  23.1 84.5 %all-gather.5.cloned.1.call-start = ((), (), s32[]{:S(2)}) async-start(), calls=%async_computation.11 | async-start | bytes 3932160 | tf_op jit(solution)/shard_map/all_gather | solution.py:633
  38.8 13.8 %collective-permute-start.2 = (bf16[128,2048]{1,0:T(8,128)(2,1)S(1)}, bf16[128,2048]{1,0:T(8,128)(2,1)S(1)}, u32[]{:S(2)}, u32[]{:S(2)}) collective-permute-start(bf16[128,2048]{1,0:T(8,128)(2,1)S(1)} %bitcast.73), channel_id=1, source_target_pairs={{0,8},{8,0},{1,9},{9,1},{2,10},{10,2},{3,11},{11,3},{4,12},{12,4},... | collective-permute-start | bytes 1572872 | tf_op jit(solution)/shard_map/ppermute | solution.py:509
  40.5 12.2 %collective-permute-start = (bf16[64,2048]{1,0:T(8,128)(2,1)S(1)}, bf16[64,2048]{1,0:T(8,128)(2,1)S(1)}, u32[]{:S(2)}, u32[]{:S(2)}) collective-permute-start(bf16[64,2048]{1,0:T(8,128)(2,1)S(1)} %get-tuple-element.169), channel_id=1, source_target_pairs={{0,2},{1,3},{2,0},{3,1},{4,6},{5,7},{6,4},{7,5},{8,10},{9,11},{10,... | collective-permute-start | bytes 786440 | tf_op jit(solution)/shard_map/ppermute | solution.py:485
  41.0 11.6 %collective-permute-start.1 = (bf16[64,2048]{1,0:T(8,128)(2,1)S(1)}, bf16[64,2048]{1,0:T(8,128)(2,1)S(1)}, u32[]{:S(2)}, u32[]{:S(2)}) collective-permute-start(bf16[64,2048]{1,0:T(8,128)(2,1)S(1)} %get-tuple-element.170), channel_id=1, source_target_pairs={{0,4},{1,5},{2,6},{3,7},{4,0},{5,1},{6,2},{7,3},{8,12},{9,13},{10,... | collective-permute-start | bytes 786440 | tf_op jit(solution)/shard_map/ppermute | solution.py:485
  52.8 12.9 %collective-permute-start.3 = (bf16[128,2048]{1,0:T(8,128)(2,1)S(1)}, bf16[128,2048]{1,0:T(8,128)(2,1)S(1)}, u32[]{:S(2)}, u32[]{:S(2)}) collective-permute-start(bf16[128,2048]{1,0:T(8,128)(2,1)S(1)} %get-tuple-element.174), channel_id=1, source_target_pairs={{0,4},{1,5},{2,6},{3,7},{4,0},{5,1},{6,2},{7,3},{8,12},{9,13},{10,... | collective-permute-start | bytes 1572872 | tf_op jit(solution)/shard_map/ppermute | solution.py:485
  54.2 12.8 %collective-permute-start.4 = (bf16[128,2048]{1,0:T(8,128)(2,1)S(1)}, bf16[128,2048]{1,0:T(8,128)(2,1)S(1)}, u32[]{:S(2)}, u32[]{:S(2)}) collective-permute-start(bf16[128,2048]{1,0:T(8,128)(2,1)S(1)} %get-tuple-element.175), channel_id=1, source_target_pairs={{0,2},{1,3},{2,0},{3,1},{4,6},{5,7},{6,4},{7,5},{8,10},{9,11},{10,... | collective-permute-start | bytes 1572872 | tf_op jit(solution)/shard_map/ppermute | solution.py:485
  70.1 31.3 %collective-permute-start.5 = (bf16[512,2048]{1,0:T(8,128)(2,1)}, bf16[512,2048]{1,0:T(8,128)(2,1)}, u32[]{:S(2)}, u32[]{:S(2)}) collective-permute-start(bf16[512,2048]{1,0:T(8,128)(2,1)} %constant_dynamic-update-slice_fusion.xa), channel_id=1, source_target_pairs={{0,1},{1,0},{2,3},{3,2},{4,5},{5,4},{6,7},{7,6},{8,9},{9,8},{10,11... | collective-permute-start | bytes 6291464 | tf_op jit(solution)/shard_map/ppermute | solution.py:485
  74.4 24.7 %all-to-all-start.1 = ((bf16[8,4,64,384]{3,2,1,0:T(8,128)(2,1)}), bf16[8,4,64,384]{3,2,1,0:T(8,128)(2,1)S(1)}, u32[]{:S(2)}, u32[]{:S(2)}) async-start(bf16[8,4,64,384]{3,2,1,0:T(8,128)(2,1)} %copy.35), calls=%async_computation.1 | async-start | bytes 3145728 | tf_op jit(solution)/shard_map/all_to_all | solution.py:630
  107.6 26.6 %all-to-all-start.2 = ((bf16[16,64,768]{2,1,0:T(8,128)(2,1)}), bf16[16,64,768]{2,1,0:T(8,128)(2,1)S(1)}, u32[]{:S(2)}, u32[]{:S(2)}) async-start(bf16[16,64,768]{2,1,0:T(8,128)(2,1)} %get-tuple-element.202), calls=%async_computation.2 | async-start | bytes 3145728 | tf_op jit(solution)/shard_map/all_to_all | solution.py:630
  111.4 102.5 %all-gather.9.cloned.1.call-start = ((), (), s32[]{:S(2)}) async-start(), calls=%async_computation.13 | async-start | bytes 4718592 | tf_op jit(solution)/shard_map/all_gather | solution.py:633
  130.7 16.1 %collective-permute-start.6 = (bf16[512,2176]{1,0:T(8,128)(2,1)}, bf16[512,2176]{1,0:T(8,128)(2,1)}, u32[]{:S(2)}, u32[]{:S(2)}) collective-permute-start(bf16[512,2176]{1,0:T(8,128)(2,1)} %get-tuple-element.191), channel_id=1, source_target_pairs={{0,1},{1,0},{2,3},{3,2},{4,5},{5,4},{6,7},{7,6},{8,9},{9,8},{10,11... | collective-permute-start | bytes 6684680 | tf_op jit(solution)/shard_map/ppermute | solution.py:485
  131.1 14.2 %collective-permute-start.7 = (bf16[128,2048]{1,0:T(8,128)(2,1)S(1)}, bf16[128,2048]{1,0:T(8,128)(2,1)}, u32[]{:S(2)}, u32[]{:S(2)}) collective-permute-start(bf16[128,2048]{1,0:T(8,128)(2,1)S(1)} %bitcast.74), channel_id=1, source_target_pairs={{0,2},{1,3},{2,0},{3,1},{4,6},{5,7},{6,4},{7,5},{8,10},{9,11},{10,... | collective-permute-start | bytes 1572872 | tf_op jit(solution)/shard_map/ppermute | solution.py:485
  132.8 14.0 %collective-permute-start.8 = (bf16[128,2048]{1,0:T(8,128)(2,1)S(1)}, bf16[128,2048]{1,0:T(8,128)(2,1)}, u32[]{:S(2)}, u32[]{:S(2)}) collective-permute-start(bf16[128,2048]{1,0:T(8,128)(2,1)S(1)} %copy-done.20), channel_id=1, source_target_pairs={{0,4},{1,5},{2,6},{3,7},{4,0},{5,1},{6,2},{7,3},{8,12},{9,13},{10,... | collective-permute-start | bytes 1572872 | tf_op jit(solution)/shard_map/ppermute | solution.py:485
  146.8 60.9 %all-to-all-start.3 = ((bf16[16,64,768]{2,1,0:T(8,128)(2,1)}), bf16[16,64,768]{2,1,0:T(8,128)(2,1)S(1)}, u32[]{:S(2)}, u32[]{:S(2)}) async-start(bf16[16,64,768]{2,1,0:T(8,128)(2,1)} %get-tuple-element.203), calls=%async_computation.3 | async-start | bytes 3145728 | tf_op jit(solution)/shard_map/all_to_all | solution.py:630
  150.6 151.2 %all-gather.11.cloned.1.call-start = ((), (), s32[]{:S(2)}) async-start(), calls=%async_computation.14 | async-start | bytes 4718592 | tf_op jit(solution)/shard_map/all_gather | solution.py:633
  154.6 51.3 %collective-permute-start.11 = (bf16[256,2048]{1,0:T(8,128)(2,1)S(1)}, bf16[256,2048]{1,0:T(8,128)(2,1)S(1)}, u32[]{:S(2)}, u32[]{:S(2)}) collective-permute-start(bf16[256,2048]{1,0:T(8,128)(2,1)S(1)} %pad_maximum_fusion.2), channel_id=1, source_target_pairs={{0,4},{1,5},{2,6},{3,7},{4,0},{5,1},{6,2},{7,3},{8,12},{9,13},{10,... | collective-permute-start | bytes 3145736 | tf_op jit(solution)/shard_map/ppermute | solution.py:485
  156.6 51.1 %collective-permute-start.12 = (bf16[256,2048]{1,0:T(8,128)(2,1)S(1)}, bf16[256,2048]{1,0:T(8,128)(2,1)}, u32[]{:S(2)}, u32[]{:S(2)}) collective-permute-start(bf16[256,2048]{1,0:T(8,128)(2,1)S(1)} %pad_maximum_fusion.3), channel_id=1, source_target_pairs={{0,2},{1,3},{2,0},{3,1},{4,6},{5,7},{6,4},{7,5},{8,10},{9,11},{10,... | collective-permute-start | bytes 3145736 | tf_op jit(solution)/shard_map/ppermute | solution.py:485
  158.1 46.9 %collective-permute-start.9 = (bf16[128,2176]{1,0:T(8,128)(2,1)S(1)}, bf16[128,2176]{1,0:T(8,128)(2,1)S(1)}, u32[]{:S(2)}, u32[]{:S(2)}) collective-permute-start(bf16[128,2176]{1,0:T(8,128)(2,1)S(1)} %get-tuple-element.198), channel_id=1, source_target_pairs={{0,4},{1,5},{2,6},{3,7},{4,0},{5,1},{6,2},{7,3},{8,12},{9,13},{10,... | collective-permute-start | bytes 1671176 | tf_op jit(solution)/shard_map/ppermute | solution.py:485
  158.6 47.3 %collective-permute-start.10 = (bf16[128,2176]{1,0:T(8,128)(2,1)S(1)}, bf16[128,2176]{1,0:T(8,128)(2,1)S(1)}, u32[]{:S(2)}, u32[]{:S(2)}) collective-permute-start(bf16[128,2176]{1,0:T(8,128)(2,1)S(1)} %get-tuple-element.199), channel_id=1, source_target_pairs={{0,2},{1,3},{2,0},{3,1},{4,6},{5,7},{6,4},{7,5},{8,10},{9,11},{10,... | collective-permute-start | bytes 1671176 | tf_op jit(solution)/shard_map/ppermute | solution.py:485
  222.9 228.6 %reduce-scatter.5.cloned.1.call-start = ((), (), s32[]{:S(2)}) async-start(), calls=%async_computation.15 | async-start | bytes 4718592 | tf_op jit(solution)/shard_map/reduce_scatter | solution.py:636
  236.3 24.1 %collective-permute-start.16 = (bf16[128,2048]{1,0:T(8,128)(2,1)S(1)}, bf16[128,2048]{1,0:T(8,128)(2,1)S(1)}, u32[]{:S(2)}, u32[]{:S(2)}) collective-permute-start(bf16[128,2048]{1,0:T(8,128)(2,1)S(1)} %get-tuple-element.213), channel_id=1, source_target_pairs={{0,8},{8,0},{1,9},{9,1},{2,10},{10,2},{3,11},{11,3},{4,12},{12,4},... | collective-permute-start | bytes 1572872 | tf_op jit(solution)/shard_map/ppermute | solution.py:509
  260.4 41.4 %collective-permute-start.17 = (bf16[128,2048]{1,0:T(8,128)(2,1)S(1)}, bf16[128,2048]{1,0:T(8,128)(2,1)}, u32[]{:S(2)}, u32[]{:S(2)}) collective-permute-start(bf16[128,2048]{1,0:T(8,128)(2,1)S(1)} %get-tuple-element.213), channel_id=1, source_target_pairs={{0,2},{1,3},{2,0},{3,1},{4,6},{5,7},{6,4},{7,5},{8,10},{9,11},{10,... | collective-permute-start | bytes 1572872 | tf_op jit(solution)/shard_map/ppermute | solution.py:485
  261.2 40.6 %collective-permute-start.18 = (bf16[128,2048]{1,0:T(8,128)(2,1)S(1)}, bf16[128,2048]{1,0:T(8,128)(2,1)S(1)}, u32[]{:S(2)}, u32[]{:S(2)}) collective-permute-start(bf16[128,2048]{1,0:T(8,128)(2,1)S(1)} %collective-permute-done.16), channel_id=1, source_target_pairs={{0,4},{1,5},{2,6},{3,7},{4,0},{5,1},{6,2},{7,3},{8,12},{9,13},{10,... | collective-permute-start | bytes 1572872 | tf_op jit(solution)/shard_map/ppermute | solution.py:485
  303.2 25.0 %collective-permute-start.19 = (bf16[256,2048]{1,0:T(8,128)(2,1)S(1)}, bf16[256,2048]{1,0:T(8,128)(2,1)S(1)}, u32[]{:S(2)}, u32[]{:S(2)}) collective-permute-start(bf16[256,2048]{1,0:T(8,128)(2,1)S(1)} %pad_maximum_fusion.4), channel_id=1, source_target_pairs={{0,4},{1,5},{2,6},{3,7},{4,0},{5,1},{6,2},{7,3},{8,12},{9,13},{10,... | collective-permute-start | bytes 3145736 | tf_op jit(solution)/shard_map/ppermute | solution.py:485
  304.7 24.6 %collective-permute-start.20 = (bf16[256,2048]{1,0:T(8,128)(2,1)S(1)}, bf16[256,2048]{1,0:T(8,128)(2,1)S(1)}, u32[]{:S(2)}, u32[]{:S(2)}) collective-permute-start(bf16[256,2048]{1,0:T(8,128)(2,1)S(1)} %pad_maximum_fusion.5), channel_id=1, source_target_pairs={{0,2},{1,3},{2,0},{3,1},{4,6},{5,7},{6,4},{7,5},{8,10},{9,11},{10,... | collective-permute-start | bytes 3145736 | tf_op jit(solution)/shard_map/ppermute | solution.py:485
  366.3 155.6 %reduce-scatter.7.cloned.1.call-start = ((), (), s32[]{:S(2)}) async-start(), calls=%async_computation.16 | async-start | bytes 4718592 | tf_op jit(solution)/shard_map/reduce_scatter | solution.py:636
  409.1 25.4 %collective-permute-start.23 = (bf16[256,2048]{1,0:T(8,128)(2,1)}, bf16[256,2048]{1,0:T(8,128)(2,1)S(1)}, u32[]{:S(2)}, u32[]{:S(2)}) collective-permute-start(bf16[256,2048]{1,0:T(8,128)(2,1)} %get-tuple-element.235), channel_id=1, source_target_pairs={{0,4},{1,5},{2,6},{3,7},{4,0},{5,1},{6,2},{7,3},{8,12},{9,13},{10,... | collective-permute-start | bytes 3145736 | tf_op jit(solution)/shard_map/ppermute | solution.py:485
  409.2 25.4 %collective-permute-start.24 = (bf16[256,2048]{1,0:T(8,128)(2,1)}, bf16[256,2048]{1,0:T(8,128)(2,1)}, u32[]{:S(2)}, u32[]{:S(2)}) collective-permute-start(bf16[256,2048]{1,0:T(8,128)(2,1)} %get-tuple-element.236), channel_id=1, source_target_pairs={{0,2},{1,3},{2,0},{3,1},{4,6},{5,7},{6,4},{7,5},{8,10},{9,11},{10,... | collective-permute-start | bytes 3145736 | tf_op jit(solution)/shard_map/ppermute | solution.py:485
  437.1 13.4 %collective-permute-start.25 = (bf16[128,2048]{1,0:T(8,128)(2,1)S(1)}, bf16[128,2048]{1,0:T(8,128)(2,1)}, u32[]{:S(2)}, u32[]{:S(2)}) collective-permute-start(bf16[128,2048]{1,0:T(8,128)(2,1)S(1)} %get-tuple-element.242), channel_id=1, source_target_pairs={{0,2},{1,3},{2,0},{3,1},{4,6},{5,7},{6,4},{7,5},{8,10},{9,11},{10,... | collective-permute-start | bytes 1572872 | tf_op jit(solution)/shard_map/ppermute | solution.py:485
  438.5 13.0 %collective-permute-start.26 = (bf16[128,2048]{1,0:T(8,128)(2,1)S(1)}, bf16[128,2048]{1,0:T(8,128)(2,1)S(1)}, u32[]{:S(2)}, u32[]{:S(2)}) collective-permute-start(bf16[128,2048]{1,0:T(8,128)(2,1)S(1)} %get-tuple-element.243), channel_id=1, source_target_pairs={{0,4},{1,5},{2,6},{3,7},{4,0},{5,1},{6,2},{7,3},{8,12},{9,13},{10,... | collective-permute-start | bytes 1572872 | tf_op jit(solution)/shard_map/ppermute | solution.py:485
  454.0 26.5 %collective-permute-start.27 = (bf16[128,2048]{1,0:T(8,128)(2,1)}, bf16[128,2048]{1,0:T(8,128)(2,1)}, u32[]{:S(2)}, u32[]{:S(2)}) collective-permute-start(bf16[128,2048]{1,0:T(8,128)(2,1)} %add_convert_fusion.12), channel_id=1, source_target_pairs={{0,8},{8,0},{1,9},{9,1},{2,10},{10,2},{3,11},{11,3},{4,12},{12,4},... | collective-permute-start | bytes 1572872 | tf_op jit(solution)/shard_map/ppermute | solution.py:509
  454.0 56.9 %all-to-all-start.4 = ((bf16[16,64,768]{2,1,0:T(8,128)(2,1)}), bf16[16,64,768]{2,1,0:T(8,128)(2,1)S(1)}, u32[]{:S(2)}, u32[]{:S(2)}) async-start(bf16[16,64,768]{2,1,0:T(8,128)(2,1)} %bitcast.80), calls=%async_computation.5 | async-start | bytes 3145728 | tf_op jit(solution)/shard_map/all_to_all | solution.py:630
  487.8 10.9 %collective-permute-start.29 = (bf16[64,2048]{1,0:T(8,128)(2,1)S(1)}, bf16[64,2048]{1,0:T(8,128)(2,1)S(1)}, u32[]{:S(2)}, u32[]{:S(2)}) collective-permute-start(bf16[64,2048]{1,0:T(8,128)(2,1)S(1)} %get-tuple-element.254), channel_id=1, source_target_pairs={{0,4},{1,5},{2,6},{3,7},{4,0},{5,1},{6,2},{7,3},{8,12},{9,13},{10,... | collective-permute-start | bytes 786440 | tf_op jit(solution)/shard_map/ppermute | solution.py:485
  499.3 11.6 %collective-permute-start.31 = (bf16[128,2048]{1,0:T(8,128)(2,1)S(1)}, bf16[128,2048]{1,0:T(8,128)(2,1)}, u32[]{:S(2)}, u32[]{:S(2)}) collective-permute-start(bf16[128,2048]{1,0:T(8,128)(2,1)S(1)} %pad_maximum_fusion.11), channel_id=1, source_target_pairs={{0,2},{1,3},{2,0},{3,1},{4,6},{5,7},{6,4},{7,5},{8,10},{9,11},{10,... | collective-permute-start | bytes 1572872 | tf_op jit(solution)/shard_map/ppermute | solution.py:485
  528.7 43.4 %all-to-all-start.5 = ((bf16[16,64,768]{2,1,0:T(8,128)(2,1)}), bf16[16,64,768]{2,1,0:T(8,128)(2,1)}, u32[]{:S(2)}, u32[]{:S(2)}) async-start(bf16[16,64,768]{2,1,0:T(8,128)(2,1)} %bitcast.79), calls=%async_computation.7 | async-start | bytes 3145728 | tf_op jit(solution)/shard_map/all_to_all | solution.py:630
  533.1 44.8 %reduce-scatter.9.cloned.1.call-start = ((), (), s32[]{:S(2)}) async-start(), calls=%async_computation.17 | async-start | bytes 1310720 | tf_op jit(solution)/shard_map/reduce_scatter | solution.py:636
  548.1 110.1 %reduce-scatter.11.cloned.1.call-start = ((), (), s32[]{:S(2)}) async-start(), calls=%async_computation.18 | async-start | bytes 4587520 | tf_op jit(solution)/shard_map/reduce_scatter | solution.py:636
  548.3 28.6 %collective-permute-start.34 = (bf16[256,2048]{1,0:T(8,128)(2,1)}, bf16[256,2048]{1,0:T(8,128)(2,1)}, u32[]{:S(2)}, u32[]{:S(2)}) collective-permute-start(bf16[256,2048]{1,0:T(8,128)(2,1)} %get-tuple-element.283), channel_id=1, source_target_pairs={{0,4},{1,5},{2,6},{3,7},{4,0},{5,1},{6,2},{7,3},{8,12},{9,13},{10,... | collective-permute-start | bytes 3145736 | tf_op jit(solution)/shard_map/ppermute | solution.py:485
  549.9 28.0 %collective-permute-start.35 = (bf16[256,2048]{1,0:T(8,128)(2,1)}, bf16[256,2048]{1,0:T(8,128)(2,1)S(1)}, u32[]{:S(2)}, u32[]{:S(2)}) collective-permute-start(bf16[256,2048]{1,0:T(8,128)(2,1)} %get-tuple-element.284), channel_id=1, source_target_pairs={{0,2},{1,3},{2,0},{3,1},{4,6},{5,7},{6,4},{7,5},{8,10},{9,11},{10,... | collective-permute-start | bytes 3145736 | tf_op jit(solution)/shard_map/ppermute | solution.py:485
  589.8 15.2 %collective-permute-start.36 = (bf16[512,2048]{1,0:T(8,128)(2,1)S(1)}, bf16[512,2048]{1,0:T(8,128)(2,1)S(1)}, u32[]{:S(2)}, u32[]{:S(2)}) collective-permute-start(bf16[512,2048]{1,0:T(8,128)(2,1)S(1)} %copy-done.43), channel_id=1, source_target_pairs={{0,1},{1,0},{2,3},{3,2},{4,5},{5,4},{6,7},{7,6},{8,9},{9,8},{10,11... | collective-permute-start | bytes 6291464 | tf_op jit(solution)/shard_map/ppermute | solution.py:485
  589.9 14.3 %collective-permute-start.37 = (bf16[128,2048]{1,0:T(8,128)(2,1)S(1)}, bf16[128,2048]{1,0:T(8,128)(2,1)S(1)}, u32[]{:S(2)}, u32[]{:S(2)}) collective-permute-start(bf16[128,2048]{1,0:T(8,128)(2,1)S(1)} %get-tuple-element.293), channel_id=1, source_target_pairs={{0,2},{1,3},{2,0},{3,1},{4,6},{5,7},{6,4},{7,5},{8,10},{9,11},{10,... | collective-permute-start | bytes 1572872 | tf_op jit(solution)/shard_map/ppermute | solution.py:485
  590.2 14.8 %collective-permute-start.38 = (bf16[128,2048]{1,0:T(8,128)(2,1)S(1)}, bf16[128,2048]{1,0:T(8,128)(2,1)S(1)}, u32[]{:S(2)}, u32[]{:S(2)}) collective-permute-start(bf16[128,2048]{1,0:T(8,128)(2,1)S(1)} %get-tuple-element.294), channel_id=1, source_target_pairs={{0,4},{1,5},{2,6},{3,7},{4,0},{5,1},{6,2},{7,3},{8,12},{9,13},{10,... | collective-permute-start | bytes 1572872 | tf_op jit(solution)/shard_map/ppermute | solution.py:485
  609.1 15.0 %collective-permute-start.39 = (bf16[128,2048]{1,0:T(8,128)(2,1)}, bf16[128,2048]{1,0:T(8,128)(2,1)}, u32[]{:S(2)}, u32[]{:S(2)}) collective-permute-start(bf16[128,2048]{1,0:T(8,128)(2,1)} %get-tuple-element.299), channel_id=1, source_target_pairs={{0,4},{1,5},{2,6},{3,7},{4,0},{5,1},{6,2},{7,3},{8,12},{9,13},{10,... | collective-permute-start | bytes 1572872 | tf_op jit(solution)/shard_map/ppermute | solution.py:485
  610.8 13.4 %collective-permute-start.40 = (bf16[128,2048]{1,0:T(8,128)(2,1)}, bf16[128,2048]{1,0:T(8,128)(2,1)}, u32[]{:S(2)}, u32[]{:S(2)}) collective-permute-start(bf16[128,2048]{1,0:T(8,128)(2,1)} %get-tuple-element.300), channel_id=1, source_target_pairs={{0,2},{1,3},{2,0},{3,1},{4,6},{5,7},{6,4},{7,5},{8,10},{9,11},{10,... | collective-permute-start | bytes 1572872 | tf_op jit(solution)/shard_map/ppermute | solution.py:485
  611.9 38.3 %collective-permute-start.41 = (bf16[128,2048]{1,0:T(8,128)(2,1)}, bf16[128,2048]{1,0:T(8,128)(2,1)}, u32[]{:S(2)}, u32[]{:S(2)}) collective-permute-start(bf16[128,2048]{1,0:T(8,128)(2,1)} %add_convert_fusion.7), channel_id=1, source_target_pairs={{0,8},{8,0},{1,9},{9,1},{2,10},{10,2},{3,11},{11,3},{4,12},{12,4},... | collective-permute-start | bytes 1572872 | tf_op jit(solution)/shard_map/ppermute | solution.py:509
  660.5 20.3 %all-to-all-start.6 = ((bf16[8,64,1152]{2,1,0:T(8,128)(2,1)}), bf16[8,64,1152]{2,1,0:T(8,128)(2,1)S(1)}, u32[]{:S(2)}, u32[]{:S(2)}) async-start(bf16[8,64,1152]{2,1,0:T(8,128)(2,1)} %bitcast.72), calls=%async_computation.10 | async-start | bytes 2359296 | tf_op jit(solution)/shard_map/all_to_all | solution.py:630
  (55 other events, 471.8 us)
Sparse Core Ops, SparseCore 0:
  10.2 31.8 all-gather.6
  43.6 64.0 all-gather.4
  135.6 78.2 all-gather.8
  223.0 78.7 all-gather.10
  366.5 76.2 reduce-scatter.4
  445.0 76.9 reduce-scatter.6
  548.2 26.1 reduce-scatter.8
  578.1 78.4 reduce-scatter.10

commit v4 on v3

--- a/solution.py
+++ b/solution.py
@@ -240,10 +240,10 @@
     )(*x_pair, gain, w_qko, w_qko, w_v, w_qko, *constants)
 
 
-def ffn_kernel(na_ref, nb_ref, da_ref, db_ref, w_ref, act_ref, back_ref):
+def ffn_kernel(na_ref, nb_ref, da_ref, db_ref, gu_ref, down_ref, act_ref, back_ref):
     cols = act_ref.shape[1]
-    gated = dot(either((na_ref, nb_ref)), w_ref[:, : 2 * cols])
-    grad_act = dot(either((da_ref, db_ref)), w_ref[:, 2 * cols :])
+    gated = dot(either((na_ref, nb_ref)), gu_ref[...])
+    grad_act = dot(either((da_ref, db_ref)), down_ref[...])
     gate, up = gated[:, :cols], gated[:, cols:]
     sig = jax.nn.sigmoid(gate)
     silu = gate * sig
@@ -254,13 +254,13 @@
 
 def ffn(n_pair, d_pair, w):
     length, width = 2 * n_pair[0].shape[0], n_pair[0].shape[1]
-    cols = w.shape[1] // 3
+    cols = w.cols
     tile = min(2 * TILE, length // 2)
     return call(
         ffn_kernel,
         length // tile,
-        (*n_pair, *d_pair, w),
-        pair_specs(length, width, tile) * 2 + [whole(w.shape)],
+        (*n_pair, *d_pair, w.gated, w.down),
+        pair_specs(length, width, tile) * 2 + w.specs(),
         [
             jax.ShapeDtypeStruct((length, cols), bf16),
             jax.ShapeDtypeStruct((length, 2 * cols), bf16),
@@ -279,12 +279,12 @@
     return t_dot(pair[0][...], right[:half, :]) + t_dot(pair[1][...], right[half:, :])
 
 
-def ffn_sums_kernel(na_ref, nb_ref, da_ref, db_ref, act_ref, back_ref, w_ref, sum_ref, gain_ref):
+def ffn_sums_kernel(na_ref, nb_ref, da_ref, db_ref, act_ref, back_ref, gu_ref, sum_ref, gain_ref):
     cols = act_ref.shape[1]
     gated = t_dot_pair((na_ref, nb_ref), back_ref)
     sum_ref[:, : 2 * cols] = gated.astype(bf16)
     sum_ref[:, 2 * cols :] = t_dot_pair((da_ref, db_ref), act_ref).astype(bf16)
-    gain = jnp.sum(gated * w_ref[:, : 2 * cols].astype(f32), axis=1, keepdims=True)
+    gain = jnp.sum(gated * gu_ref[...].astype(f32), axis=1, keepdims=True)
     gain_ref[...] = jnp.broadcast_to(gain, gain_ref.shape)
 
 
@@ -295,9 +295,9 @@
     return call(
         ffn_sums_kernel,
         width // tile,
-        (*n_pair, *d_pair, act, back, w),
+        (*n_pair, *d_pair, act, back, w.gated),
         [cols_of(half, tile)] * 4
-        + [whole(act.shape), whole(back.shape), rows_of(tile, 3 * cols)],
+        + [whole(act.shape), whole(back.shape), rows_of(tile, 2 * cols)],
         [
             jax.ShapeDtypeStruct((width, 3 * cols), bf16),
             jax.ShapeDtypeStruct((width, LANES), f32),
@@ -326,12 +326,9 @@
     )
 
 
-def back_kernel(count, first, *refs):
+def back_kernel(count, *refs):
     lefts, rights, outs = refs[:count], refs[count : 2 * count], refs[2 * count :]
-    total = 0.0
-    for left, right in zip(lefts, rights):
-        cols = left.shape[1]
-        total = total + dot_t(left[...], right[:, first : first + cols])
+    total = sum(dot_t(left[...], right[...]) for left, right in zip(lefts, rights))
     store_half(total.astype(bf16), outs)
 
 
@@ -340,7 +337,7 @@
     width = w_v.shape[0]
     tile, steps, outs, specs = halves(length, width)
     return call(
-        functools.partial(back_kernel, 3, 0),
+        functools.partial(back_kernel, 3),
         steps,
         (*lefts, w_qko, w_qko, w_v),
         [rows_of(tile, cols)] * 3
@@ -351,15 +348,24 @@
     )
 
 
-def back(lefts, rights, first=0):
+class Chunk:
+    def __init__(self, gated, down, at):
+        self.gated, self.down, self.at = gated, down, at
+        self.cols = down.shape[1] // (at + 1)
+
+    def specs(self):
+        return [columns(self.gated, 0, 2 * self.cols), columns(self.down, self.at, self.cols)]
+
+
+def back(lefts, chunks, which):
     length = lefts[0].shape[0]
-    width = rights[0].shape[0]
+    width = chunks[0].gated.shape[0]
     tile, steps, outs, specs = halves(length, width)
     return call(
-        functools.partial(back_kernel, len(lefts), first),
+        functools.partial(back_kernel, len(lefts)),
         steps,
-        (*lefts, *rights),
-        [rows_of(tile, a.shape[1]) for a in lefts] + [whole(a.shape) for a in rights],
+        (*lefts, *((w.gated, w.down)[which] for w in chunks)),
+        [rows_of(tile, a.shape[1]) for a in lefts] + [w.specs()[which] for w in chunks],
         outs,
         specs,
         2 * length * width * sum(a.shape[1] for a in lefts),
@@ -584,12 +590,14 @@
             self.moves, self.result = None, end.value
 
 
-def run(steps, riders=(), waits=(), then=(), late=0):
+def run(steps, riders=(), waits=(), then=(), at=None):
     main = steps if isinstance(steps, Ride) else Ride(steps)
     waits, then = list(waits), list(then)
+    stage = 0
     while main.moves is not None:
-        active = [main] + [rider for rider in riders if rider.moves is not None and late <= 0]
-        late -= 1
+        riding = riders if at is None or stage in at else ()
+        active = [main] + [rider for rider in riding if rider.moves is not None]
+        stage += 1
         got = exchange(
             [move for ride in active for move in ride.moves], waits.pop(0) if waits else ()
         )
@@ -704,7 +712,8 @@
         [[(ffn_blocks, 1)], [(w_ffn, 0), (ffn_blocks, 1)]],
         [second],
     )
-    w_ffn.append(gather_z(ffn_blocks[1], "pair"))
+    w_ffn.append(gather_z(ffn_blocks[1][:, : 2 * ffn_cols], "pair"))
+    w_ffn.append(gather_z(ffn_blocks[1][:, 2 * ffn_cols :], "pair"))
     attn_mass = attn_own[:, width]
     x_own_f = x_own.astype(f32)
     hidden_own = x_own_f + attn_own[:, :width]
@@ -718,19 +727,21 @@
     dy_all = dy_ride.result
 
     acts, backs, sums, gain_sums = [], [], [], []
+    chunks = [Chunk(w_ffn[0], w_ffn[0], 2)]
     for c in range(CHUNKS):
-        act, grads = ffn(normed_ffn, dy_all, w_ffn[c])
+        act, grads = ffn(normed_ffn, dy_all, chunks[c])
         acts.append(act)
         backs.append(grads)
         if c + 1 == CHUNKS:
             break
-        part, gains = ffn_sums(normed_ffn, dy_all, act, grads, w_ffn[c])
+        part, gains = ffn_sums(normed_ffn, dy_all, act, grads, chunks[c])
         gain_sums.append(gains)
-        acts[c], backs[c], part, w_ffn[c + 1] = lax.optimization_barrier(
-            (act, grads, part, w_ffn[c + 1])
+        acts[c], backs[c], part, w_ffn[1:] = lax.optimization_barrier(
+            (act, grads, part, w_ffn[1:])
         )
+        chunks.append(Chunk(w_ffn[1], w_ffn[2], 0))
         sums.append(scatter_z(part, "pair"))
-    grads_pair = back(backs, w_ffn)
+    grads_pair = back(backs, chunks, 0)
 
     def home(part, axes="seq"):
         return swap(part.reshape(lax.axis_size(axes), rows, -1), axes)
@@ -738,7 +749,7 @@
     made = []
 
     def last_sums():
-        part, gains = ffn_sums(normed_ffn, dy_all, acts[-1], backs[-1], w_ffn[-1])
+        part, gains = ffn_sums(normed_ffn, dy_all, acts[-1], backs[-1], chunks[-1])
         gain_sums.append(gains)
         made.append(part)
 
@@ -746,7 +757,7 @@
         sums.append(scatter_z(made[0], "pair"))
 
     def output():
-        made.append(back(acts, w_ffn, 2 * ffn_cols))
+        made.append(back(acts, chunks, 1))
 
     grad_normed_two = run(
         scatter_two(grads_pair),
@@ -761,7 +772,8 @@
     ffn_sum = [home(sums[0], near)]
     out_ride = Ride(scatter_two(made[1]))
     waits = [[], [(ffn_sum, 0), (sums, 1)]]
-    branch = run(gather_one(grad_hidden.astype(bf16)), [out_ride], waits, late=2)
+    left = len(link_bits(ns))
+    branch = run(gather_one(grad_hidden.astype(bf16)), [out_ride], waits, (), (left,))
     out_sum = branch_sums(branch, attended)
     moves = out_ride.moves
     branch, out_sum, sent = lax.optimization_barrier((branch, out_sum, [b for b, _ in moves]))
@@ -777,9 +789,10 @@
     out_ride.feed(flying)
     qkv_sum = scatter_z(qkv_local)
     part = enter_back([dq, dk, dv], w_qko, w_v)
-    grad_normed = run(scatter_one(part), [out_ride])
-    while out_ride.moves is not None:
-        out_ride.feed(exchange(out_ride.moves))
+    grad_normed = run(scatter_one(part), [out_ride], at=range(left - 1))
+    moves = out_ride.moves
+    qkv_sum, sent = lax.optimization_barrier((qkv_sum, [b for b, _ in moves]))
+    out_ride.feed([f(b) for (_, f), b in zip(moves, sent)])
     layer_out = (hidden_own + out_ride.result).astype(bf16)
     scale_one = norm_scale(x_own_f)
     input_grad = (

time: 705 us -> 679 us (0.963)
  waiting for transfers between devices: 337 us -> 303 us
  local copies, waits for them, and re-layouts: 42.8 us -> 50.8 us
    all_gather x4 -> x5, waiting for transfers between devices: 51.6 us -> 30.4 us  [gather_z(): return lax.all_gather(block, axes, axis=0, tiled=True)]
    ppermute x4, waiting for transfers between devices: 59.5 us -> 39.5 us  [swap_side(): return lax.ppermute(block, 'side', [(0, 1), (1, 0)])]
    reduce_scatter x4, waiting for transfers between devices: 11.1 us -> 24.8 us  [scatter_z(): return lax.psum_scatter(full, axes, scatter_dimension=0, tiled=True)]
    unnamed x107 -> x103, local copies, waits for them, and re-layouts: 25.4 us -> 30.5 us
  transfers between devices with their start and end apart: 59 -> 60, of which waited for: 38 -> 40; matrix products, arithmetic and copies ran while one was open for 11% -> 12% of each run, Pallas kernels for 19% -> 24%
where the time goes in v4:
time: 679 us; the launch traced here: 670 us
  waiting for transfers between devices  303 us (45%)
  Pallas kernels  164 us (24%)
  starting transfers between devices  71.6 us (11%)
  other arithmetic  66 us (10%)
  local copies, waits for them, and re-layouts  50.8 us (7%)
  between operations  14.6 us (2%)
    ppermute x40, waiting for transfers between devices, swap_bit(): return lax.ppermute(block, 'seq', [(i, i ^ bit) for i in range(size)])  175 us
    pallas_call x12, Pallas kernels, call(): pl.pallas_call(kernel, grid_spec=pltpu.PrefetchScalarGridSpec(num_scalar_...  125 us
    ppermute x4, waiting for transfers between devices, swap_side(): return lax.ppermute(block, 'side', [(0, 1), (1, 0)])  39.5 us
    ppermute x40, starting transfers between devices, swap_bit(): return lax.ppermute(block, 'seq', [(i, i ^ bit) for i in range(size)])  39.4 us
    all_to_all x7, waiting for transfers between devices, swap(): return lax.all_to_all(blocks, axes, split_axis=0, concat_axis=0, tiled=True)  33.6 us
    unnamed x103, local copies, waits for them, and re-layouts  30.5 us
    all_gather x5, waiting for transfers between devices, gather_z(): return lax.all_gather(block, axes, axis=0, tiled=True)  30.4 us
    all_to_all x7, starting transfers between devices, swap(): return lax.all_to_all(blocks, axes, split_axis=0, concat_axis=0, tiled=True)  28.2 us
  transfers between devices with their start and end apart: 60, of which 40 were waited for; matrix products, arithmetic and copies ran while one was open for 12% of the time, Pallas kernels for 24%

profile of v4, /device:TPU:0, one launch (start us, length us, event | category | flops | bytes accessed | tf_op | source)
XLA Modules:
  0.0 670.4 jit_solution(13004763685197817060)
XLA Ops:
  12.9 5.0 shard_map.220
  17.9 5.2 all-to-all-start
  25.9 11.2 %all-to-all-done = bf16[8,64,896]{2,1,0:T(8,128)(2,1)S(1)} async-done(((bf16[8,64,896]{2,1,0:T(8,128)(2,1)}), bf16[8,64,896]{2,1,0:T(8,128)(2,1)S(1)}, u32[]{:S(2)}, u32[]{:S(2)}) %all-to-all-start) | async-done | bytes 917536 | tf_op jit(solution)/shard_map/all_to_all | solution.py:638
  42.4 10.2 %shard_map.221 = (bf16[16,64,768]{2,1,0:T(8,128)(2,1)}, bf16[16,64,768]{2,1,0:T(8,128)(2,1)}) custom-call(f32[64,8192]{1,0:T(8,128)} %refs_0_.3, f32[64,8192]{1,0:T(8,128)} %refs_1_.3, bf16[64,8192]{1,0:T(8,128)(2,1)} %convert_bitcast_fusion.refs_2_), custom_call_target="tpu_custom_call" | custom-call | bytes 8388608 | tf_op jit(solution)/shard_map/pallas_call | solution.py:62
  57.4 8.2 %collective-permute-done.3 = bf16[128,2048]{1,0:T(8,128)(2,1)S(1)} collective-permute-done((bf16[128,2048]{1,0:T(8,128)(2,1)S(1)}, bf16[128,2048]{1,0:T(8,128)(2,1)S(1)}, u32[]{:S(2)}, u32[]{:S(2)}) %collective-permute-start.3) | collective-permute-done | bytes 524320 | tf_op jit(solution)/shard_map/ppermute | solution.py:491
  74.4 3.7 all-to-all-start.1
  84.3 14.8 %all-to-all-done.1 = bf16[8,4,64,384]{3,2,1,0:T(8,128)(2,1)S(1)} async-done(((bf16[8,4,64,384]{3,2,1,0:T(8,128)(2,1)}), bf16[8,4,64,384]{3,2,1,0:T(8,128)(2,1)S(1)}, u32[]{:S(2)}, u32[]{:S(2)}) %all-to-all-start.1) | async-done | bytes 1572896 | tf_op jit(solution)/shard_map/all_to_all | solution.py:638
  101.4 6.2 all-gather.6.cloned.1.call-done.wq.wk.wo.refs_3_.refs_4_
  107.6 3.8 all-to-all-start.2
  112.7 18.0 %shard_map.222 = (bf16[1024,2048]{1,0:T(8,128)(2,1)}, bf16[1024,256]{1,0:T(8,128)(2,1)}, bf16[1024,256]{1,0:T(8,128)(2,1)}, bf16[1024,256]{1,0:T(8,128)(2,1)}, b...) custom-call(bf16[512,2048]{1,0:T(8,128)(2,1)} %constant_dynamic-update-slice_fusion.xa, ...), custom_call_target="tpu_custom_call" | custom-call | flops 4294967296 | bytes 25165824 | tf_op jit(solution)/shard_map/pallas_call | solution.py:211
  135.5 9.9 %collective-permute-done.7 = bf16[128,2048]{1,0:T(8,128)(2,1)} collective-permute-done((bf16[128,2048]{1,0:T(8,128)(2,1)S(1)}, bf16[128,2048]{1,0:T(8,128)(2,1)}, u32[]{:S(2)}, u32[]{:S(2)}) %collective-permute-start.7) | collective-permute-done | bytes 524320 | tf_op jit(solution)/shard_map/ppermute | solution.py:491
  146.8 3.8 all-to-all-start.3
  161.5 43.5 %collective-permute-done.9 = bf16[128,2176]{1,0:T(8,128)(2,1)S(1)} collective-permute-done((bf16[128,2176]{1,0:T(8,128)(2,1)S(1)}, bf16[128,2176]{1,0:T(8,128)(2,1)S(1)}, u32[]{:S(2)}, u32[]{:S(2)}) %collective-permute-start.9) | collective-permute-done | bytes 557088 | tf_op jit(solution)/shard_map/ppermute | solution.py:491
  207.7 6.1 all-gather.10.cloned.1.call-done.gu_ref.down_ref.refs_2_
  227.6 5.2 collective-permute-done.13
  237.2 24.3 %collective-permute-done.16 = bf16[128,2048]{1,0:T(8,128)(2,1)} collective-permute-done((bf16[128,2048]{1,0:T(8,128)(2,1)}, bf16[128,2048]{1,0:T(8,128)(2,1)}, u32[]{:S(2)}, u32[]{:S(2)}) %collective-permute-start.16) | collective-permute-done | bytes 524320 | tf_op jit(solution)/shard_map/ppermute | solution.py:515
  263.5 18.0 %all-gather.12.cloned.1.call-done.gu_ref.refs_3_ = bf16[2048,512]{1,0:T(8,128)(2,1)} async-done(((bf16[1024,512]{1,0:T(8,128)(2,1)}), bf16[2048,512]{1,0:T(8,128)(2,1)}) %all-gather.12.cloned.1.call-update) | async-done | bytes 2097168 | tf_op jit(solution)/shard_map/all_gather | solution.py:641
  288.9 20.1 %collective-permute-done.19 = bf16[256,2048]{1,0:T(8,128)(2,1)S(1)} collective-permute-done((bf16[256,2048]{1,0:T(8,128)(2,1)S(1)}, bf16[256,2048]{1,0:T(8,128)(2,1)S(1)}, u32[]{:S(2)}, u32[]{:S(2)}) %collective-permute-start.19) | collective-permute-done | bytes 1048608 | tf_op jit(solution)/shard_map/ppermute | solution.py:491
  317.5 6.2 collective-permute-done.21.nb_ref
  323.6 13.4 %shard_map.223 = (bf16[2048,256]{1,0:T(8,128)(2,1)}, bf16[2048,512]{1,0:T(8,128)(2,1)}) custom-call(bf16[1024,2048]{1,0:T(8,128)(2,1)} %constant_dynamic-update-slice_fusion.12.na_ref, bf16[1024,2048]{1,0:T(8,128)(2,1)} %collective-permute-done.21.nb_ref, bf16[1024,2048]{1,0:T(8,128)(2,1)} %constant_dynamic-update-slice_fusion.6.da_ref, ...), custom_call_target="tpu_custom_call" | custom-call | flops 6442450944 | bytes 26214400 | tf_op jit(solution)/shard_map/pallas_call | solution.py:62
  337.0 13.7 %shard_map.224 = (bf16[2048,768]{1,0:T(8,128)(2,1)}, f32[2048,128]{1,0:T(8,128)}) custom-call(bf16[1024,2048]{1,0:T(8,128)(2,1)} %constant_dynamic-update-slice_fusion.12.na_ref, bf16[1024,2048]{1,0:T(8,128)(2,1)} %collective-permute-done.21.nb_ref, bf16[1024,2048]{1,0:T(8,128)(2,1)} %constant_dynamic-update-slice_fusion.6.da_ref, ...), custom_call_target="tpu_custom_call" | custom-call | flops 6442450944 | bytes 27262976 | tf_op jit(solution)/shard_map/pallas_call | solution.py:62
  350.8 13.4 %shard_map.225 = (bf16[2048,256]{1,0:T(8,128)(2,1)}, bf16[2048,512]{1,0:T(8,128)(2,1)}) custom-call(bf16[1024,2048]{1,0:T(8,128)(2,1)} %constant_dynamic-update-slice_fusion.12.na_ref, bf16[1024,2048]{1,0:T(8,128)(2,1)} %collective-permute-done.21.nb_ref, bf16[1024,2048]{1,0:T(8,128)(2,1)} %constant_dynamic-update-slice_fusion.6.da_ref, ...), custom_call_target="tpu_custom_call" | custom-call | flops 6442450944 | bytes 23068672 | tf_op jit(solution)/shard_map/pallas_call | solution.py:62
  364.2 15.2 %shard_map.226 = (bf16[1024,2048]{1,0:T(8,128)(2,1)}, bf16[1024,2048]{1,0:T(8,128)(2,1)}) custom-call(bf16[2048,512]{1,0:T(8,128)(2,1)} %get-tuple-element.229.back_ref.refs_0_, bf16[2048,512]{1,0:T(8,128)(2,1)} %get-tuple-element.240.refs_1_.back_ref, bf16[2048,768]{1,0:T(8,128)(2,1)} %all-gather.10.cloned.1.call-done.gu_ref.down_ref.refs_2_, ...), custom_call_target="tpu_custom_call" | custom-call | flops 8589934592 | bytes 17825792 | tf_op jit(solution)/shard_map/pallas_call | solution.py:62
  379.6 7.2 %collective-permute-done.22 = bf16[1024,2048]{1,0:T(8,128)(2,1)S(1)} collective-permute-done((bf16[1024,2048]{1,0:T(8,128)(2,1)}, bf16[1024,2048]{1,0:T(8,128)(2,1)S(1)}, u32[]{:S(2)}, u32[]{:S(2)}) %collective-permute-start.22) | collective-permute-done | bytes 4194336 | tf_op jit(solution)/shard_map/ppermute | solution.py:491
  386.8 5.2 add_convert_fusion.2
  394.2 13.8 %shard_map.227 = (bf16[2048,768]{1,0:T(8,128)(2,1)}, f32[2048,128]{1,0:T(8,128)}) custom-call(bf16[1024,2048]{1,0:T(8,128)(2,1)} %constant_dynamic-update-slice_fusion.12.na_ref, bf16[1024,2048]{1,0:T(8,128)(2,1)} %collective-permute-done.21.nb_ref, bf16[1024,2048]{1,0:T(8,128)(2,1)} %constant_dynamic-update-slice_fusion.6.da_ref, ...), custom_call_target="tpu_custom_call" | custom-call | flops 6442450944 | bytes 26214400 | tf_op jit(solution)/shard_map/pallas_call | solution.py:62
  408.0 9.5 %collective-permute-done.23 = bf16[256,2048]{1,0:T(8,128)(2,1)S(1)} collective-permute-done((bf16[256,2048]{1,0:T(8,128)(2,1)}, bf16[256,2048]{1,0:T(8,128)(2,1)S(1)}, u32[]{:S(2)}, u32[]{:S(2)}) %collective-permute-start.23) | collective-permute-done | bytes 1048608 | tf_op jit(solution)/shard_map/ppermute | solution.py:491
  423.1 10.4 %collective-permute-done.25 = bf16[128,2048]{1,0:T(8,128)(2,1)} collective-permute-done((bf16[128,2048]{1,0:T(8,128)(2,1)S(1)}, bf16[128,2048]{1,0:T(8,128)(2,1)}, u32[]{:S(2)}, u32[]{:S(2)}) %collective-permute-start.25) | collective-permute-done | bytes 524320 | tf_op jit(solution)/shard_map/ppermute | solution.py:491
  437.5 3.7 all-to-all-start.4
  441.2 11.4 %shard_map.228 = (bf16[1024,2048]{1,0:T(8,128)(2,1)}, bf16[1024,2048]{1,0:T(8,128)(2,1)}) custom-call(bf16[2048,256]{1,0:T(8,128)(2,1)} %get-tuple-element.249.act_ref.refs_0_, bf16[2048,256]{1,0:T(8,128)(2,1)} %get-tuple-element.239.act_ref.refs_1_, bf16[2048,768]{1,0:T(8,128)(2,1)} %all-gather.10.cloned.1.call-done.gu_ref.down_ref.refs_2_, ...), custom_call_target="tpu_custom_call" | custom-call | flops 4294967296 | bytes 14680064 | tf_op jit(solution)/shard_map/pallas_call | solution.py:62
  452.7 11.3 %collective-permute-done.27 = bf16[128,2048]{1,0:T(8,128)(2,1)} collective-permute-done((bf16[128,2048]{1,0:T(8,128)(2,1)}, bf16[128,2048]{1,0:T(8,128)(2,1)}, u32[]{:S(2)}, u32[]{:S(2)}) %collective-permute-start.27) | collective-permute-done | bytes 524320 | tf_op jit(solution)/shard_map/ppermute | solution.py:515
  471.5 9.4 %collective-permute-done.28 = bf16[64,2048]{1,0:T(8,128)(2,1)S(1)} collective-permute-done((bf16[64,2048]{1,0:T(8,128)(2,1)S(1)}, bf16[64,2048]{1,0:T(8,128)(2,1)S(1)}, u32[]{:S(2)}, u32[]{:S(2)}) %collective-permute-start.28) | collective-permute-done | bytes 262176 | tf_op jit(solution)/shard_map/ppermute | solution.py:491
  485.5 7.7 %collective-permute-done.30 = bf16[128,2048]{1,0:T(8,128)(2,1)S(1)} collective-permute-done((bf16[128,2048]{1,0:T(8,128)(2,1)S(1)}, bf16[128,2048]{1,0:T(8,128)(2,1)S(1)}, u32[]{:S(2)}, u32[]{:S(2)}) %collective-permute-start.30) | collective-permute-done | bytes 524320 | tf_op jit(solution)/shard_map/ppermute | solution.py:491
  494.1 13.5 %reduce-scatter.7.cloned.1.call-done = bf16[1024,768]{1,0:T(8,128)(2,1)} async-done(((bf16[2048,768]{1,0:T(8,128)(2,1)}), bf16[1024,768]{1,0:T(8,128)(2,1)}) %reduce-scatter.7.cloned.1.call-update) | async-done | bytes 1572880 | tf_op jit(solution)/shard_map/reduce_scatter | solution.py:644
  514.3 4.4 all-to-all-start.5
  518.7 5.5 collective-permute-done.32.b_ref.bb
  524.2 5.0 shard_map.229
  529.3 4.4 add_convert_fusion
  536.9 20.7 %shard_map.230 = (bf16[1024,256]{1,0:T(8,128)(2,1)}, bf16[1024,256]{1,0:T(8,128)(2,1)}, bf16[1024,256]{1,0:T(8,128)(2,1)}, bf16[2048,896]{1,0:T(8,128)(2,1)}) custom-call(bf16[512,2048]{1,0:T(8,128)(2,1)} %constant_dynamic-update-slice_fusion.18.a_ref.ba, bf16[512,2048]{1,0:T(8,128)(2,1)} %collective-permute-done.32.b_ref.bb, ...), custom_call_target="tpu_custom_call" | custom-call | flops 4294967296 | bytes 16777216 | tf_op jit(solution)/shard_map/pallas_call | solution.py:432
  557.7 4.9 collective-permute-done.34
  564.5 8.3 %shard_map.231 = (bf16[512,2048]{1,0:T(8,128)(2,1)}, bf16[512,2048]{1,0:T(8,128)(2,1)}) custom-call(bf16[1024,256]{1,0:T(8,128)(2,1)} %get-tuple-element.289.refs_0_, bf16[1024,256]{1,0:T(8,128)(2,1)} %get-tuple-element.290.refs_1_, bf16[1024,256]{1,0:T(8,128)(2,1)} %get-tuple-element.291.refs_2_, ...), custom_call_target="tpu_custom_call" | custom-call | flops 3221225472 | bytes 13107200 | tf_op jit(solution)/shard_map/pallas_call | solution.py:62
  578.4 11.5 %collective-permute-done.37 = bf16[128,2048]{1,0:T(8,128)(2,1)S(1)} collective-permute-done((bf16[128,2048]{1,0:T(8,128)(2,1)S(1)}, bf16[128,2048]{1,0:T(8,128)(2,1)S(1)}, u32[]{:S(2)}, u32[]{:S(2)}) %collective-permute-start.37) | collective-permute-done | bytes 524320 | tf_op jit(solution)/shard_map/ppermute | solution.py:491
  596.2 10.5 %shard_map.233 = (f32[64,8192]{1,0:T(8,128)}, f32[64,8192]{1,0:T(8,128)}, f32[64,8192]{1,0:T(8,128)}) custom-call(bf16[16,64,768]{2,1,0:T(8,128)(2,1)} %copy-done.1, bf16[16,64,768]{2,1,0:T(8,128)(2,1)} %all-to-all-done.5.refs_1_), custom_call_target="tpu_custom_call" | custom-call | bytes 9437184 | tf_op jit(solution)/shard_map/pallas_call | solution.py:62
  619.6 11.4 %reduce-scatter.11.cloned.1.call-done = bf16[512,896]{1,0:T(8,128)(2,1)} async-done(((bf16[2048,896]{1,0:T(8,128)(2,1)}), bf16[512,896]{1,0:T(8,128)(2,1)}) %reduce-scatter.11.cloned.1.call-update) | async-done | bytes 917520 | tf_op jit(solution)/shard_map/reduce_scatter | solution.py:644
  634.6 3.7 all-to-all-start.6
  640.9 3.9 collective-permute-done.39
  647.5 7.6 %all-to-all-done.6.refs_0_ = bf16[8,64,1152]{2,1,0:T(8,128)(2,1)S(1)} async-done(((bf16[8,64,1152]{2,1,0:T(8,128)(2,1)}), bf16[8,64,1152]{2,1,0:T(8,128)(2,1)S(1)}, u32[]{:S(2)}, u32[]{:S(2)}) %all-to-all-start.6) | async-done | bytes 1179680 | tf_op jit(solution)/shard_map/all_to_all | solution.py:638
  656.1 5.4 shard_map.232
  (282 shorter events, 166.6 us)
Async XLA Ops:
  7.2 63.0 %all-gather.8.cloned.1.call-start = ((), (), s32[]{:S(2)}) async-start(), calls=%async_computation.12 | async-start | bytes 1392640 | tf_op jit(solution)/shard_map/all_gather | solution.py:641
  17.9 19.2 %all-to-all-start = ((bf16[8,64,896]{2,1,0:T(8,128)(2,1)}), bf16[8,64,896]{2,1,0:T(8,128)(2,1)S(1)}, u32[]{:S(2)}, u32[]{:S(2)}) async-start(bf16[8,64,896]{2,1,0:T(8,128)(2,1)} %shard_map.220), calls=%async_computation | async-start | bytes 1835008 | tf_op jit(solution)/shard_map/all_to_all | solution.py:638
  23.1 84.5 %all-gather.6.cloned.1.call-start = ((), (), s32[]{:S(2)}) async-start(), calls=%async_computation.11 | async-start | bytes 3932160 | tf_op jit(solution)/shard_map/all_gather | solution.py:641
  38.8 13.8 %collective-permute-start.2 = (bf16[128,2048]{1,0:T(8,128)(2,1)S(1)}, bf16[128,2048]{1,0:T(8,128)(2,1)S(1)}, u32[]{:S(2)}, u32[]{:S(2)}) collective-permute-start(bf16[128,2048]{1,0:T(8,128)(2,1)S(1)} %bitcast.74), channel_id=1, source_target_pairs={{0,8},{8,0},{1,9},{9,1},{2,10},{10,2},{3,11},{11,3},{4,12},{12,4},... | collective-permute-start | bytes 1572872 | tf_op jit(solution)/shard_map/ppermute | solution.py:515
  40.5 12.1 %collective-permute-start = (bf16[64,2048]{1,0:T(8,128)(2,1)S(1)}, bf16[64,2048]{1,0:T(8,128)(2,1)S(1)}, u32[]{:S(2)}, u32[]{:S(2)}) collective-permute-start(bf16[64,2048]{1,0:T(8,128)(2,1)S(1)} %get-tuple-element.170), channel_id=1, source_target_pairs={{0,2},{1,3},{2,0},{3,1},{4,6},{5,7},{6,4},{7,5},{8,10},{9,11},{10,... | collective-permute-start | bytes 786440 | tf_op jit(solution)/shard_map/ppermute | solution.py:491
  41.1 11.6 %collective-permute-start.1 = (bf16[64,2048]{1,0:T(8,128)(2,1)S(1)}, bf16[64,2048]{1,0:T(8,128)(2,1)S(1)}, u32[]{:S(2)}, u32[]{:S(2)}) collective-permute-start(bf16[64,2048]{1,0:T(8,128)(2,1)S(1)} %get-tuple-element.171), channel_id=1, source_target_pairs={{0,4},{1,5},{2,6},{3,7},{4,0},{5,1},{6,2},{7,3},{8,12},{9,13},{10,... | collective-permute-start | bytes 786440 | tf_op jit(solution)/shard_map/ppermute | solution.py:491
  52.8 12.9 %collective-permute-start.3 = (bf16[128,2048]{1,0:T(8,128)(2,1)S(1)}, bf16[128,2048]{1,0:T(8,128)(2,1)S(1)}, u32[]{:S(2)}, u32[]{:S(2)}) collective-permute-start(bf16[128,2048]{1,0:T(8,128)(2,1)S(1)} %get-tuple-element.175), channel_id=1, source_target_pairs={{0,4},{1,5},{2,6},{3,7},{4,0},{5,1},{6,2},{7,3},{8,12},{9,13},{10,... | collective-permute-start | bytes 1572872 | tf_op jit(solution)/shard_map/ppermute | solution.py:491
  54.2 12.9 %collective-permute-start.4 = (bf16[128,2048]{1,0:T(8,128)(2,1)S(1)}, bf16[128,2048]{1,0:T(8,128)(2,1)S(1)}, u32[]{:S(2)}, u32[]{:S(2)}) collective-permute-start(bf16[128,2048]{1,0:T(8,128)(2,1)S(1)} %get-tuple-element.176), channel_id=1, source_target_pairs={{0,2},{1,3},{2,0},{3,1},{4,6},{5,7},{6,4},{7,5},{8,10},{9,11},{10,... | collective-permute-start | bytes 1572872 | tf_op jit(solution)/shard_map/ppermute | solution.py:491
  70.1 31.3 %collective-permute-start.5 = (bf16[512,2048]{1,0:T(8,128)(2,1)}, bf16[512,2048]{1,0:T(8,128)(2,1)}, u32[]{:S(2)}, u32[]{:S(2)}) collective-permute-start(bf16[512,2048]{1,0:T(8,128)(2,1)} %constant_dynamic-update-slice_fusion.xa), channel_id=1, source_target_pairs={{0,1},{1,0},{2,3},{3,2},{4,5},{5,4},{6,7},{7,6},{8,9},{9,8},{10,11... | collective-permute-start | bytes 6291464 | tf_op jit(solution)/shard_map/ppermute | solution.py:491
  74.4 24.7 %all-to-all-start.1 = ((bf16[8,4,64,384]{3,2,1,0:T(8,128)(2,1)}), bf16[8,4,64,384]{3,2,1,0:T(8,128)(2,1)S(1)}, u32[]{:S(2)}, u32[]{:S(2)}) async-start(bf16[8,4,64,384]{3,2,1,0:T(8,128)(2,1)} %copy.35), calls=%async_computation.1 | async-start | bytes 3145728 | tf_op jit(solution)/shard_map/all_to_all | solution.py:638
  107.6 26.6 %all-to-all-start.2 = ((bf16[16,64,768]{2,1,0:T(8,128)(2,1)}), bf16[16,64,768]{2,1,0:T(8,128)(2,1)S(1)}, u32[]{:S(2)}, u32[]{:S(2)}) async-start(bf16[16,64,768]{2,1,0:T(8,128)(2,1)} %get-tuple-element.203), calls=%async_computation.2 | async-start | bytes 3145728 | tf_op jit(solution)/shard_map/all_to_all | solution.py:638
  111.4 102.5 %all-gather.10.cloned.1.call-start = ((), (), s32[]{:S(2)}) async-start(), calls=%async_computation.13 | async-start | bytes 4718592 | tf_op jit(solution)/shard_map/all_gather | solution.py:641
  130.7 16.1 %collective-permute-start.6 = (bf16[512,2176]{1,0:T(8,128)(2,1)}, bf16[512,2176]{1,0:T(8,128)(2,1)}, u32[]{:S(2)}, u32[]{:S(2)}) collective-permute-start(bf16[512,2176]{1,0:T(8,128)(2,1)} %get-tuple-element.192), channel_id=1, source_target_pairs={{0,1},{1,0},{2,3},{3,2},{4,5},{5,4},{6,7},{7,6},{8,9},{9,8},{10,11... | collective-permute-start | bytes 6684680 | tf_op jit(solution)/shard_map/ppermute | solution.py:491
  131.1 14.2 %collective-permute-start.7 = (bf16[128,2048]{1,0:T(8,128)(2,1)S(1)}, bf16[128,2048]{1,0:T(8,128)(2,1)}, u32[]{:S(2)}, u32[]{:S(2)}) collective-permute-start(bf16[128,2048]{1,0:T(8,128)(2,1)S(1)} %bitcast.75), channel_id=1, source_target_pairs={{0,2},{1,3},{2,0},{3,1},{4,6},{5,7},{6,4},{7,5},{8,10},{9,11},{10,... | collective-permute-start | bytes 1572872 | tf_op jit(solution)/shard_map/ppermute | solution.py:491
  132.8 14.0 %collective-permute-start.8 = (bf16[128,2048]{1,0:T(8,128)(2,1)S(1)}, bf16[128,2048]{1,0:T(8,128)(2,1)}, u32[]{:S(2)}, u32[]{:S(2)}) collective-permute-start(bf16[128,2048]{1,0:T(8,128)(2,1)S(1)} %copy-done.19), channel_id=1, source_target_pairs={{0,4},{1,5},{2,6},{3,7},{4,0},{5,1},{6,2},{7,3},{8,12},{9,13},{10,... | collective-permute-start | bytes 1572872 | tf_op jit(solution)/shard_map/ppermute | solution.py:491
  146.8 60.9 %all-to-all-start.3 = ((bf16[16,64,768]{2,1,0:T(8,128)(2,1)}), bf16[16,64,768]{2,1,0:T(8,128)(2,1)S(1)}, u32[]{:S(2)}, u32[]{:S(2)}) async-start(bf16[16,64,768]{2,1,0:T(8,128)(2,1)} %get-tuple-element.204), calls=%async_computation.3 | async-start | bytes 3145728 | tf_op jit(solution)/shard_map/all_to_all | solution.py:638
  150.6 130.9 %all-gather.12.cloned.1.call-start = ((), (), s32[]{:S(2)}) async-start(), calls=%async_computation.14 | async-start | bytes 3145728 | tf_op jit(solution)/shard_map/all_gather | solution.py:641
  154.6 51.3 %collective-permute-start.11 = (bf16[256,2048]{1,0:T(8,128)(2,1)S(1)}, bf16[256,2048]{1,0:T(8,128)(2,1)S(1)}, u32[]{:S(2)}, u32[]{:S(2)}) collective-permute-start(bf16[256,2048]{1,0:T(8,128)(2,1)S(1)} %pad_maximum_fusion.2), channel_id=1, source_target_pairs={{0,4},{1,5},{2,6},{3,7},{4,0},{5,1},{6,2},{7,3},{8,12},{9,13},{10,... | collective-permute-start | bytes 3145736 | tf_op jit(solution)/shard_map/ppermute | solution.py:491
  156.6 51.1 %collective-permute-start.12 = (bf16[256,2048]{1,0:T(8,128)(2,1)S(1)}, bf16[256,2048]{1,0:T(8,128)(2,1)}, u32[]{:S(2)}, u32[]{:S(2)}) collective-permute-start(bf16[256,2048]{1,0:T(8,128)(2,1)S(1)} %pad_maximum_fusion.3), channel_id=1, source_target_pairs={{0,2},{1,3},{2,0},{3,1},{4,6},{5,7},{6,4},{7,5},{8,10},{9,11},{10,... | collective-permute-start | bytes 3145736 | tf_op jit(solution)/shard_map/ppermute | solution.py:491
  158.1 46.9 %collective-permute-start.9 = (bf16[128,2176]{1,0:T(8,128)(2,1)S(1)}, bf16[128,2176]{1,0:T(8,128)(2,1)S(1)}, u32[]{:S(2)}, u32[]{:S(2)}) collective-permute-start(bf16[128,2176]{1,0:T(8,128)(2,1)S(1)} %get-tuple-element.199), channel_id=1, source_target_pairs={{0,4},{1,5},{2,6},{3,7},{4,0},{5,1},{6,2},{7,3},{8,12},{9,13},{10,... | collective-permute-start | bytes 1671176 | tf_op jit(solution)/shard_map/ppermute | solution.py:491
  158.6 47.3 %collective-permute-start.10 = (bf16[128,2176]{1,0:T(8,128)(2,1)S(1)}, bf16[128,2176]{1,0:T(8,128)(2,1)S(1)}, u32[]{:S(2)}, u32[]{:S(2)}) collective-permute-start(bf16[128,2176]{1,0:T(8,128)(2,1)S(1)} %get-tuple-element.200), channel_id=1, source_target_pairs={{0,2},{1,3},{2,0},{3,1},{4,6},{5,7},{6,4},{7,5},{8,10},{9,11},{10,... | collective-permute-start | bytes 1671176 | tf_op jit(solution)/shard_map/ppermute | solution.py:491
  227.6 123.1 %all-gather.14.cloned.1.call-start = ((), (), s32[]{:S(2)}) async-start(), calls=%async_computation.15 | async-start | bytes 1572864 | tf_op jit(solution)/shard_map/all_gather | solution.py:641
  237.2 24.3 %collective-permute-start.16 = (bf16[128,2048]{1,0:T(8,128)(2,1)}, bf16[128,2048]{1,0:T(8,128)(2,1)}, u32[]{:S(2)}, u32[]{:S(2)}) collective-permute-start(bf16[128,2048]{1,0:T(8,128)(2,1)} %get-tuple-element.214), channel_id=1, source_target_pairs={{0,8},{8,0},{1,9},{9,1},{2,10},{10,2},{3,11},{11,3},{4,12},{12,4},... | collective-permute-start | bytes 1572872 | tf_op jit(solution)/shard_map/ppermute | solution.py:515
  261.5 20.0 %collective-permute-start.17 = (bf16[128,2048]{1,0:T(8,128)(2,1)}, bf16[128,2048]{1,0:T(8,128)(2,1)}, u32[]{:S(2)}, u32[]{:S(2)}) collective-permute-start(bf16[128,2048]{1,0:T(8,128)(2,1)} %get-tuple-element.214), channel_id=1, source_target_pairs={{0,2},{1,3},{2,0},{3,1},{4,6},{5,7},{6,4},{7,5},{8,10},{9,11},{10,... | collective-permute-start | bytes 1572872 | tf_op jit(solution)/shard_map/ppermute | solution.py:491
  262.1 19.4 %collective-permute-start.18 = (bf16[128,2048]{1,0:T(8,128)(2,1)}, bf16[128,2048]{1,0:T(8,128)(2,1)}, u32[]{:S(2)}, u32[]{:S(2)}) collective-permute-start(bf16[128,2048]{1,0:T(8,128)(2,1)} %collective-permute-done.16), channel_id=1, source_target_pairs={{0,4},{1,5},{2,6},{3,7},{4,0},{5,1},{6,2},{7,3},{8,12},{9,13},{10,... | collective-permute-start | bytes 1572872 | tf_op jit(solution)/shard_map/ppermute | solution.py:491
  284.0 25.0 %collective-permute-start.19 = (bf16[256,2048]{1,0:T(8,128)(2,1)S(1)}, bf16[256,2048]{1,0:T(8,128)(2,1)S(1)}, u32[]{:S(2)}, u32[]{:S(2)}) collective-permute-start(bf16[256,2048]{1,0:T(8,128)(2,1)S(1)} %pad_maximum_fusion.4), channel_id=1, source_target_pairs={{0,4},{1,5},{2,6},{3,7},{4,0},{5,1},{6,2},{7,3},{8,12},{9,13},{10,... | collective-permute-start | bytes 3145736 | tf_op jit(solution)/shard_map/ppermute | solution.py:491
  285.6 24.6 %collective-permute-start.20 = (bf16[256,2048]{1,0:T(8,128)(2,1)S(1)}, bf16[256,2048]{1,0:T(8,128)(2,1)S(1)}, u32[]{:S(2)}, u32[]{:S(2)}) collective-permute-start(bf16[256,2048]{1,0:T(8,128)(2,1)S(1)} %pad_maximum_fusion.5), channel_id=1, source_target_pairs={{0,2},{1,3},{2,0},{3,1},{4,6},{5,7},{6,4},{7,5},{8,10},{9,11},{10,... | collective-permute-start | bytes 3145736 | tf_op jit(solution)/shard_map/ppermute | solution.py:491
  317.0 117.6 %reduce-scatter.5.cloned.1.call-start = ((), (), s32[]{:S(2)}) async-start(), calls=%async_computation.16 | async-start | bytes 4718592 | tf_op jit(solution)/shard_map/reduce_scatter | solution.py:644
  350.8 156.8 %reduce-scatter.7.cloned.1.call-start = ((), (), s32[]{:S(2)}) async-start(), calls=%async_computation.17 | async-start | bytes 4718592 | tf_op jit(solution)/shard_map/reduce_scatter | solution.py:644
  392.0 25.4 %collective-permute-start.23 = (bf16[256,2048]{1,0:T(8,128)(2,1)}, bf16[256,2048]{1,0:T(8,128)(2,1)S(1)}, u32[]{:S(2)}, u32[]{:S(2)}) collective-permute-start(bf16[256,2048]{1,0:T(8,128)(2,1)} %get-tuple-element.237), channel_id=1, source_target_pairs={{0,4},{1,5},{2,6},{3,7},{4,0},{5,1},{6,2},{7,3},{8,12},{9,13},{10,... | collective-permute-start | bytes 3145736 | tf_op jit(solution)/shard_map/ppermute | solution.py:491
  392.7 25.2 %collective-permute-start.24 = (bf16[256,2048]{1,0:T(8,128)(2,1)}, bf16[256,2048]{1,0:T(8,128)(2,1)}, u32[]{:S(2)}, u32[]{:S(2)}) collective-permute-start(bf16[256,2048]{1,0:T(8,128)(2,1)} %get-tuple-element.238), channel_id=1, source_target_pairs={{0,2},{1,3},{2,0},{3,1},{4,6},{5,7},{6,4},{7,5},{8,10},{9,11},{10,... | collective-permute-start | bytes 3145736 | tf_op jit(solution)/shard_map/ppermute | solution.py:491
  420.2 13.3 %collective-permute-start.25 = (bf16[128,2048]{1,0:T(8,128)(2,1)S(1)}, bf16[128,2048]{1,0:T(8,128)(2,1)}, u32[]{:S(2)}, u32[]{:S(2)}) collective-permute-start(bf16[128,2048]{1,0:T(8,128)(2,1)S(1)} %get-tuple-element.244), channel_id=1, source_target_pairs={{0,2},{1,3},{2,0},{3,1},{4,6},{5,7},{6,4},{7,5},{8,10},{9,11},{10,... | collective-permute-start | bytes 1572872 | tf_op jit(solution)/shard_map/ppermute | solution.py:491
  421.8 12.8 %collective-permute-start.26 = (bf16[128,2048]{1,0:T(8,128)(2,1)S(1)}, bf16[128,2048]{1,0:T(8,128)(2,1)S(1)}, u32[]{:S(2)}, u32[]{:S(2)}) collective-permute-start(bf16[128,2048]{1,0:T(8,128)(2,1)S(1)} %get-tuple-element.245), channel_id=1, source_target_pairs={{0,4},{1,5},{2,6},{3,7},{4,0},{5,1},{6,2},{7,3},{8,12},{9,13},{10,... | collective-permute-start | bytes 1572872 | tf_op jit(solution)/shard_map/ppermute | solution.py:491
  437.5 26.5 %collective-permute-start.27 = (bf16[128,2048]{1,0:T(8,128)(2,1)}, bf16[128,2048]{1,0:T(8,128)(2,1)}, u32[]{:S(2)}, u32[]{:S(2)}) collective-permute-start(bf16[128,2048]{1,0:T(8,128)(2,1)} %add_convert_fusion.12), channel_id=1, source_target_pairs={{0,8},{8,0},{1,9},{9,1},{2,10},{10,2},{3,11},{11,3},{4,12},{12,4},... | collective-permute-start | bytes 1572872 | tf_op jit(solution)/shard_map/ppermute | solution.py:515
  437.5 56.6 %all-to-all-start.4 = ((bf16[16,64,768]{2,1,0:T(8,128)(2,1)}), bf16[16,64,768]{2,1,0:T(8,128)(2,1)S(1)}, u32[]{:S(2)}, u32[]{:S(2)}) async-start(bf16[16,64,768]{2,1,0:T(8,128)(2,1)} %bitcast.81), calls=%async_computation.5 | async-start | bytes 3145728 | tf_op jit(solution)/shard_map/all_to_all | solution.py:638
  482.2 11.9 %collective-permute-start.31 = (bf16[128,2048]{1,0:T(8,128)(2,1)S(1)}, bf16[128,2048]{1,0:T(8,128)(2,1)}, u32[]{:S(2)}, u32[]{:S(2)}) collective-permute-start(bf16[128,2048]{1,0:T(8,128)(2,1)S(1)} %pad_maximum_fusion.11), channel_id=1, source_target_pairs={{0,2},{1,3},{2,0},{3,1},{4,6},{5,7},{6,4},{7,5},{8,10},{9,11},{10,... | collective-permute-start | bytes 1572872 | tf_op jit(solution)/shard_map/ppermute | solution.py:491
  514.3 43.4 %all-to-all-start.5 = ((bf16[16,64,768]{2,1,0:T(8,128)(2,1)}), bf16[16,64,768]{2,1,0:T(8,128)(2,1)}, u32[]{:S(2)}, u32[]{:S(2)}) async-start(bf16[16,64,768]{2,1,0:T(8,128)(2,1)} %bitcast.80), calls=%async_computation.7 | async-start | bytes 3145728 | tf_op jit(solution)/shard_map/all_to_all | solution.py:638
  518.7 44.8 %reduce-scatter.9.cloned.1.call-start = ((), (), s32[]{:S(2)}) async-start(), calls=%async_computation.18 | async-start | bytes 1310720 | tf_op jit(solution)/shard_map/reduce_scatter | solution.py:644
  533.7 97.3 %reduce-scatter.11.cloned.1.call-start = ((), (), s32[]{:S(2)}) async-start(), calls=%async_computation.19 | async-start | bytes 4587520 | tf_op jit(solution)/shard_map/reduce_scatter | solution.py:644
  533.9 28.6 %collective-permute-start.34 = (bf16[256,2048]{1,0:T(8,128)(2,1)}, bf16[256,2048]{1,0:T(8,128)(2,1)}, u32[]{:S(2)}, u32[]{:S(2)}) collective-permute-start(bf16[256,2048]{1,0:T(8,128)(2,1)} %get-tuple-element.285), channel_id=1, source_target_pairs={{0,4},{1,5},{2,6},{3,7},{4,0},{5,1},{6,2},{7,3},{8,12},{9,13},{10,... | collective-permute-start | bytes 3145736 | tf_op jit(solution)/shard_map/ppermute | solution.py:491
  535.4 28.1 %collective-permute-start.35 = (bf16[256,2048]{1,0:T(8,128)(2,1)}, bf16[256,2048]{1,0:T(8,128)(2,1)S(1)}, u32[]{:S(2)}, u32[]{:S(2)}) collective-permute-start(bf16[256,2048]{1,0:T(8,128)(2,1)} %get-tuple-element.286), channel_id=1, source_target_pairs={{0,2},{1,3},{2,0},{3,1},{4,6},{5,7},{6,4},{7,5},{8,10},{9,11},{10,... | collective-permute-start | bytes 3145736 | tf_op jit(solution)/shard_map/ppermute | solution.py:491
  575.5 15.2 %collective-permute-start.36 = (bf16[512,2048]{1,0:T(8,128)(2,1)S(1)}, bf16[512,2048]{1,0:T(8,128)(2,1)S(1)}, u32[]{:S(2)}, u32[]{:S(2)}) collective-permute-start(bf16[512,2048]{1,0:T(8,128)(2,1)S(1)} %copy-done.41), channel_id=1, source_target_pairs={{0,1},{1,0},{2,3},{3,2},{4,5},{5,4},{6,7},{7,6},{8,9},{9,8},{10,11... | collective-permute-start | bytes 6291464 | tf_op jit(solution)/shard_map/ppermute | solution.py:491
  575.5 14.3 %collective-permute-start.37 = (bf16[128,2048]{1,0:T(8,128)(2,1)S(1)}, bf16[128,2048]{1,0:T(8,128)(2,1)S(1)}, u32[]{:S(2)}, u32[]{:S(2)}) collective-permute-start(bf16[128,2048]{1,0:T(8,128)(2,1)S(1)} %get-tuple-element.295), channel_id=1, source_target_pairs={{0,2},{1,3},{2,0},{3,1},{4,6},{5,7},{6,4},{7,5},{8,10},{9,11},{10,... | collective-permute-start | bytes 1572872 | tf_op jit(solution)/shard_map/ppermute | solution.py:491
  575.9 14.8 %collective-permute-start.38 = (bf16[128,2048]{1,0:T(8,128)(2,1)S(1)}, bf16[128,2048]{1,0:T(8,128)(2,1)S(1)}, u32[]{:S(2)}, u32[]{:S(2)}) collective-permute-start(bf16[128,2048]{1,0:T(8,128)(2,1)S(1)} %get-tuple-element.296), channel_id=1, source_target_pairs={{0,4},{1,5},{2,6},{3,7},{4,0},{5,1},{6,2},{7,3},{8,12},{9,13},{10,... | collective-permute-start | bytes 1572872 | tf_op jit(solution)/shard_map/ppermute | solution.py:491
  593.1 13.9 %collective-permute-start.40 = (bf16[128,2048]{1,0:T(8,128)(2,1)}, bf16[128,2048]{1,0:T(8,128)(2,1)}, u32[]{:S(2)}, u32[]{:S(2)}) collective-permute-start(bf16[128,2048]{1,0:T(8,128)(2,1)} %get-tuple-element.303), channel_id=1, source_target_pairs={{0,4},{1,5},{2,6},{3,7},{4,0},{5,1},{6,2},{7,3},{8,12},{9,13},{10,... | collective-permute-start | bytes 1572872 | tf_op jit(solution)/shard_map/ppermute | solution.py:491
  594.9 13.3 %collective-permute-start.41 = (bf16[128,2048]{1,0:T(8,128)(2,1)}, bf16[128,2048]{1,0:T(8,128)(2,1)}, u32[]{:S(2)}, u32[]{:S(2)}) collective-permute-start(bf16[128,2048]{1,0:T(8,128)(2,1)} %get-tuple-element.304), channel_id=1, source_target_pairs={{0,2},{1,3},{2,0},{3,1},{4,6},{5,7},{6,4},{7,5},{8,10},{9,11},{10,... | collective-permute-start | bytes 1572872 | tf_op jit(solution)/shard_map/ppermute | solution.py:491
  631.0 13.8 %collective-permute-start.39 = (bf16[128,2048]{1,0:T(8,128)(2,1)}, bf16[128,2048]{1,0:T(8,128)(2,1)}, u32[]{:S(2)}, u32[]{:S(2)}) collective-permute-start(bf16[128,2048]{1,0:T(8,128)(2,1)} %add_convert_fusion.9), channel_id=1, source_target_pairs={{0,8},{8,0},{1,9},{9,1},{2,10},{10,2},{3,11},{11,3},{4,12},{12,4},... | collective-permute-start | bytes 1572872 | tf_op jit(solution)/shard_map/ppermute | solution.py:515
  634.6 20.5 %all-to-all-start.6 = ((bf16[8,64,1152]{2,1,0:T(8,128)(2,1)}), bf16[8,64,1152]{2,1,0:T(8,128)(2,1)S(1)}, u32[]{:S(2)}, u32[]{:S(2)}) async-start(bf16[8,64,1152]{2,1,0:T(8,128)(2,1)} %bitcast.73), calls=%async_computation.10 | async-start | bytes 2359296 | tf_op jit(solution)/shard_map/all_to_all | solution.py:638
  (54 other events, 474.8 us)
Sparse Core Ops, SparseCore 0:
  10.2 31.8 all-gather.7
  43.6 64.0 all-gather.5
  135.6 78.2 all-gather.9
  227.7 53.7 all-gather.11
  317.1 31.9 all-gather.13
  351.2 76.9 reduce-scatter.4
  430.5 77.0 reduce-scatter.6
  533.8 26.0 reduce-scatter.8
  563.7 67.2 reduce-scatter.10

commit v5 on v4

--- a/solution.py
+++ b/solution.py
@@ -375,7 +375,7 @@
 def rear_kernel(
     steps, ba, bb, wo, q_ref, k_ref, v_ref, cos, sin, col, row, n_ref, wq, wk, wv, g0, g1, *refs
 ):
-    dq, dk, dv, out_ref, grads = refs
+    dq, dk, dv, out_ref, gain_ref, grads = refs
     i = pl.program_id(0)
     tile = ba.shape[0]
     cols = wo.shape[1]
@@ -415,8 +415,7 @@
             out_ref[:, j * cols : (j + 1) * cols] = part.astype(bf16)
             gain = gain + jnp.sum(part * w[...].astype(f32), axis=1, keepdims=True)
         lane = lax.broadcasted_iota(jnp.int32, g0.shape, 1)
-        gains = jnp.where(lane == 0, gain, g0[...] + g1[...])
-        out_ref[:, 3 * cols :] = gains.astype(bf16)
+        gain_ref[...] = jnp.where(lane == 0, gain, g0[...] + g1[...])
 
 
 def rear(pair, queries, keys, values, constants, normed, w_qko, w_v, gain_sums):
@@ -442,8 +441,12 @@
         + [place(0), place(1), place(0)]
         + [pl.BlockSpec((block, LANES), lambda i: (later(i, steps, blocks), 0))] * 2,
         out_specs=[pl.BlockSpec((length, cols), lambda i: (0, 0))] * 3
-        + [pl.BlockSpec((block, 3 * cols + LANES), lambda i: (later(i, steps, blocks), 0))],
-        out_shape=[rows] * 3 + [jax.ShapeDtypeStruct((width, 3 * cols + LANES), bf16)],
+        + [pl.BlockSpec((block, n), lambda i: (later(i, steps, blocks), 0)) for n in (3 * cols, LANES)],
+        out_shape=[rows] * 3
+        + [
+            jax.ShapeDtypeStruct((width, 3 * cols), bf16),
+            jax.ShapeDtypeStruct((width, LANES), f32),
+        ],
         scratch_shapes=[pltpu.VMEM((length, cols), bf16)],
         compiler_params=pltpu.CompilerParams(
             dimension_semantics=("arbitrary",), vmem_limit_bytes=60 * MIB
@@ -577,6 +580,27 @@
     return mine + got.astype(f32)
 
 
+def sum_all(block):
+    bit = 1
+    while bit < lax.axis_size("seq"):
+        (got,) = yield [(block, along(bit))]
+        block = block + got
+        bit *= 2
+    (got,) = yield [(block, swap_side)]
+    block = block + got
+    bit = 1
+    while bit < lax.axis_size("pair"):
+        (got,) = yield [(block, swap_pair(bit))]
+        block = block + got
+        bit *= 2
+    return block
+
+
+def swap_pair(bit):
+    pairs = [(i, i ^ bit) for i in range(lax.axis_size("pair"))]
+    return lambda block: lax.ppermute(block, "pair", pairs)
+
+
 class Ride:
     def __init__(self, steps):
         self.steps = steps
@@ -595,7 +619,7 @@
     waits, then = list(waits), list(then)
     stage = 0
     while main.moves is not None:
-        riding = riders if at is None or stage in at else ()
+        riding = [r for r in riders if at is None or stage in at.get(r, range(8))]
         active = [main] + [rider for rider in riding if rider.moves is not None]
         stage += 1
         got = exchange(
@@ -773,13 +797,13 @@
     out_ride = Ride(scatter_two(made[1]))
     waits = [[], [(ffn_sum, 0), (sums, 1)]]
     left = len(link_bits(ns))
-    branch = run(gather_one(grad_hidden.astype(bf16)), [out_ride], waits, (), (left,))
+    branch = run(gather_one(grad_hidden.astype(bf16)), [out_ride], waits, (), {out_ride: (left,)})
     out_sum = branch_sums(branch, attended)
     moves = out_ride.moves
     branch, out_sum, sent = lax.optimization_barrier((branch, out_sum, [b for b, _ in moves]))
     flying = [f(b) for (_, f), b in zip(moves, sent)]
     out_sum = scatter_z(out_sum)
-    dq, dk, dv, qkv_local = rear(
+    dq, dk, dv, qkv_local, gains = rear(
         branch, queries, keys, values, constants, normed, w_qko, w_v, gain_sums
     )
     ffn_sum.append(home(sums[1], near))
@@ -789,7 +813,9 @@
     out_ride.feed(flying)
     qkv_sum = scatter_z(qkv_local)
     part = enter_back([dq, dk, dv], w_qko, w_v)
-    grad_normed = run(scatter_one(part), [out_ride], at=range(left - 1))
+    gains = jnp.stack([gains[:, i].reshape(-1, LANES) for i in range(2)])
+    gain_ride = Ride(sum_all(lax.optimization_barrier(gains.reshape(-1, LANES))))
+    grad_normed = run(scatter_one(part), [out_ride, gain_ride], at={out_ride: range(left - 1)})
     moves = out_ride.moves
     qkv_sum, sent = lax.optimization_barrier((qkv_sum, [b for b, _ in moves]))
     out_ride.feed([f(b) for (_, f), b in zip(moves, sent)])
@@ -801,18 +827,22 @@
 
     gate_grad, up_grad, down_grad = unpack(ffn_sum, 3)
     attn_sums = home(jnp.concatenate([out_sum, qkv_sum], axis=1))
-    out_grad, query_grad, key_grad, value_grad, gains = unpack([attn_sums], 4, True)
+    out_grad, query_grad, key_grad, value_grad = unpack([attn_sums], 4)
+    while gain_ride.moves is not None:
+        gain_ride.feed(exchange(gain_ride.moves))
+    place = lax.axis_index(batch) * ns + lax.axis_index("seq")
+    gains = lax.dynamic_slice_in_dim(gain_ride.result.reshape(2, width), place * rows, rows, 1)
     out_grad, down_grad = out_grad.T, down_grad.T
     return (
         layer_out[None],
         input_grad[None],
         attn_mass[None],
-        gains[:, 0] / low_gains[0].astype(f32),
+        gains[0] / low_gains[0].astype(f32),
         query_grad,
         key_grad,
         value_grad,
         out_grad,
-        gains[:, 1] / low_gains[1].astype(f32),
+        gains[1] / low_gains[1].astype(f32),
         gate_grad,
         up_grad,
         down_grad,

time: 679 us -> 667 us (0.982)
  waiting for transfers between devices: 303 us -> 290 us
    reduce_scatter x4, waiting for transfers between devices: 24.8 us -> 14.5 us  [scatter_z(): return lax.psum_scatter(full, axes, scatter_dimension=0, tiled=True)]
    unnamed x103 -> x93, local copies, waits for them, and re-layouts: 30.5 us -> 27.2 us
    ppermute x40 -> x43, starting transfers between devices: 39.4 us -> 42 us  [swap_bit(): return lax.ppermute(block, 'seq', [(i, i ^ bit) for i in range(size)])]
    ppermute x40 -> x43, waiting for transfers between devices: 175 us -> 173 us  [swap_bit(): return lax.ppermute(block, 'seq', [(i, i ^ bit) for i in range(size)])]
    ppermute x4 -> x5, waiting for transfers between devices: 39.5 us -> 39.2 us  [swap_side(): return lax.ppermute(block, 'side', [(0, 1), (1, 0)])]
  transfers between devices with their start and end apart: 60 -> 65, of which waited for: 40 -> 41; matrix products, arithmetic and copies ran while one was open for 12% -> 12% of each run, Pallas kernels for 24% -> 24%
where the time goes in v5:
time: 667 us; the launch traced here: 659 us
  waiting for transfers between devices  290 us (43%)
  Pallas kernels  165 us (25%)
  starting transfers between devices  76.8 us (12%)
  other arithmetic  65.7 us (10%)
  local copies, waits for them, and re-layouts  47.4 us (7%)
  between operations  14.7 us (2%)
    ppermute x43, waiting for transfers between devices, swap_bit(): return lax.ppermute(block, 'seq', [(i, i ^ bit) for i in range(size)])  173 us
    pallas_call x12, Pallas kernels, call(): pl.pallas_call(kernel, grid_spec=pltpu.PrefetchScalarGridSpec(num_scalar_...  126 us
    ppermute x43, starting transfers between devices, swap_bit(): return lax.ppermute(block, 'seq', [(i, i ^ bit) for i in range(size)])  42 us
    ppermute x5, waiting for transfers between devices, swap_side(): return lax.ppermute(block, 'side', [(0, 1), (1, 0)])  39.2 us
    all_to_all x7, waiting for transfers between devices, swap(): return lax.all_to_all(blocks, axes, split_axis=0, concat_axis=0, tiled=True)  32.7 us
    all_gather x5, waiting for transfers between devices, gather_z(): return lax.all_gather(block, axes, axis=0, tiled=True)  30.3 us
    all_to_all x7, starting transfers between devices, swap(): return lax.all_to_all(blocks, axes, split_axis=0, concat_axis=0, tiled=True)  28.8 us
    unnamed x93, local copies, waits for them, and re-layouts  27.2 us
  transfers between devices with their start and end apart: 65, of which 41 were waited for; matrix products, arithmetic and copies ran while one was open for 12% of the time, Pallas kernels for 24%

profile of v5, /device:TPU:0, one launch (start us, length us, event | category | flops | bytes accessed | tf_op | source)
XLA Modules:
  0.0 658.8 jit_solution(9473588780059241745)
XLA Ops:
  12.9 5.0 shard_map.220
  17.9 5.2 all-to-all-start
  25.9 11.2 %all-to-all-done = bf16[8,64,896]{2,1,0:T(8,128)(2,1)S(1)} async-done(((bf16[8,64,896]{2,1,0:T(8,128)(2,1)}), bf16[8,64,896]{2,1,0:T(8,128)(2,1)S(1)}, u32[]{:S(2)}, u32[]{:S(2)}) %all-to-all-start) | async-done | bytes 917536 | tf_op jit(solution)/shard_map/all_to_all | solution.py:662
  42.4 10.3 %shard_map.221 = (bf16[16,64,768]{2,1,0:T(8,128)(2,1)}, bf16[16,64,768]{2,1,0:T(8,128)(2,1)}) custom-call(f32[64,8192]{1,0:T(8,128)} %refs_0_.3, f32[64,8192]{1,0:T(8,128)} %refs_1_.3, bf16[64,8192]{1,0:T(8,128)(2,1)} %convert_bitcast_fusion.refs_2_), custom_call_target="tpu_custom_call" | custom-call | bytes 8388608 | tf_op jit(solution)/shard_map/pallas_call | solution.py:62
  57.5 8.2 %collective-permute-done.3 = bf16[128,2048]{1,0:T(8,128)(2,1)S(1)} collective-permute-done((bf16[128,2048]{1,0:T(8,128)(2,1)S(1)}, bf16[128,2048]{1,0:T(8,128)(2,1)S(1)}, u32[]{:S(2)}, u32[]{:S(2)}) %collective-permute-start.3) | collective-permute-done | bytes 524320 | tf_op jit(solution)/shard_map/ppermute | solution.py:494
  74.4 3.7 all-to-all-start.1
  84.3 14.8 %all-to-all-done.1 = bf16[8,4,64,384]{3,2,1,0:T(8,128)(2,1)S(1)} async-done(((bf16[8,4,64,384]{3,2,1,0:T(8,128)(2,1)}), bf16[8,4,64,384]{3,2,1,0:T(8,128)(2,1)S(1)}, u32[]{:S(2)}, u32[]{:S(2)}) %all-to-all-start.1) | async-done | bytes 1572896 | tf_op jit(solution)/shard_map/all_to_all | solution.py:662
  101.4 6.2 all-gather.6.cloned.1.call-done.wq.wk.wo.refs_3_.refs_4_
  107.6 3.8 all-to-all-start.2
  112.7 18.0 %shard_map.222 = (bf16[1024,2048]{1,0:T(8,128)(2,1)}, bf16[1024,256]{1,0:T(8,128)(2,1)}, bf16[1024,256]{1,0:T(8,128)(2,1)}, bf16[1024,256]{1,0:T(8,128)(2,1)}, b...) custom-call(bf16[512,2048]{1,0:T(8,128)(2,1)} %constant_dynamic-update-slice_fusion.xa, ...), custom_call_target="tpu_custom_call" | custom-call | flops 4294967296 | bytes 25165824 | tf_op jit(solution)/shard_map/pallas_call | solution.py:211
  135.5 9.9 %collective-permute-done.7 = bf16[128,2048]{1,0:T(8,128)(2,1)} collective-permute-done((bf16[128,2048]{1,0:T(8,128)(2,1)S(1)}, bf16[128,2048]{1,0:T(8,128)(2,1)}, u32[]{:S(2)}, u32[]{:S(2)}) %collective-permute-start.7) | collective-permute-done | bytes 524320 | tf_op jit(solution)/shard_map/ppermute | solution.py:494
  146.9 3.7 all-to-all-start.3
  161.5 43.5 %collective-permute-done.9 = bf16[128,2176]{1,0:T(8,128)(2,1)S(1)} collective-permute-done((bf16[128,2176]{1,0:T(8,128)(2,1)S(1)}, bf16[128,2176]{1,0:T(8,128)(2,1)S(1)}, u32[]{:S(2)}, u32[]{:S(2)}) %collective-permute-start.9) | collective-permute-done | bytes 557088 | tf_op jit(solution)/shard_map/ppermute | solution.py:494
  207.8 6.1 all-gather.10.cloned.1.call-done.gu_ref.down_ref.refs_2_
  227.6 5.2 collective-permute-done.13
  237.2 24.3 %collective-permute-done.16 = bf16[128,2048]{1,0:T(8,128)(2,1)} collective-permute-done((bf16[128,2048]{1,0:T(8,128)(2,1)}, bf16[128,2048]{1,0:T(8,128)(2,1)}, u32[]{:S(2)}, u32[]{:S(2)}) %collective-permute-start.16) | collective-permute-done | bytes 524320 | tf_op jit(solution)/shard_map/ppermute | solution.py:518
  263.5 18.0 %all-gather.12.cloned.1.call-done.gu_ref.refs_3_ = bf16[2048,512]{1,0:T(8,128)(2,1)} async-done(((bf16[1024,512]{1,0:T(8,128)(2,1)}), bf16[2048,512]{1,0:T(8,128)(2,1)}) %all-gather.12.cloned.1.call-update) | async-done | bytes 2097168 | tf_op jit(solution)/shard_map/all_gather | solution.py:665
  288.9 20.0 %collective-permute-done.19 = bf16[256,2048]{1,0:T(8,128)(2,1)S(1)} collective-permute-done((bf16[256,2048]{1,0:T(8,128)(2,1)S(1)}, bf16[256,2048]{1,0:T(8,128)(2,1)S(1)}, u32[]{:S(2)}, u32[]{:S(2)}) %collective-permute-start.19) | collective-permute-done | bytes 1048608 | tf_op jit(solution)/shard_map/ppermute | solution.py:494
  317.5 6.1 collective-permute-done.21.nb_ref
  323.7 13.4 %shard_map.223 = (bf16[2048,256]{1,0:T(8,128)(2,1)}, bf16[2048,512]{1,0:T(8,128)(2,1)}) custom-call(bf16[1024,2048]{1,0:T(8,128)(2,1)} %constant_dynamic-update-slice_fusion.12.na_ref, bf16[1024,2048]{1,0:T(8,128)(2,1)} %collective-permute-done.21.nb_ref, bf16[1024,2048]{1,0:T(8,128)(2,1)} %constant_dynamic-update-slice_fusion.6.da_ref, ...), custom_call_target="tpu_custom_call" | custom-call | flops 6442450944 | bytes 26214400 | tf_op jit(solution)/shard_map/pallas_call | solution.py:62
  337.0 13.8 %shard_map.224 = (bf16[2048,768]{1,0:T(8,128)(2,1)}, f32[2048,128]{1,0:T(8,128)}) custom-call(bf16[1024,2048]{1,0:T(8,128)(2,1)} %constant_dynamic-update-slice_fusion.12.na_ref, bf16[1024,2048]{1,0:T(8,128)(2,1)} %collective-permute-done.21.nb_ref, bf16[1024,2048]{1,0:T(8,128)(2,1)} %constant_dynamic-update-slice_fusion.6.da_ref, ...), custom_call_target="tpu_custom_call" | custom-call | flops 6442450944 | bytes 27262976 | tf_op jit(solution)/shard_map/pallas_call | solution.py:62
  350.9 13.4 %shard_map.225 = (bf16[2048,256]{1,0:T(8,128)(2,1)}, bf16[2048,512]{1,0:T(8,128)(2,1)}) custom-call(bf16[1024,2048]{1,0:T(8,128)(2,1)} %constant_dynamic-update-slice_fusion.12.na_ref, bf16[1024,2048]{1,0:T(8,128)(2,1)} %collective-permute-done.21.nb_ref, bf16[1024,2048]{1,0:T(8,128)(2,1)} %constant_dynamic-update-slice_fusion.6.da_ref, ...), custom_call_target="tpu_custom_call" | custom-call | flops 6442450944 | bytes 23068672 | tf_op jit(solution)/shard_map/pallas_call | solution.py:62
  364.3 15.2 %shard_map.226 = (bf16[1024,2048]{1,0:T(8,128)(2,1)}, bf16[1024,2048]{1,0:T(8,128)(2,1)}) custom-call(bf16[2048,512]{1,0:T(8,128)(2,1)} %get-tuple-element.235.back_ref.refs_0_, bf16[2048,512]{1,0:T(8,128)(2,1)} %get-tuple-element.246.refs_1_.back_ref, bf16[2048,768]{1,0:T(8,128)(2,1)} %all-gather.10.cloned.1.call-done.gu_ref.down_ref.refs_2_, ...), custom_call_target="tpu_custom_call" | custom-call | flops 8589934592 | bytes 17825792 | tf_op jit(solution)/shard_map/pallas_call | solution.py:62
  379.7 7.2 %collective-permute-done.22 = bf16[1024,2048]{1,0:T(8,128)(2,1)S(1)} collective-permute-done((bf16[1024,2048]{1,0:T(8,128)(2,1)}, bf16[1024,2048]{1,0:T(8,128)(2,1)S(1)}, u32[]{:S(2)}, u32[]{:S(2)}) %collective-permute-start.22) | collective-permute-done | bytes 4194336 | tf_op jit(solution)/shard_map/ppermute | solution.py:494
  386.9 5.2 add_convert_fusion.2
  394.3 13.8 %shard_map.227 = (bf16[2048,768]{1,0:T(8,128)(2,1)}, f32[2048,128]{1,0:T(8,128)}) custom-call(bf16[1024,2048]{1,0:T(8,128)(2,1)} %constant_dynamic-update-slice_fusion.12.na_ref, bf16[1024,2048]{1,0:T(8,128)(2,1)} %collective-permute-done.21.nb_ref, bf16[1024,2048]{1,0:T(8,128)(2,1)} %constant_dynamic-update-slice_fusion.6.da_ref, ...), custom_call_target="tpu_custom_call" | custom-call | flops 6442450944 | bytes 26214400 | tf_op jit(solution)/shard_map/pallas_call | solution.py:62
  408.1 9.4 %collective-permute-done.23 = bf16[256,2048]{1,0:T(8,128)(2,1)S(1)} collective-permute-done((bf16[256,2048]{1,0:T(8,128)(2,1)}, bf16[256,2048]{1,0:T(8,128)(2,1)S(1)}, u32[]{:S(2)}, u32[]{:S(2)}) %collective-permute-start.23) | collective-permute-done | bytes 1048608 | tf_op jit(solution)/shard_map/ppermute | solution.py:494
  423.2 10.4 %collective-permute-done.25 = bf16[128,2048]{1,0:T(8,128)(2,1)} collective-permute-done((bf16[128,2048]{1,0:T(8,128)(2,1)S(1)}, bf16[128,2048]{1,0:T(8,128)(2,1)}, u32[]{:S(2)}, u32[]{:S(2)}) %collective-permute-start.25) | collective-permute-done | bytes 524320 | tf_op jit(solution)/shard_map/ppermute | solution.py:494
  434.7 2.9 add_convert_fusion.12
  437.6 3.7 all-to-all-start.4
  441.3 11.4 %shard_map.228 = (bf16[1024,2048]{1,0:T(8,128)(2,1)}, bf16[1024,2048]{1,0:T(8,128)(2,1)}) custom-call(bf16[2048,256]{1,0:T(8,128)(2,1)} %get-tuple-element.255.act_ref.refs_0_, bf16[2048,256]{1,0:T(8,128)(2,1)} %get-tuple-element.245.act_ref.refs_1_, bf16[2048,768]{1,0:T(8,128)(2,1)} %all-gather.10.cloned.1.call-done.gu_ref.down_ref.refs_2_, ...), custom_call_target="tpu_custom_call" | custom-call | flops 4294967296 | bytes 14680064 | tf_op jit(solution)/shard_map/pallas_call | solution.py:62
  452.8 11.3 %collective-permute-done.27 = bf16[128,2048]{1,0:T(8,128)(2,1)} collective-permute-done((bf16[128,2048]{1,0:T(8,128)(2,1)}, bf16[128,2048]{1,0:T(8,128)(2,1)}, u32[]{:S(2)}, u32[]{:S(2)}) %collective-permute-start.27) | collective-permute-done | bytes 524320 | tf_op jit(solution)/shard_map/ppermute | solution.py:518
  466.3 3.2 fusion.22
  471.5 9.5 %collective-permute-done.28 = bf16[64,2048]{1,0:T(8,128)(2,1)S(1)} collective-permute-done((bf16[64,2048]{1,0:T(8,128)(2,1)S(1)}, bf16[64,2048]{1,0:T(8,128)(2,1)S(1)}, u32[]{:S(2)}, u32[]{:S(2)}) %collective-permute-start.28) | collective-permute-done | bytes 262176 | tf_op jit(solution)/shard_map/ppermute | solution.py:494
  485.5 7.8 %collective-permute-done.30 = bf16[128,2048]{1,0:T(8,128)(2,1)S(1)} collective-permute-done((bf16[128,2048]{1,0:T(8,128)(2,1)S(1)}, bf16[128,2048]{1,0:T(8,128)(2,1)S(1)}, u32[]{:S(2)}, u32[]{:S(2)}) %collective-permute-start.30) | collective-permute-done | bytes 524320 | tf_op jit(solution)/shard_map/ppermute | solution.py:494
  494.2 13.4 %reduce-scatter.7.cloned.1.call-done = bf16[1024,768]{1,0:T(8,128)(2,1)} async-done(((bf16[2048,768]{1,0:T(8,128)(2,1)}), bf16[1024,768]{1,0:T(8,128)(2,1)}) %reduce-scatter.7.cloned.1.call-update) | async-done | bytes 1572880 | tf_op jit(solution)/shard_map/reduce_scatter | solution.py:668
  514.3 4.4 all-to-all-start.5
  518.7 5.5 collective-permute-done.32.b_ref.bb
  524.3 5.0 shard_map.229
  529.3 4.4 add_convert_fusion
  536.8 21.0 %shard_map.230 = (bf16[1024,256]{1,0:T(8,128)(2,1)}, bf16[1024,256]{1,0:T(8,128)(2,1)}, bf16[1024,256]{1,0:T(8,128)(2,1)}, bf16[2048,768]{1,0:T(8,128)(2,1)}, f32[2048,128]{1,0:T(8,128)}) custom-call(bf16[512,2048]{1,0:T(8,128)(2,1)} %constant_dynamic-update-slice_fusion.18.a_ref.ba, bf16[512,2048]{1,0:T(8,128)(2,1)} %collective-permute-done.32.b_ref.bb, ...), custom_call_target="tpu_custom_call" | custom-call | flops 4294967296 | bytes 16777216 | tf_op jit(solution)/shard_map/pallas_call | solution.py:431
  557.8 4.8 collective-permute-done.34
  564.6 8.4 %shard_map.231 = (bf16[512,2048]{1,0:T(8,128)(2,1)}, bf16[512,2048]{1,0:T(8,128)(2,1)}) custom-call(bf16[1024,256]{1,0:T(8,128)(2,1)} %get-tuple-element.295.refs_0_, bf16[1024,256]{1,0:T(8,128)(2,1)} %get-tuple-element.296.refs_1_, bf16[1024,256]{1,0:T(8,128)(2,1)} %get-tuple-element.297.refs_2_, ...), custom_call_target="tpu_custom_call" | custom-call | flops 3221225472 | bytes 13107200 | tf_op jit(solution)/shard_map/pallas_call | solution.py:62
  579.8 10.2 %collective-permute-done.37 = bf16[128,2048]{1,0:T(8,128)(2,1)S(1)} collective-permute-done((bf16[128,2048]{1,0:T(8,128)(2,1)S(1)}, bf16[128,2048]{1,0:T(8,128)(2,1)S(1)}, u32[]{:S(2)}, u32[]{:S(2)}) %collective-permute-start.37) | collective-permute-done | bytes 524320 | tf_op jit(solution)/shard_map/ppermute | solution.py:494
  596.6 10.5 %shard_map.233 = (f32[64,8192]{1,0:T(8,128)}, f32[64,8192]{1,0:T(8,128)}, f32[64,8192]{1,0:T(8,128)}) custom-call(bf16[16,64,768]{2,1,0:T(8,128)(2,1)} %copy-done.1, bf16[16,64,768]{2,1,0:T(8,128)(2,1)} %all-to-all-done.5.refs_1_), custom_call_target="tpu_custom_call" | custom-call | bytes 9437184 | tf_op jit(solution)/shard_map/pallas_call | solution.py:62
  626.9 4.3 all-to-all-start.6
  640.0 6.6 %all-to-all-done.6.refs_0_ = bf16[8,64,1024]{2,1,0:T(8,128)(2,1)} async-done(((bf16[8,64,1024]{2,1,0:T(8,128)(2,1)}), bf16[8,64,1024]{2,1,0:T(8,128)(2,1)}, u32[]{:S(2)}, u32[]{:S(2)}) %all-to-all-start.6) | async-done | bytes 1048608 | tf_op jit(solution)/shard_map/all_to_all | solution.py:662
  646.6 5.4 shard_map.232
  (289 shorter events, 165.4 us)
Async XLA Ops:
  7.2 63.0 %all-gather.8.cloned.1.call-start = ((), (), s32[]{:S(2)}) async-start(), calls=%async_computation.12 | async-start | bytes 1392640 | tf_op jit(solution)/shard_map/all_gather | solution.py:665
  17.9 19.2 %all-to-all-start = ((bf16[8,64,896]{2,1,0:T(8,128)(2,1)}), bf16[8,64,896]{2,1,0:T(8,128)(2,1)S(1)}, u32[]{:S(2)}, u32[]{:S(2)}) async-start(bf16[8,64,896]{2,1,0:T(8,128)(2,1)} %shard_map.220), calls=%async_computation | async-start | bytes 1835008 | tf_op jit(solution)/shard_map/all_to_all | solution.py:662
  23.1 84.5 %all-gather.6.cloned.1.call-start = ((), (), s32[]{:S(2)}) async-start(), calls=%async_computation.11 | async-start | bytes 3932160 | tf_op jit(solution)/shard_map/all_gather | solution.py:665
  38.8 13.8 %collective-permute-start.2 = (bf16[128,2048]{1,0:T(8,128)(2,1)S(1)}, bf16[128,2048]{1,0:T(8,128)(2,1)S(1)}, u32[]{:S(2)}, u32[]{:S(2)}) collective-permute-start(bf16[128,2048]{1,0:T(8,128)(2,1)S(1)} %bitcast.80), channel_id=1, source_target_pairs={{0,8},{8,0},{1,9},{9,1},{2,10},{10,2},{3,11},{11,3},{4,12},{12,4},... | collective-permute-start | bytes 1572872 | tf_op jit(solution)/shard_map/ppermute | solution.py:518
  40.5 12.2 %collective-permute-start = (bf16[64,2048]{1,0:T(8,128)(2,1)S(1)}, bf16[64,2048]{1,0:T(8,128)(2,1)S(1)}, u32[]{:S(2)}, u32[]{:S(2)}) collective-permute-start(bf16[64,2048]{1,0:T(8,128)(2,1)S(1)} %get-tuple-element.176), channel_id=1, source_target_pairs={{0,2},{1,3},{2,0},{3,1},{4,6},{5,7},{6,4},{7,5},{8,10},{9,11},{10,... | collective-permute-start | bytes 786440 | tf_op jit(solution)/shard_map/ppermute | solution.py:494
  52.8 12.9 %collective-permute-start.3 = (bf16[128,2048]{1,0:T(8,128)(2,1)S(1)}, bf16[128,2048]{1,0:T(8,128)(2,1)S(1)}, u32[]{:S(2)}, u32[]{:S(2)}) collective-permute-start(bf16[128,2048]{1,0:T(8,128)(2,1)S(1)} %get-tuple-element.181), channel_id=1, source_target_pairs={{0,4},{1,5},{2,6},{3,7},{4,0},{5,1},{6,2},{7,3},{8,12},{9,13},{10,... | collective-permute-start | bytes 1572872 | tf_op jit(solution)/shard_map/ppermute | solution.py:494
  54.2 12.8 %collective-permute-start.4 = (bf16[128,2048]{1,0:T(8,128)(2,1)S(1)}, bf16[128,2048]{1,0:T(8,128)(2,1)S(1)}, u32[]{:S(2)}, u32[]{:S(2)}) collective-permute-start(bf16[128,2048]{1,0:T(8,128)(2,1)S(1)} %get-tuple-element.182), channel_id=1, source_target_pairs={{0,2},{1,3},{2,0},{3,1},{4,6},{5,7},{6,4},{7,5},{8,10},{9,11},{10,... | collective-permute-start | bytes 1572872 | tf_op jit(solution)/shard_map/ppermute | solution.py:494
  70.1 31.3 %collective-permute-start.5 = (bf16[512,2048]{1,0:T(8,128)(2,1)}, bf16[512,2048]{1,0:T(8,128)(2,1)}, u32[]{:S(2)}, u32[]{:S(2)}) collective-permute-start(bf16[512,2048]{1,0:T(8,128)(2,1)} %constant_dynamic-update-slice_fusion.xa), channel_id=1, source_target_pairs={{0,1},{1,0},{2,3},{3,2},{4,5},{5,4},{6,7},{7,6},{8,9},{9,8},{10,11... | collective-permute-start | bytes 6291464 | tf_op jit(solution)/shard_map/ppermute | solution.py:494
  74.4 24.7 %all-to-all-start.1 = ((bf16[8,4,64,384]{3,2,1,0:T(8,128)(2,1)}), bf16[8,4,64,384]{3,2,1,0:T(8,128)(2,1)S(1)}, u32[]{:S(2)}, u32[]{:S(2)}) async-start(bf16[8,4,64,384]{3,2,1,0:T(8,128)(2,1)} %copy.35), calls=%async_computation.1 | async-start | bytes 3145728 | tf_op jit(solution)/shard_map/all_to_all | solution.py:662
  107.6 26.7 %all-to-all-start.2 = ((bf16[16,64,768]{2,1,0:T(8,128)(2,1)}), bf16[16,64,768]{2,1,0:T(8,128)(2,1)S(1)}, u32[]{:S(2)}, u32[]{:S(2)}) async-start(bf16[16,64,768]{2,1,0:T(8,128)(2,1)} %get-tuple-element.209), calls=%async_computation.2 | async-start | bytes 3145728 | tf_op jit(solution)/shard_map/all_to_all | solution.py:662
  111.4 102.5 %all-gather.10.cloned.1.call-start = ((), (), s32[]{:S(2)}) async-start(), calls=%async_computation.13 | async-start | bytes 4718592 | tf_op jit(solution)/shard_map/all_gather | solution.py:665
  130.7 16.2 %collective-permute-start.6 = (bf16[512,2176]{1,0:T(8,128)(2,1)}, bf16[512,2176]{1,0:T(8,128)(2,1)}, u32[]{:S(2)}, u32[]{:S(2)}) collective-permute-start(bf16[512,2176]{1,0:T(8,128)(2,1)} %get-tuple-element.198), channel_id=1, source_target_pairs={{0,1},{1,0},{2,3},{3,2},{4,5},{5,4},{6,7},{7,6},{8,9},{9,8},{10,11... | collective-permute-start | bytes 6684680 | tf_op jit(solution)/shard_map/ppermute | solution.py:494
  131.2 14.2 %collective-permute-start.7 = (bf16[128,2048]{1,0:T(8,128)(2,1)S(1)}, bf16[128,2048]{1,0:T(8,128)(2,1)}, u32[]{:S(2)}, u32[]{:S(2)}) collective-permute-start(bf16[128,2048]{1,0:T(8,128)(2,1)S(1)} %bitcast.81), channel_id=1, source_target_pairs={{0,2},{1,3},{2,0},{3,1},{4,6},{5,7},{6,4},{7,5},{8,10},{9,11},{10,... | collective-permute-start | bytes 1572872 | tf_op jit(solution)/shard_map/ppermute | solution.py:494
  132.9 14.0 %collective-permute-start.8 = (bf16[128,2048]{1,0:T(8,128)(2,1)S(1)}, bf16[128,2048]{1,0:T(8,128)(2,1)}, u32[]{:S(2)}, u32[]{:S(2)}) collective-permute-start(bf16[128,2048]{1,0:T(8,128)(2,1)S(1)} %copy-done.18), channel_id=1, source_target_pairs={{0,4},{1,5},{2,6},{3,7},{4,0},{5,1},{6,2},{7,3},{8,12},{9,13},{10,... | collective-permute-start | bytes 1572872 | tf_op jit(solution)/shard_map/ppermute | solution.py:494
  146.9 60.9 %all-to-all-start.3 = ((bf16[16,64,768]{2,1,0:T(8,128)(2,1)}), bf16[16,64,768]{2,1,0:T(8,128)(2,1)S(1)}, u32[]{:S(2)}, u32[]{:S(2)}) async-start(bf16[16,64,768]{2,1,0:T(8,128)(2,1)} %get-tuple-element.210), calls=%async_computation.3 | async-start | bytes 3145728 | tf_op jit(solution)/shard_map/all_to_all | solution.py:662
  150.6 130.9 %all-gather.12.cloned.1.call-start = ((), (), s32[]{:S(2)}) async-start(), calls=%async_computation.14 | async-start | bytes 3145728 | tf_op jit(solution)/shard_map/all_gather | solution.py:665
  154.6 51.3 %collective-permute-start.11 = (bf16[256,2048]{1,0:T(8,128)(2,1)S(1)}, bf16[256,2048]{1,0:T(8,128)(2,1)S(1)}, u32[]{:S(2)}, u32[]{:S(2)}) collective-permute-start(bf16[256,2048]{1,0:T(8,128)(2,1)S(1)} %pad_maximum_fusion.1), channel_id=1, source_target_pairs={{0,4},{1,5},{2,6},{3,7},{4,0},{5,1},{6,2},{7,3},{8,12},{9,13},{10,... | collective-permute-start | bytes 3145736 | tf_op jit(solution)/shard_map/ppermute | solution.py:494
  156.6 51.1 %collective-permute-start.12 = (bf16[256,2048]{1,0:T(8,128)(2,1)S(1)}, bf16[256,2048]{1,0:T(8,128)(2,1)}, u32[]{:S(2)}, u32[]{:S(2)}) collective-permute-start(bf16[256,2048]{1,0:T(8,128)(2,1)S(1)} %pad_maximum_fusion.2), channel_id=1, source_target_pairs={{0,2},{1,3},{2,0},{3,1},{4,6},{5,7},{6,4},{7,5},{8,10},{9,11},{10,... | collective-permute-start | bytes 3145736 | tf_op jit(solution)/shard_map/ppermute | solution.py:494
  158.1 46.9 %collective-permute-start.9 = (bf16[128,2176]{1,0:T(8,128)(2,1)S(1)}, bf16[128,2176]{1,0:T(8,128)(2,1)S(1)}, u32[]{:S(2)}, u32[]{:S(2)}) collective-permute-start(bf16[128,2176]{1,0:T(8,128)(2,1)S(1)} %get-tuple-element.205), channel_id=1, source_target_pairs={{0,4},{1,5},{2,6},{3,7},{4,0},{5,1},{6,2},{7,3},{8,12},{9,13},{10,... | collective-permute-start | bytes 1671176 | tf_op jit(solution)/shard_map/ppermute | solution.py:494
  158.7 47.3 %collective-permute-start.10 = (bf16[128,2176]{1,0:T(8,128)(2,1)S(1)}, bf16[128,2176]{1,0:T(8,128)(2,1)S(1)}, u32[]{:S(2)}, u32[]{:S(2)}) collective-permute-start(bf16[128,2176]{1,0:T(8,128)(2,1)S(1)} %get-tuple-element.206), channel_id=1, source_target_pairs={{0,2},{1,3},{2,0},{3,1},{4,6},{5,7},{6,4},{7,5},{8,10},{9,11},{10,... | collective-permute-start | bytes 1671176 | tf_op jit(solution)/shard_map/ppermute | solution.py:494
  227.6 123.2 %all-gather.14.cloned.1.call-start = ((), (), s32[]{:S(2)}) async-start(), calls=%async_computation.15 | async-start | bytes 1572864 | tf_op jit(solution)/shard_map/all_gather | solution.py:665
  237.2 24.3 %collective-permute-start.16 = (bf16[128,2048]{1,0:T(8,128)(2,1)}, bf16[128,2048]{1,0:T(8,128)(2,1)}, u32[]{:S(2)}, u32[]{:S(2)}) collective-permute-start(bf16[128,2048]{1,0:T(8,128)(2,1)} %get-tuple-element.220), channel_id=1, source_target_pairs={{0,8},{8,0},{1,9},{9,1},{2,10},{10,2},{3,11},{11,3},{4,12},{12,4},... | collective-permute-start | bytes 1572872 | tf_op jit(solution)/shard_map/ppermute | solution.py:518
  261.5 20.0 %collective-permute-start.17 = (bf16[128,2048]{1,0:T(8,128)(2,1)}, bf16[128,2048]{1,0:T(8,128)(2,1)}, u32[]{:S(2)}, u32[]{:S(2)}) collective-permute-start(bf16[128,2048]{1,0:T(8,128)(2,1)} %get-tuple-element.220), channel_id=1, source_target_pairs={{0,2},{1,3},{2,0},{3,1},{4,6},{5,7},{6,4},{7,5},{8,10},{9,11},{10,... | collective-permute-start | bytes 1572872 | tf_op jit(solution)/shard_map/ppermute | solution.py:494
  262.1 19.4 %collective-permute-start.18 = (bf16[128,2048]{1,0:T(8,128)(2,1)}, bf16[128,2048]{1,0:T(8,128)(2,1)}, u32[]{:S(2)}, u32[]{:S(2)}) collective-permute-start(bf16[128,2048]{1,0:T(8,128)(2,1)} %collective-permute-done.16), channel_id=1, source_target_pairs={{0,4},{1,5},{2,6},{3,7},{4,0},{5,1},{6,2},{7,3},{8,12},{9,13},{10,... | collective-permute-start | bytes 1572872 | tf_op jit(solution)/shard_map/ppermute | solution.py:494
  284.0 25.0 %collective-permute-start.19 = (bf16[256,2048]{1,0:T(8,128)(2,1)S(1)}, bf16[256,2048]{1,0:T(8,128)(2,1)S(1)}, u32[]{:S(2)}, u32[]{:S(2)}) collective-permute-start(bf16[256,2048]{1,0:T(8,128)(2,1)S(1)} %pad_maximum_fusion.3), channel_id=1, source_target_pairs={{0,4},{1,5},{2,6},{3,7},{4,0},{5,1},{6,2},{7,3},{8,12},{9,13},{10,... | collective-permute-start | bytes 3145736 | tf_op jit(solution)/shard_map/ppermute | solution.py:494
  285.6 24.6 %collective-permute-start.20 = (bf16[256,2048]{1,0:T(8,128)(2,1)S(1)}, bf16[256,2048]{1,0:T(8,128)(2,1)S(1)}, u32[]{:S(2)}, u32[]{:S(2)}) collective-permute-start(bf16[256,2048]{1,0:T(8,128)(2,1)S(1)} %pad_maximum_fusion.4), channel_id=1, source_target_pairs={{0,2},{1,3},{2,0},{3,1},{4,6},{5,7},{6,4},{7,5},{8,10},{9,11},{10,... | collective-permute-start | bytes 3145736 | tf_op jit(solution)/shard_map/ppermute | solution.py:494
  317.0 117.7 %reduce-scatter.5.cloned.1.call-start = ((), (), s32[]{:S(2)}) async-start(), calls=%async_computation.16 | async-start | bytes 4718592 | tf_op jit(solution)/shard_map/reduce_scatter | solution.py:668
  350.8 156.7 %reduce-scatter.7.cloned.1.call-start = ((), (), s32[]{:S(2)}) async-start(), calls=%async_computation.17 | async-start | bytes 4718592 | tf_op jit(solution)/shard_map/reduce_scatter | solution.py:668
  392.1 25.5 %collective-permute-start.23 = (bf16[256,2048]{1,0:T(8,128)(2,1)}, bf16[256,2048]{1,0:T(8,128)(2,1)S(1)}, u32[]{:S(2)}, u32[]{:S(2)}) collective-permute-start(bf16[256,2048]{1,0:T(8,128)(2,1)} %get-tuple-element.243), channel_id=1, source_target_pairs={{0,4},{1,5},{2,6},{3,7},{4,0},{5,1},{6,2},{7,3},{8,12},{9,13},{10,... | collective-permute-start | bytes 3145736 | tf_op jit(solution)/shard_map/ppermute | solution.py:494
  392.8 25.2 %collective-permute-start.24 = (bf16[256,2048]{1,0:T(8,128)(2,1)}, bf16[256,2048]{1,0:T(8,128)(2,1)}, u32[]{:S(2)}, u32[]{:S(2)}) collective-permute-start(bf16[256,2048]{1,0:T(8,128)(2,1)} %get-tuple-element.244), channel_id=1, source_target_pairs={{0,2},{1,3},{2,0},{3,1},{4,6},{5,7},{6,4},{7,5},{8,10},{9,11},{10,... | collective-permute-start | bytes 3145736 | tf_op jit(solution)/shard_map/ppermute | solution.py:494
  420.3 13.3 %collective-permute-start.25 = (bf16[128,2048]{1,0:T(8,128)(2,1)S(1)}, bf16[128,2048]{1,0:T(8,128)(2,1)}, u32[]{:S(2)}, u32[]{:S(2)}) collective-permute-start(bf16[128,2048]{1,0:T(8,128)(2,1)S(1)} %get-tuple-element.250), channel_id=1, source_target_pairs={{0,2},{1,3},{2,0},{3,1},{4,6},{5,7},{6,4},{7,5},{8,10},{9,11},{10,... | collective-permute-start | bytes 1572872 | tf_op jit(solution)/shard_map/ppermute | solution.py:494
  421.8 12.8 %collective-permute-start.26 = (bf16[128,2048]{1,0:T(8,128)(2,1)S(1)}, bf16[128,2048]{1,0:T(8,128)(2,1)S(1)}, u32[]{:S(2)}, u32[]{:S(2)}) collective-permute-start(bf16[128,2048]{1,0:T(8,128)(2,1)S(1)} %get-tuple-element.251), channel_id=1, source_target_pairs={{0,4},{1,5},{2,6},{3,7},{4,0},{5,1},{6,2},{7,3},{8,12},{9,13},{10,... | collective-permute-start | bytes 1572872 | tf_op jit(solution)/shard_map/ppermute | solution.py:494
  437.6 26.5 %collective-permute-start.27 = (bf16[128,2048]{1,0:T(8,128)(2,1)}, bf16[128,2048]{1,0:T(8,128)(2,1)}, u32[]{:S(2)}, u32[]{:S(2)}) collective-permute-start(bf16[128,2048]{1,0:T(8,128)(2,1)} %add_convert_fusion.12), channel_id=1, source_target_pairs={{0,8},{8,0},{1,9},{9,1},{2,10},{10,2},{3,11},{11,3},{4,12},{12,4},... | collective-permute-start | bytes 1572872 | tf_op jit(solution)/shard_map/ppermute | solution.py:518
  437.6 56.6 %all-to-all-start.4 = ((bf16[16,64,768]{2,1,0:T(8,128)(2,1)}), bf16[16,64,768]{2,1,0:T(8,128)(2,1)S(1)}, u32[]{:S(2)}, u32[]{:S(2)}) async-start(bf16[16,64,768]{2,1,0:T(8,128)(2,1)} %bitcast.88), calls=%async_computation.5 | async-start | bytes 3145728 | tf_op jit(solution)/shard_map/all_to_all | solution.py:662
  514.3 43.5 %all-to-all-start.5 = ((bf16[16,64,768]{2,1,0:T(8,128)(2,1)}), bf16[16,64,768]{2,1,0:T(8,128)(2,1)}, u32[]{:S(2)}, u32[]{:S(2)}) async-start(bf16[16,64,768]{2,1,0:T(8,128)(2,1)} %bitcast.87), calls=%async_computation.7 | async-start | bytes 3145728 | tf_op jit(solution)/shard_map/all_to_all | solution.py:662
  518.7 44.9 %reduce-scatter.9.cloned.1.call-start = ((), (), s32[]{:S(2)}) async-start(), calls=%async_computation.18 | async-start | bytes 1310720 | tf_op jit(solution)/shard_map/reduce_scatter | solution.py:668
  533.7 89.6 %reduce-scatter.11.cloned.1.call-start = ((), (), s32[]{:S(2)}) async-start(), calls=%async_computation.19 | async-start | bytes 3932160 | tf_op jit(solution)/shard_map/reduce_scatter | solution.py:668
  533.8 28.8 %collective-permute-start.34 = (bf16[256,2048]{1,0:T(8,128)(2,1)}, bf16[256,2048]{1,0:T(8,128)(2,1)}, u32[]{:S(2)}, u32[]{:S(2)}) collective-permute-start(bf16[256,2048]{1,0:T(8,128)(2,1)} %get-tuple-element.291), channel_id=1, source_target_pairs={{0,4},{1,5},{2,6},{3,7},{4,0},{5,1},{6,2},{7,3},{8,12},{9,13},{10,... | collective-permute-start | bytes 3145736 | tf_op jit(solution)/shard_map/ppermute | solution.py:494
  535.3 28.3 %collective-permute-start.35 = (bf16[256,2048]{1,0:T(8,128)(2,1)}, bf16[256,2048]{1,0:T(8,128)(2,1)}, u32[]{:S(2)}, u32[]{:S(2)}) collective-permute-start(bf16[256,2048]{1,0:T(8,128)(2,1)} %get-tuple-element.292), channel_id=1, source_target_pairs={{0,2},{1,3},{2,0},{3,1},{4,6},{5,7},{6,4},{7,5},{8,10},{9,11},{10,... | collective-permute-start | bytes 3145736 | tf_op jit(solution)/shard_map/ppermute | solution.py:494
  575.5 15.2 %collective-permute-start.36 = (bf16[512,2048]{1,0:T(8,128)(2,1)S(1)}, bf16[512,2048]{1,0:T(8,128)(2,1)S(1)}, u32[]{:S(2)}, u32[]{:S(2)}) collective-permute-start(bf16[512,2048]{1,0:T(8,128)(2,1)S(1)} %copy-done.36), channel_id=1, source_target_pairs={{0,1},{1,0},{2,3},{3,2},{4,5},{5,4},{6,7},{7,6},{8,9},{9,8},{10,11... | collective-permute-start | bytes 6291464 | tf_op jit(solution)/shard_map/ppermute | solution.py:494
  575.6 14.3 %collective-permute-start.37 = (bf16[128,2048]{1,0:T(8,128)(2,1)S(1)}, bf16[128,2048]{1,0:T(8,128)(2,1)S(1)}, u32[]{:S(2)}, u32[]{:S(2)}) collective-permute-start(bf16[128,2048]{1,0:T(8,128)(2,1)S(1)} %get-tuple-element.302), channel_id=1, source_target_pairs={{0,2},{1,3},{2,0},{3,1},{4,6},{5,7},{6,4},{7,5},{8,10},{9,11},{10,... | collective-permute-start | bytes 1572872 | tf_op jit(solution)/shard_map/ppermute | solution.py:494
  575.8 14.8 %collective-permute-start.38 = (bf16[128,2048]{1,0:T(8,128)(2,1)S(1)}, bf16[128,2048]{1,0:T(8,128)(2,1)S(1)}, u32[]{:S(2)}, u32[]{:S(2)}) collective-permute-start(bf16[128,2048]{1,0:T(8,128)(2,1)S(1)} %get-tuple-element.303), channel_id=1, source_target_pairs={{0,4},{1,5},{2,6},{3,7},{4,0},{5,1},{6,2},{7,3},{8,12},{9,13},{10,... | collective-permute-start | bytes 1572872 | tf_op jit(solution)/shard_map/ppermute | solution.py:494
  592.4 15.3 %collective-permute-start.41 = (bf16[128,2048]{1,0:T(8,128)(2,1)}, bf16[128,2048]{1,0:T(8,128)(2,1)}, u32[]{:S(2)}, u32[]{:S(2)}) collective-permute-start(bf16[128,2048]{1,0:T(8,128)(2,1)} %get-tuple-element.312), channel_id=1, source_target_pairs={{0,4},{1,5},{2,6},{3,7},{4,0},{5,1},{6,2},{7,3},{8,12},{9,13},{10,... | collective-permute-start | bytes 1572872 | tf_op jit(solution)/shard_map/ppermute | solution.py:494
  593.9 13.8 %collective-permute-start.42 = (bf16[128,2048]{1,0:T(8,128)(2,1)}, bf16[128,2048]{1,0:T(8,128)(2,1)}, u32[]{:S(2)}, u32[]{:S(2)}) collective-permute-start(bf16[128,2048]{1,0:T(8,128)(2,1)} %get-tuple-element.313), channel_id=1, source_target_pairs={{0,2},{1,3},{2,0},{3,1},{4,6},{5,7},{6,4},{7,5},{8,10},{9,11},{10,... | collective-permute-start | bytes 1572872 | tf_op jit(solution)/shard_map/ppermute | solution.py:494
  595.0 12.7 %collective-permute-start.43 = (f32[32,128]{1,0:T(8,128)S(1)}, f32[32,128]{1,0:T(8,128)S(1)}, u32[]{:S(2)}, u32[]{:S(2)}) collective-permute-start(f32[32,128]{1,0:T(8,128)S(1)} %add.282), channel_id=1, source_target_pairs={{0,2},{1,3},{2,0},{3,1},{4,6},{5,7},{6,4},{7,5},{8,10},{9,11},{10,... | collective-permute-start | bytes 49160 | tf_op jit(solution)/shard_map/ppermute | solution.py:494
  621.7 11.9 %collective-permute-start.48 = (f32[32,128]{1,0:T(8,128)S(1)}, f32[32,128]{1,0:T(8,128)S(1)}, u32[]{:S(2)}, u32[]{:S(2)}) collective-permute-start(f32[32,128]{1,0:T(8,128)S(1)} %add.295), channel_id=1, source_target_pairs={{0,16},{16,0},{1,17},{17,1},{2,18},{18,2},{3,19},{19,3},{4,20},{20... | collective-permute-start | bytes 49160 | tf_op jit(solution)/shard_map/ppermute | solution.py:601
  623.3 13.8 %collective-permute-start.40 = (bf16[128,2048]{1,0:T(8,128)(2,1)S(1)}, bf16[128,2048]{1,0:T(8,128)(2,1)}, u32[]{:S(2)}, u32[]{:S(2)}) collective-permute-start(bf16[128,2048]{1,0:T(8,128)(2,1)S(1)} %copy-done.25), channel_id=1, source_target_pairs={{0,8},{8,0},{1,9},{9,1},{2,10},{10,2},{3,11},{11,3},{4,12},{12,4},... | collective-permute-start | bytes 1572872 | tf_op jit(solution)/shard_map/ppermute | solution.py:518
  626.9 19.7 %all-to-all-start.6 = ((bf16[8,64,1024]{2,1,0:T(8,128)(2,1)}), bf16[8,64,1024]{2,1,0:T(8,128)(2,1)}, u32[]{:S(2)}, u32[]{:S(2)}) async-start(bf16[8,64,1024]{2,1,0:T(8,128)(2,1)} %bitcast.83), calls=%async_computation.10 | async-start | bytes 2097152 | tf_op jit(solution)/shard_map/all_to_all | solution.py:662
  (54 other events, 449.1 us)
Sparse Core Ops, SparseCore 0:
  10.2 31.8 all-gather.7
  43.6 64.0 all-gather.5
  135.6 78.2 all-gather.9
  227.7 53.7 all-gather.11
  317.1 31.9 all-gather.13
  351.2 76.9 reduce-scatter.4
  430.5 77.0 reduce-scatter.6
  533.8 26.0 reduce-scatter.8
  563.8 59.4 reduce-scatter.10

commit v6 on v5

--- a/solution.py
+++ b/solution.py
@@ -332,19 +332,26 @@
     store_half(total.astype(bf16), outs)
 
 
-def enter_back(lefts, w_qko, w_v):
+def enter_back_kernel(*refs):
+    lefts, rights, out = refs[:3], refs[3:6], refs[6]
+    total = sum(dot_t(left[...], right[...]) for left, right in zip(lefts, rights))
+    out[...] = total.astype(bf16)
+
+
+def enter_back(lefts, w_qko, w_v, side):
     length, cols = lefts[0].shape
     width = w_v.shape[0]
-    tile, steps, outs, specs = halves(length, width)
+    tile = min(TILE, length // 2)
+    steps = length // 2 // tile
     return call(
-        functools.partial(back_kernel, 3),
+        enter_back_kernel,
         steps,
         (*lefts, w_qko, w_qko, w_v),
-        [rows_of(tile, cols)] * 3
+        [pl.BlockSpec((tile, cols), lambda i: (i + side * steps, 0))] * 3
         + [columns(w_qko, 0, cols), columns(w_qko, 1, cols), whole(w_v.shape)],
-        outs,
-        specs,
-        6 * length * width * cols,
+        [jax.ShapeDtypeStruct((length // 2, width), bf16)],
+        [rows_of(tile, width)],
+        3 * length * width * cols,
     )
 
 
@@ -462,30 +469,27 @@
 def unpack_kernel(count, parts, *refs):
     ins, outs = refs[:count], refs[count:]
     cols = outs[0].shape[1] // count
+    each = ins[0].shape[0]
+    cols = cols // each
     for c, ref in enumerate(ins):
-        for i in range(parts):
-            outs[i][:, c * cols : (c + 1) * cols] = ref[0, :, i * cols : (i + 1) * cols].astype(f32)
-    for i, out in enumerate(outs[parts:]):
-        step = pl.program_id(0)
-        part = ref[0, :, parts * cols :].astype(f32)
-        out[...] = jnp.where(step == 0, part, out[...] + part)
-
-
-def unpack(blocks, parts, extra=False):
+        for s in range(each):
+            for i in range(parts):
+                value = ref[s, :, i * cols : (i + 1) * cols].astype(f32)
+                to = (s * count + c) * cols
+                outs[i][:, to : to + cols] = value
+
+
+def unpack(blocks, parts):
     ns, rows, cols = blocks[0].shape
-    cols = (cols - LANES * extra) // parts
-    outs = [jax.ShapeDtypeStruct((rows, ns * len(blocks) * cols), f32)] * parts
-    specs = [pl.BlockSpec((rows, len(blocks) * cols), lambda i: (0, i))] * parts
-    if extra:
-        outs = outs + [jax.ShapeDtypeStruct((rows, LANES), f32)]
-        specs = specs + [pl.BlockSpec((rows, LANES), lambda i: (0, 0))]
+    cols = cols // parts
+    each = 4 if ns % 4 == 0 else 1
     return call(
         functools.partial(unpack_kernel, len(blocks), parts),
-        ns,
+        ns // each,
         tuple(blocks),
-        [pl.BlockSpec((1,) + a.shape[1:], lambda i: (i, 0, 0)) for a in blocks],
-        outs,
-        specs,
+        [pl.BlockSpec((each,) + a.shape[1:], lambda i: (i, 0, 0)) for a in blocks],
+        [jax.ShapeDtypeStruct((rows, ns * len(blocks) * cols), f32)] * parts,
+        [pl.BlockSpec((rows, each * len(blocks) * cols), lambda i: (0, i))] * parts,
         0,
     )
 
@@ -812,7 +816,8 @@
     )
     out_ride.feed(flying)
     qkv_sum = scatter_z(qkv_local)
-    part = enter_back([dq, dk, dv], w_qko, w_v)
+    away = enter_back([dq, dk, dv], w_qko, w_v, 1)
+    part = (enter_back([dq, dk, dv], w_qko, w_v, 0), away)
     gains = jnp.stack([gains[:, i].reshape(-1, LANES) for i in range(2)])
     gain_ride = Ride(sum_all(lax.optimization_barrier(gains.reshape(-1, LANES))))
     grad_normed = run(scatter_one(part), [out_ride, gain_ride], at={out_ride: range(left - 1)})

time: 667 us -> 664 us (level)
  Pallas kernels: 165 us -> 158 us
    pallas_call x12 -> x13, Pallas kernels: 126 us -> 119 us  [call(): pl.pallas_call(kernel, grid_spec=pltpu.PrefetchScalarGridSpec(num_scalar_...]
    unnamed x93 -> x91, local copies, waits for them, and re-layouts: 27.2 us -> 29 us
  transfers between devices with their start and end apart: 65 -> 65, of which waited for: 41 -> 40; matrix products, arithmetic and copies ran while one was open for 12% -> 13% of each run, Pallas kernels for 24% -> 24%
where the time goes in v6:
time: 664 us; the launch traced here: 656 us
  waiting for transfers between devices  289 us (44%)
  Pallas kernels  158 us (24%)
  starting transfers between devices  76.6 us (12%)
  other arithmetic  68.1 us (10%)
  local copies, waits for them, and re-layouts  49.3 us (7%)
  between operations  14.7 us (2%)
    ppermute x43, waiting for transfers between devices, swap_bit(): return lax.ppermute(block, 'seq', [(i, i ^ bit) for i in range(size)])  172 us
    pallas_call x13, Pallas kernels, call(): pl.pallas_call(kernel, grid_spec=pltpu.PrefetchScalarGridSpec(num_scalar_...  119 us
    ppermute x43, starting transfers between devices, swap_bit(): return lax.ppermute(block, 'seq', [(i, i ^ bit) for i in range(size)])  42 us
    ppermute x5, waiting for transfers between devices, swap_side(): return lax.ppermute(block, 'side', [(0, 1), (1, 0)])  39.7 us
    all_to_all x7, waiting for transfers between devices, swap(): return lax.all_to_all(blocks, axes, split_axis=0, concat_axis=0, tiled=True)  32.8 us
    all_gather x5, waiting for transfers between devices, gather_z(): return lax.all_gather(block, axes, axis=0, tiled=True)  30.4 us
    unnamed x91, local copies, waits for them, and re-layouts  29 us
    all_to_all x7, starting transfers between devices, swap(): return lax.all_to_all(blocks, axes, split_axis=0, concat_axis=0, tiled=True)  28.7 us
  transfers between devices with their start and end apart: 65, of which 40 were waited for; matrix products, arithmetic and copies ran while one was open for 13% of the time, Pallas kernels for 24%

profile of v6, /device:TPU:0, one launch (start us, length us, event | category | flops | bytes accessed | tf_op | source)
XLA Modules:
  0.0 655.6 jit_solution(9891284048605621654)
XLA Ops:
  12.9 5.0 shard_map.220
  17.9 5.2 all-to-all-start
  25.9 11.2 %all-to-all-done = bf16[8,64,896]{2,1,0:T(8,128)(2,1)S(1)} async-done(((bf16[8,64,896]{2,1,0:T(8,128)(2,1)}), bf16[8,64,896]{2,1,0:T(8,128)(2,1)S(1)}, u32[]{:S(2)}, u32[]{:S(2)}) %all-to-all-start) | async-done | bytes 917536 | tf_op jit(solution)/shard_map/all_to_all | solution.py:666
  42.4 10.3 %shard_map.221 = (bf16[16,64,768]{2,1,0:T(8,128)(2,1)}, bf16[16,64,768]{2,1,0:T(8,128)(2,1)}) custom-call(f32[64,8192]{1,0:T(8,128)} %refs_0_.3, f32[64,8192]{1,0:T(8,128)} %refs_1_.3, bf16[64,8192]{1,0:T(8,128)(2,1)} %convert_bitcast_fusion.refs_2_), custom_call_target="tpu_custom_call" | custom-call | bytes 8388608 | tf_op jit(solution)/shard_map/pallas_call | solution.py:62
  57.5 8.2 %collective-permute-done.3 = bf16[128,2048]{1,0:T(8,128)(2,1)S(1)} collective-permute-done((bf16[128,2048]{1,0:T(8,128)(2,1)S(1)}, bf16[128,2048]{1,0:T(8,128)(2,1)S(1)}, u32[]{:S(2)}, u32[]{:S(2)}) %collective-permute-start.3) | collective-permute-done | bytes 524320 | tf_op jit(solution)/shard_map/ppermute | solution.py:498
  74.4 3.7 all-to-all-start.1
  84.3 14.8 %all-to-all-done.1 = bf16[8,4,64,384]{3,2,1,0:T(8,128)(2,1)S(1)} async-done(((bf16[8,4,64,384]{3,2,1,0:T(8,128)(2,1)}), bf16[8,4,64,384]{3,2,1,0:T(8,128)(2,1)S(1)}, u32[]{:S(2)}, u32[]{:S(2)}) %all-to-all-start.1) | async-done | bytes 1572896 | tf_op jit(solution)/shard_map/all_to_all | solution.py:666
  101.4 6.2 all-gather.6.cloned.1.call-done.wq.wk.wo.refs_3_.refs_4_
  107.6 3.8 all-to-all-start.2
  112.7 18.0 %shard_map.222 = (bf16[1024,2048]{1,0:T(8,128)(2,1)}, bf16[1024,256]{1,0:T(8,128)(2,1)}, bf16[1024,256]{1,0:T(8,128)(2,1)}, bf16[1024,256]{1,0:T(8,128)(2,1)}, b...) custom-call(bf16[512,2048]{1,0:T(8,128)(2,1)} %constant_dynamic-update-slice_fusion.xa, ...), custom_call_target="tpu_custom_call" | custom-call | flops 4294967296 | bytes 25165824 | tf_op jit(solution)/shard_map/pallas_call | solution.py:211
  135.5 9.9 %collective-permute-done.7 = bf16[128,2048]{1,0:T(8,128)(2,1)} collective-permute-done((bf16[128,2048]{1,0:T(8,128)(2,1)S(1)}, bf16[128,2048]{1,0:T(8,128)(2,1)}, u32[]{:S(2)}, u32[]{:S(2)}) %collective-permute-start.7) | collective-permute-done | bytes 524320 | tf_op jit(solution)/shard_map/ppermute | solution.py:498
  146.9 3.7 all-to-all-start.3
  161.6 43.4 %collective-permute-done.9 = bf16[128,2176]{1,0:T(8,128)(2,1)S(1)} collective-permute-done((bf16[128,2176]{1,0:T(8,128)(2,1)S(1)}, bf16[128,2176]{1,0:T(8,128)(2,1)S(1)}, u32[]{:S(2)}, u32[]{:S(2)}) %collective-permute-start.9) | collective-permute-done | bytes 557088 | tf_op jit(solution)/shard_map/ppermute | solution.py:498
  207.8 6.1 all-gather.10.cloned.1.call-done.gu_ref.down_ref.refs_2_
  227.6 5.2 collective-permute-done.13
  237.1 24.3 %collective-permute-done.16 = bf16[128,2048]{1,0:T(8,128)(2,1)} collective-permute-done((bf16[128,2048]{1,0:T(8,128)(2,1)}, bf16[128,2048]{1,0:T(8,128)(2,1)}, u32[]{:S(2)}, u32[]{:S(2)}) %collective-permute-start.16) | collective-permute-done | bytes 524320 | tf_op jit(solution)/shard_map/ppermute | solution.py:522
  263.4 18.0 %all-gather.12.cloned.1.call-done.gu_ref.refs_3_ = bf16[2048,512]{1,0:T(8,128)(2,1)} async-done(((bf16[1024,512]{1,0:T(8,128)(2,1)}), bf16[2048,512]{1,0:T(8,128)(2,1)}) %all-gather.12.cloned.1.call-update) | async-done | bytes 2097168 | tf_op jit(solution)/shard_map/all_gather | solution.py:669
  288.9 20.1 %collective-permute-done.19 = bf16[256,2048]{1,0:T(8,128)(2,1)S(1)} collective-permute-done((bf16[256,2048]{1,0:T(8,128)(2,1)S(1)}, bf16[256,2048]{1,0:T(8,128)(2,1)S(1)}, u32[]{:S(2)}, u32[]{:S(2)}) %collective-permute-start.19) | collective-permute-done | bytes 1048608 | tf_op jit(solution)/shard_map/ppermute | solution.py:498
  317.5 6.1 collective-permute-done.21.nb_ref
  323.6 13.4 %shard_map.223 = (bf16[2048,256]{1,0:T(8,128)(2,1)}, bf16[2048,512]{1,0:T(8,128)(2,1)}) custom-call(bf16[1024,2048]{1,0:T(8,128)(2,1)} %constant_dynamic-update-slice_fusion.12.na_ref, bf16[1024,2048]{1,0:T(8,128)(2,1)} %collective-permute-done.21.nb_ref, bf16[1024,2048]{1,0:T(8,128)(2,1)} %constant_dynamic-update-slice_fusion.6.da_ref, ...), custom_call_target="tpu_custom_call" | custom-call | flops 6442450944 | bytes 26214400 | tf_op jit(solution)/shard_map/pallas_call | solution.py:62
  337.0 13.7 %shard_map.224 = (bf16[2048,768]{1,0:T(8,128)(2,1)}, f32[2048,128]{1,0:T(8,128)}) custom-call(bf16[1024,2048]{1,0:T(8,128)(2,1)} %constant_dynamic-update-slice_fusion.12.na_ref, bf16[1024,2048]{1,0:T(8,128)(2,1)} %collective-permute-done.21.nb_ref, bf16[1024,2048]{1,0:T(8,128)(2,1)} %constant_dynamic-update-slice_fusion.6.da_ref, ...), custom_call_target="tpu_custom_call" | custom-call | flops 6442450944 | bytes 27262976 | tf_op jit(solution)/shard_map/pallas_call | solution.py:62
  350.8 13.4 %shard_map.225 = (bf16[2048,256]{1,0:T(8,128)(2,1)}, bf16[2048,512]{1,0:T(8,128)(2,1)}) custom-call(bf16[1024,2048]{1,0:T(8,128)(2,1)} %constant_dynamic-update-slice_fusion.12.na_ref, bf16[1024,2048]{1,0:T(8,128)(2,1)} %collective-permute-done.21.nb_ref, bf16[1024,2048]{1,0:T(8,128)(2,1)} %constant_dynamic-update-slice_fusion.6.da_ref, ...), custom_call_target="tpu_custom_call" | custom-call | flops 6442450944 | bytes 23068672 | tf_op jit(solution)/shard_map/pallas_call | solution.py:62
  364.2 15.2 %shard_map.226 = (bf16[1024,2048]{1,0:T(8,128)(2,1)}, bf16[1024,2048]{1,0:T(8,128)(2,1)}) custom-call(bf16[2048,512]{1,0:T(8,128)(2,1)} %get-tuple-element.233.back_ref.refs_0_, bf16[2048,512]{1,0:T(8,128)(2,1)} %get-tuple-element.244.refs_1_.back_ref, bf16[2048,768]{1,0:T(8,128)(2,1)} %all-gather.10.cloned.1.call-done.gu_ref.down_ref.refs_2_, ...), custom_call_target="tpu_custom_call" | custom-call | flops 8589934592 | bytes 17825792 | tf_op jit(solution)/shard_map/pallas_call | solution.py:62
  379.6 7.2 %collective-permute-done.22 = bf16[1024,2048]{1,0:T(8,128)(2,1)S(1)} collective-permute-done((bf16[1024,2048]{1,0:T(8,128)(2,1)}, bf16[1024,2048]{1,0:T(8,128)(2,1)S(1)}, u32[]{:S(2)}, u32[]{:S(2)}) %collective-permute-start.22) | collective-permute-done | bytes 4194336 | tf_op jit(solution)/shard_map/ppermute | solution.py:498
  386.8 5.2 add_convert_fusion.2
  394.2 13.8 %shard_map.227 = (bf16[2048,768]{1,0:T(8,128)(2,1)}, f32[2048,128]{1,0:T(8,128)}) custom-call(bf16[1024,2048]{1,0:T(8,128)(2,1)} %constant_dynamic-update-slice_fusion.12.na_ref, bf16[1024,2048]{1,0:T(8,128)(2,1)} %collective-permute-done.21.nb_ref, bf16[1024,2048]{1,0:T(8,128)(2,1)} %constant_dynamic-update-slice_fusion.6.da_ref, ...), custom_call_target="tpu_custom_call" | custom-call | flops 6442450944 | bytes 26214400 | tf_op jit(solution)/shard_map/pallas_call | solution.py:62
  408.0 9.4 %collective-permute-done.23 = bf16[256,2048]{1,0:T(8,128)(2,1)S(1)} collective-permute-done((bf16[256,2048]{1,0:T(8,128)(2,1)}, bf16[256,2048]{1,0:T(8,128)(2,1)S(1)}, u32[]{:S(2)}, u32[]{:S(2)}) %collective-permute-start.23) | collective-permute-done | bytes 1048608 | tf_op jit(solution)/shard_map/ppermute | solution.py:498
  423.1 10.4 %collective-permute-done.25 = bf16[128,2048]{1,0:T(8,128)(2,1)} collective-permute-done((bf16[128,2048]{1,0:T(8,128)(2,1)S(1)}, bf16[128,2048]{1,0:T(8,128)(2,1)}, u32[]{:S(2)}, u32[]{:S(2)}) %collective-permute-start.25) | collective-permute-done | bytes 524320 | tf_op jit(solution)/shard_map/ppermute | solution.py:498
  437.5 3.7 all-to-all-start.4
  441.2 11.4 %shard_map.228 = (bf16[1024,2048]{1,0:T(8,128)(2,1)}, bf16[1024,2048]{1,0:T(8,128)(2,1)}) custom-call(bf16[2048,256]{1,0:T(8,128)(2,1)} %get-tuple-element.253.act_ref.refs_0_, bf16[2048,256]{1,0:T(8,128)(2,1)} %get-tuple-element.243.act_ref.refs_1_, bf16[2048,768]{1,0:T(8,128)(2,1)} %all-gather.10.cloned.1.call-done.gu_ref.down_ref.refs_2_, ...), custom_call_target="tpu_custom_call" | custom-call | flops 4294967296 | bytes 14680064 | tf_op jit(solution)/shard_map/pallas_call | solution.py:62
  452.7 11.3 %collective-permute-done.27 = bf16[128,2048]{1,0:T(8,128)(2,1)} collective-permute-done((bf16[128,2048]{1,0:T(8,128)(2,1)}, bf16[128,2048]{1,0:T(8,128)(2,1)}, u32[]{:S(2)}, u32[]{:S(2)}) %collective-permute-start.27) | collective-permute-done | bytes 524320 | tf_op jit(solution)/shard_map/ppermute | solution.py:522
  471.5 9.4 %collective-permute-done.28 = bf16[64,2048]{1,0:T(8,128)(2,1)S(1)} collective-permute-done((bf16[64,2048]{1,0:T(8,128)(2,1)S(1)}, bf16[64,2048]{1,0:T(8,128)(2,1)S(1)}, u32[]{:S(2)}, u32[]{:S(2)}) %collective-permute-start.28) | collective-permute-done | bytes 262176 | tf_op jit(solution)/shard_map/ppermute | solution.py:498
  485.5 7.6 %collective-permute-done.30 = bf16[128,2048]{1,0:T(8,128)(2,1)S(1)} collective-permute-done((bf16[128,2048]{1,0:T(8,128)(2,1)S(1)}, bf16[128,2048]{1,0:T(8,128)(2,1)S(1)}, u32[]{:S(2)}, u32[]{:S(2)}) %collective-permute-start.30) | collective-permute-done | bytes 524320 | tf_op jit(solution)/shard_map/ppermute | solution.py:498
  494.1 13.5 %reduce-scatter.7.cloned.1.call-done = bf16[1024,768]{1,0:T(8,128)(2,1)} async-done(((bf16[2048,768]{1,0:T(8,128)(2,1)}), bf16[1024,768]{1,0:T(8,128)(2,1)}) %reduce-scatter.7.cloned.1.call-update) | async-done | bytes 1572880 | tf_op jit(solution)/shard_map/reduce_scatter | solution.py:672
  514.3 4.4 all-to-all-start.5
  518.7 5.5 collective-permute-done.32.b_ref.bb
  524.2 5.0 shard_map.229
  529.3 4.4 add_convert_fusion
  536.9 20.8 %shard_map.230 = (bf16[1024,256]{1,0:T(8,128)(2,1)}, bf16[1024,256]{1,0:T(8,128)(2,1)}, bf16[1024,256]{1,0:T(8,128)(2,1)}, bf16[2048,768]{1,0:T(8,128)(2,1)}, f32[2048,128]{1,0:T(8,128)}) custom-call(bf16[512,2048]{1,0:T(8,128)(2,1)} %constant_dynamic-update-slice_fusion.18.a_ref.ba, bf16[512,2048]{1,0:T(8,128)(2,1)} %collective-permute-done.32.b_ref.bb, ...), custom_call_target="tpu_custom_call" | custom-call | flops 4294967296 | bytes 16777216 | tf_op jit(solution)/shard_map/pallas_call | solution.py:438
  557.7 4.8 collective-permute-done.34
  564.6 5.2 shard_map.231
  569.8 3.4 add_convert_fusion.10
  575.9 5.4 shard_map.232
  581.3 6.5 collective-permute-done.37
  597.8 4.9 shard_map.234
  602.7 5.0 collective-permute-done.43
  626.8 4.3 all-to-all-start.6
  639.7 6.7 %all-to-all-done.6.refs_0_ = bf16[8,64,1024]{2,1,0:T(8,128)(2,1)} async-done(((bf16[8,64,1024]{2,1,0:T(8,128)(2,1)}), bf16[8,64,1024]{2,1,0:T(8,128)(2,1)}, u32[]{:S(2)}, u32[]{:S(2)}) %all-to-all-start.6) | async-done | bytes 1048608 | tf_op jit(solution)/shard_map/all_to_all | solution.py:666
  (288 shorter events, 172.8 us)
Async XLA Ops:
  7.2 63.0 %all-gather.8.cloned.1.call-start = ((), (), s32[]{:S(2)}) async-start(), calls=%async_computation.12 | async-start | bytes 1392640 | tf_op jit(solution)/shard_map/all_gather | solution.py:669
  17.9 19.2 %all-to-all-start = ((bf16[8,64,896]{2,1,0:T(8,128)(2,1)}), bf16[8,64,896]{2,1,0:T(8,128)(2,1)S(1)}, u32[]{:S(2)}, u32[]{:S(2)}) async-start(bf16[8,64,896]{2,1,0:T(8,128)(2,1)} %shard_map.220), calls=%async_computation | async-start | bytes 1835008 | tf_op jit(solution)/shard_map/all_to_all | solution.py:666
  23.1 84.5 %all-gather.6.cloned.1.call-start = ((), (), s32[]{:S(2)}) async-start(), calls=%async_computation.11 | async-start | bytes 3932160 | tf_op jit(solution)/shard_map/all_gather | solution.py:669
  38.8 13.8 %collective-permute-start.2 = (bf16[128,2048]{1,0:T(8,128)(2,1)S(1)}, bf16[128,2048]{1,0:T(8,128)(2,1)S(1)}, u32[]{:S(2)}, u32[]{:S(2)}) collective-permute-start(bf16[128,2048]{1,0:T(8,128)(2,1)S(1)} %bitcast.80), channel_id=1, source_target_pairs={{0,8},{8,0},{1,9},{9,1},{2,10},{10,2},{3,11},{11,3},{4,12},{12,4},... | collective-permute-start | bytes 1572872 | tf_op jit(solution)/shard_map/ppermute | solution.py:522
  40.5 12.2 %collective-permute-start = (bf16[64,2048]{1,0:T(8,128)(2,1)S(1)}, bf16[64,2048]{1,0:T(8,128)(2,1)S(1)}, u32[]{:S(2)}, u32[]{:S(2)}) collective-permute-start(bf16[64,2048]{1,0:T(8,128)(2,1)S(1)} %get-tuple-element.174), channel_id=1, source_target_pairs={{0,2},{1,3},{2,0},{3,1},{4,6},{5,7},{6,4},{7,5},{8,10},{9,11},{10,... | collective-permute-start | bytes 786440 | tf_op jit(solution)/shard_map/ppermute | solution.py:498
  52.8 12.9 %collective-permute-start.3 = (bf16[128,2048]{1,0:T(8,128)(2,1)S(1)}, bf16[128,2048]{1,0:T(8,128)(2,1)S(1)}, u32[]{:S(2)}, u32[]{:S(2)}) collective-permute-start(bf16[128,2048]{1,0:T(8,128)(2,1)S(1)} %get-tuple-element.179), channel_id=1, source_target_pairs={{0,4},{1,5},{2,6},{3,7},{4,0},{5,1},{6,2},{7,3},{8,12},{9,13},{10,... | collective-permute-start | bytes 1572872 | tf_op jit(solution)/shard_map/ppermute | solution.py:498
  54.2 12.8 %collective-permute-start.4 = (bf16[128,2048]{1,0:T(8,128)(2,1)S(1)}, bf16[128,2048]{1,0:T(8,128)(2,1)S(1)}, u32[]{:S(2)}, u32[]{:S(2)}) collective-permute-start(bf16[128,2048]{1,0:T(8,128)(2,1)S(1)} %get-tuple-element.180), channel_id=1, source_target_pairs={{0,2},{1,3},{2,0},{3,1},{4,6},{5,7},{6,4},{7,5},{8,10},{9,11},{10,... | collective-permute-start | bytes 1572872 | tf_op jit(solution)/shard_map/ppermute | solution.py:498
  70.1 31.3 %collective-permute-start.5 = (bf16[512,2048]{1,0:T(8,128)(2,1)}, bf16[512,2048]{1,0:T(8,128)(2,1)}, u32[]{:S(2)}, u32[]{:S(2)}) collective-permute-start(bf16[512,2048]{1,0:T(8,128)(2,1)} %constant_dynamic-update-slice_fusion.xa), channel_id=1, source_target_pairs={{0,1},{1,0},{2,3},{3,2},{4,5},{5,4},{6,7},{7,6},{8,9},{9,8},{10,11... | collective-permute-start | bytes 6291464 | tf_op jit(solution)/shard_map/ppermute | solution.py:498
  74.4 24.7 %all-to-all-start.1 = ((bf16[8,4,64,384]{3,2,1,0:T(8,128)(2,1)}), bf16[8,4,64,384]{3,2,1,0:T(8,128)(2,1)S(1)}, u32[]{:S(2)}, u32[]{:S(2)}) async-start(bf16[8,4,64,384]{3,2,1,0:T(8,128)(2,1)} %copy.35), calls=%async_computation.1 | async-start | bytes 3145728 | tf_op jit(solution)/shard_map/all_to_all | solution.py:666
  107.6 26.7 %all-to-all-start.2 = ((bf16[16,64,768]{2,1,0:T(8,128)(2,1)}), bf16[16,64,768]{2,1,0:T(8,128)(2,1)S(1)}, u32[]{:S(2)}, u32[]{:S(2)}) async-start(bf16[16,64,768]{2,1,0:T(8,128)(2,1)} %get-tuple-element.207), calls=%async_computation.2 | async-start | bytes 3145728 | tf_op jit(solution)/shard_map/all_to_all | solution.py:666
  111.4 102.5 %all-gather.10.cloned.1.call-start = ((), (), s32[]{:S(2)}) async-start(), calls=%async_computation.13 | async-start | bytes 4718592 | tf_op jit(solution)/shard_map/all_gather | solution.py:669
  130.7 16.2 %collective-permute-start.6 = (bf16[512,2176]{1,0:T(8,128)(2,1)}, bf16[512,2176]{1,0:T(8,128)(2,1)}, u32[]{:S(2)}, u32[]{:S(2)}) collective-permute-start(bf16[512,2176]{1,0:T(8,128)(2,1)} %get-tuple-element.196), channel_id=1, source_target_pairs={{0,1},{1,0},{2,3},{3,2},{4,5},{5,4},{6,7},{7,6},{8,9},{9,8},{10,11... | collective-permute-start | bytes 6684680 | tf_op jit(solution)/shard_map/ppermute | solution.py:498
  131.2 14.2 %collective-permute-start.7 = (bf16[128,2048]{1,0:T(8,128)(2,1)S(1)}, bf16[128,2048]{1,0:T(8,128)(2,1)}, u32[]{:S(2)}, u32[]{:S(2)}) collective-permute-start(bf16[128,2048]{1,0:T(8,128)(2,1)S(1)} %bitcast.81), channel_id=1, source_target_pairs={{0,2},{1,3},{2,0},{3,1},{4,6},{5,7},{6,4},{7,5},{8,10},{9,11},{10,... | collective-permute-start | bytes 1572872 | tf_op jit(solution)/shard_map/ppermute | solution.py:498
  132.9 14.0 %collective-permute-start.8 = (bf16[128,2048]{1,0:T(8,128)(2,1)S(1)}, bf16[128,2048]{1,0:T(8,128)(2,1)}, u32[]{:S(2)}, u32[]{:S(2)}) collective-permute-start(bf16[128,2048]{1,0:T(8,128)(2,1)S(1)} %copy-done.20), channel_id=1, source_target_pairs={{0,4},{1,5},{2,6},{3,7},{4,0},{5,1},{6,2},{7,3},{8,12},{9,13},{10,... | collective-permute-start | bytes 1572872 | tf_op jit(solution)/shard_map/ppermute | solution.py:498
  146.9 60.9 %all-to-all-start.3 = ((bf16[16,64,768]{2,1,0:T(8,128)(2,1)}), bf16[16,64,768]{2,1,0:T(8,128)(2,1)S(1)}, u32[]{:S(2)}, u32[]{:S(2)}) async-start(bf16[16,64,768]{2,1,0:T(8,128)(2,1)} %get-tuple-element.208), calls=%async_computation.3 | async-start | bytes 3145728 | tf_op jit(solution)/shard_map/all_to_all | solution.py:666
  150.6 130.8 %all-gather.12.cloned.1.call-start = ((), (), s32[]{:S(2)}) async-start(), calls=%async_computation.14 | async-start | bytes 3145728 | tf_op jit(solution)/shard_map/all_gather | solution.py:669
  154.7 51.3 %collective-permute-start.11 = (bf16[256,2048]{1,0:T(8,128)(2,1)S(1)}, bf16[256,2048]{1,0:T(8,128)(2,1)S(1)}, u32[]{:S(2)}, u32[]{:S(2)}) collective-permute-start(bf16[256,2048]{1,0:T(8,128)(2,1)S(1)} %pad_maximum_fusion.1), channel_id=1, source_target_pairs={{0,4},{1,5},{2,6},{3,7},{4,0},{5,1},{6,2},{7,3},{8,12},{9,13},{10,... | collective-permute-start | bytes 3145736 | tf_op jit(solution)/shard_map/ppermute | solution.py:498
  156.6 51.1 %collective-permute-start.12 = (bf16[256,2048]{1,0:T(8,128)(2,1)S(1)}, bf16[256,2048]{1,0:T(8,128)(2,1)}, u32[]{:S(2)}, u32[]{:S(2)}) collective-permute-start(bf16[256,2048]{1,0:T(8,128)(2,1)S(1)} %pad_maximum_fusion.2), channel_id=1, source_target_pairs={{0,2},{1,3},{2,0},{3,1},{4,6},{5,7},{6,4},{7,5},{8,10},{9,11},{10,... | collective-permute-start | bytes 3145736 | tf_op jit(solution)/shard_map/ppermute | solution.py:498
  158.1 46.9 %collective-permute-start.9 = (bf16[128,2176]{1,0:T(8,128)(2,1)S(1)}, bf16[128,2176]{1,0:T(8,128)(2,1)S(1)}, u32[]{:S(2)}, u32[]{:S(2)}) collective-permute-start(bf16[128,2176]{1,0:T(8,128)(2,1)S(1)} %get-tuple-element.203), channel_id=1, source_target_pairs={{0,4},{1,5},{2,6},{3,7},{4,0},{5,1},{6,2},{7,3},{8,12},{9,13},{10,... | collective-permute-start | bytes 1671176 | tf_op jit(solution)/shard_map/ppermute | solution.py:498
  158.7 47.3 %collective-permute-start.10 = (bf16[128,2176]{1,0:T(8,128)(2,1)S(1)}, bf16[128,2176]{1,0:T(8,128)(2,1)S(1)}, u32[]{:S(2)}, u32[]{:S(2)}) collective-permute-start(bf16[128,2176]{1,0:T(8,128)(2,1)S(1)} %get-tuple-element.204), channel_id=1, source_target_pairs={{0,2},{1,3},{2,0},{3,1},{4,6},{5,7},{6,4},{7,5},{8,10},{9,11},{10,... | collective-permute-start | bytes 1671176 | tf_op jit(solution)/shard_map/ppermute | solution.py:498
  227.6 123.2 %all-gather.14.cloned.1.call-start = ((), (), s32[]{:S(2)}) async-start(), calls=%async_computation.15 | async-start | bytes 1572864 | tf_op jit(solution)/shard_map/all_gather | solution.py:669
  237.1 24.3 %collective-permute-start.16 = (bf16[128,2048]{1,0:T(8,128)(2,1)}, bf16[128,2048]{1,0:T(8,128)(2,1)}, u32[]{:S(2)}, u32[]{:S(2)}) collective-permute-start(bf16[128,2048]{1,0:T(8,128)(2,1)} %get-tuple-element.218), channel_id=1, source_target_pairs={{0,8},{8,0},{1,9},{9,1},{2,10},{10,2},{3,11},{11,3},{4,12},{12,4},... | collective-permute-start | bytes 1572872 | tf_op jit(solution)/shard_map/ppermute | solution.py:522
  261.4 20.0 %collective-permute-start.17 = (bf16[128,2048]{1,0:T(8,128)(2,1)}, bf16[128,2048]{1,0:T(8,128)(2,1)}, u32[]{:S(2)}, u32[]{:S(2)}) collective-permute-start(bf16[128,2048]{1,0:T(8,128)(2,1)} %get-tuple-element.218), channel_id=1, source_target_pairs={{0,2},{1,3},{2,0},{3,1},{4,6},{5,7},{6,4},{7,5},{8,10},{9,11},{10,... | collective-permute-start | bytes 1572872 | tf_op jit(solution)/shard_map/ppermute | solution.py:498
  262.1 19.4 %collective-permute-start.18 = (bf16[128,2048]{1,0:T(8,128)(2,1)}, bf16[128,2048]{1,0:T(8,128)(2,1)}, u32[]{:S(2)}, u32[]{:S(2)}) collective-permute-start(bf16[128,2048]{1,0:T(8,128)(2,1)} %collective-permute-done.16), channel_id=1, source_target_pairs={{0,4},{1,5},{2,6},{3,7},{4,0},{5,1},{6,2},{7,3},{8,12},{9,13},{10,... | collective-permute-start | bytes 1572872 | tf_op jit(solution)/shard_map/ppermute | solution.py:498
  284.0 25.0 %collective-permute-start.19 = (bf16[256,2048]{1,0:T(8,128)(2,1)S(1)}, bf16[256,2048]{1,0:T(8,128)(2,1)S(1)}, u32[]{:S(2)}, u32[]{:S(2)}) collective-permute-start(bf16[256,2048]{1,0:T(8,128)(2,1)S(1)} %pad_maximum_fusion.3), channel_id=1, source_target_pairs={{0,4},{1,5},{2,6},{3,7},{4,0},{5,1},{6,2},{7,3},{8,12},{9,13},{10,... | collective-permute-start | bytes 3145736 | tf_op jit(solution)/shard_map/ppermute | solution.py:498
  285.5 24.6 %collective-permute-start.20 = (bf16[256,2048]{1,0:T(8,128)(2,1)S(1)}, bf16[256,2048]{1,0:T(8,128)(2,1)S(1)}, u32[]{:S(2)}, u32[]{:S(2)}) collective-permute-start(bf16[256,2048]{1,0:T(8,128)(2,1)S(1)} %pad_maximum_fusion.4), channel_id=1, source_target_pairs={{0,2},{1,3},{2,0},{3,1},{4,6},{5,7},{6,4},{7,5},{8,10},{9,11},{10,... | collective-permute-start | bytes 3145736 | tf_op jit(solution)/shard_map/ppermute | solution.py:498
  317.0 117.6 %reduce-scatter.5.cloned.1.call-start = ((), (), s32[]{:S(2)}) async-start(), calls=%async_computation.16 | async-start | bytes 4718592 | tf_op jit(solution)/shard_map/reduce_scatter | solution.py:672
  350.8 156.8 %reduce-scatter.7.cloned.1.call-start = ((), (), s32[]{:S(2)}) async-start(), calls=%async_computation.17 | async-start | bytes 4718592 | tf_op jit(solution)/shard_map/reduce_scatter | solution.py:672
  392.0 25.4 %collective-permute-start.23 = (bf16[256,2048]{1,0:T(8,128)(2,1)}, bf16[256,2048]{1,0:T(8,128)(2,1)S(1)}, u32[]{:S(2)}, u32[]{:S(2)}) collective-permute-start(bf16[256,2048]{1,0:T(8,128)(2,1)} %get-tuple-element.241), channel_id=1, source_target_pairs={{0,4},{1,5},{2,6},{3,7},{4,0},{5,1},{6,2},{7,3},{8,12},{9,13},{10,... | collective-permute-start | bytes 3145736 | tf_op jit(solution)/shard_map/ppermute | solution.py:498
  392.7 25.2 %collective-permute-start.24 = (bf16[256,2048]{1,0:T(8,128)(2,1)}, bf16[256,2048]{1,0:T(8,128)(2,1)}, u32[]{:S(2)}, u32[]{:S(2)}) collective-permute-start(bf16[256,2048]{1,0:T(8,128)(2,1)} %get-tuple-element.242), channel_id=1, source_target_pairs={{0,2},{1,3},{2,0},{3,1},{4,6},{5,7},{6,4},{7,5},{8,10},{9,11},{10,... | collective-permute-start | bytes 3145736 | tf_op jit(solution)/shard_map/ppermute | solution.py:498
  420.2 13.3 %collective-permute-start.25 = (bf16[128,2048]{1,0:T(8,128)(2,1)S(1)}, bf16[128,2048]{1,0:T(8,128)(2,1)}, u32[]{:S(2)}, u32[]{:S(2)}) collective-permute-start(bf16[128,2048]{1,0:T(8,128)(2,1)S(1)} %get-tuple-element.248), channel_id=1, source_target_pairs={{0,2},{1,3},{2,0},{3,1},{4,6},{5,7},{6,4},{7,5},{8,10},{9,11},{10,... | collective-permute-start | bytes 1572872 | tf_op jit(solution)/shard_map/ppermute | solution.py:498
  421.7 12.8 %collective-permute-start.26 = (bf16[128,2048]{1,0:T(8,128)(2,1)S(1)}, bf16[128,2048]{1,0:T(8,128)(2,1)S(1)}, u32[]{:S(2)}, u32[]{:S(2)}) collective-permute-start(bf16[128,2048]{1,0:T(8,128)(2,1)S(1)} %get-tuple-element.249), channel_id=1, source_target_pairs={{0,4},{1,5},{2,6},{3,7},{4,0},{5,1},{6,2},{7,3},{8,12},{9,13},{10,... | collective-permute-start | bytes 1572872 | tf_op jit(solution)/shard_map/ppermute | solution.py:498
  437.5 26.5 %collective-permute-start.27 = (bf16[128,2048]{1,0:T(8,128)(2,1)}, bf16[128,2048]{1,0:T(8,128)(2,1)}, u32[]{:S(2)}, u32[]{:S(2)}) collective-permute-start(bf16[128,2048]{1,0:T(8,128)(2,1)} %add_convert_fusion.12), channel_id=1, source_target_pairs={{0,8},{8,0},{1,9},{9,1},{2,10},{10,2},{3,11},{11,3},{4,12},{12,4},... | collective-permute-start | bytes 1572872 | tf_op jit(solution)/shard_map/ppermute | solution.py:522
  437.5 56.6 %all-to-all-start.4 = ((bf16[16,64,768]{2,1,0:T(8,128)(2,1)}), bf16[16,64,768]{2,1,0:T(8,128)(2,1)S(1)}, u32[]{:S(2)}, u32[]{:S(2)}) async-start(bf16[16,64,768]{2,1,0:T(8,128)(2,1)} %bitcast.88), calls=%async_computation.5 | async-start | bytes 3145728 | tf_op jit(solution)/shard_map/all_to_all | solution.py:666
  482.2 11.9 %collective-permute-start.31 = (bf16[128,2048]{1,0:T(8,128)(2,1)S(1)}, bf16[128,2048]{1,0:T(8,128)(2,1)}, u32[]{:S(2)}, u32[]{:S(2)}) collective-permute-start(bf16[128,2048]{1,0:T(8,128)(2,1)S(1)} %pad_maximum_fusion.11), channel_id=1, source_target_pairs={{0,2},{1,3},{2,0},{3,1},{4,6},{5,7},{6,4},{7,5},{8,10},{9,11},{10,... | collective-permute-start | bytes 1572872 | tf_op jit(solution)/shard_map/ppermute | solution.py:498
  514.3 43.5 %all-to-all-start.5 = ((bf16[16,64,768]{2,1,0:T(8,128)(2,1)}), bf16[16,64,768]{2,1,0:T(8,128)(2,1)}, u32[]{:S(2)}, u32[]{:S(2)}) async-start(bf16[16,64,768]{2,1,0:T(8,128)(2,1)} %bitcast.87), calls=%async_computation.7 | async-start | bytes 3145728 | tf_op jit(solution)/shard_map/all_to_all | solution.py:666
  518.7 44.9 %reduce-scatter.9.cloned.1.call-start = ((), (), s32[]{:S(2)}) async-start(), calls=%async_computation.18 | async-start | bytes 1310720 | tf_op jit(solution)/shard_map/reduce_scatter | solution.py:672
  533.7 89.7 %reduce-scatter.11.cloned.1.call-start = ((), (), s32[]{:S(2)}) async-start(), calls=%async_computation.19 | async-start | bytes 3932160 | tf_op jit(solution)/shard_map/reduce_scatter | solution.py:672
  533.9 28.6 %collective-permute-start.34 = (bf16[256,2048]{1,0:T(8,128)(2,1)}, bf16[256,2048]{1,0:T(8,128)(2,1)}, u32[]{:S(2)}, u32[]{:S(2)}) collective-permute-start(bf16[256,2048]{1,0:T(8,128)(2,1)} %get-tuple-element.289), channel_id=1, source_target_pairs={{0,4},{1,5},{2,6},{3,7},{4,0},{5,1},{6,2},{7,3},{8,12},{9,13},{10,... | collective-permute-start | bytes 3145736 | tf_op jit(solution)/shard_map/ppermute | solution.py:498
  535.5 28.2 %collective-permute-start.35 = (bf16[256,2048]{1,0:T(8,128)(2,1)}, bf16[256,2048]{1,0:T(8,128)(2,1)}, u32[]{:S(2)}, u32[]{:S(2)}) collective-permute-start(bf16[256,2048]{1,0:T(8,128)(2,1)} %get-tuple-element.290), channel_id=1, source_target_pairs={{0,2},{1,3},{2,0},{3,1},{4,6},{5,7},{6,4},{7,5},{8,10},{9,11},{10,... | collective-permute-start | bytes 3145736 | tf_op jit(solution)/shard_map/ppermute | solution.py:498
  573.2 15.4 %collective-permute-start.36 = (bf16[512,2048]{1,0:T(8,128)(2,1)}, bf16[512,2048]{1,0:T(8,128)(2,1)S(1)}, u32[]{:S(2)}, u32[]{:S(2)}) collective-permute-start(bf16[512,2048]{1,0:T(8,128)(2,1)} %shard_map.231), channel_id=1, source_target_pairs={{0,1},{1,0},{2,3},{3,2},{4,5},{5,4},{6,7},{7,6},{8,9},{9,8},{10,11... | collective-permute-start | bytes 6291464 | tf_op jit(solution)/shard_map/ppermute | solution.py:498
  573.2 14.7 %collective-permute-start.37 = (bf16[128,2048]{1,0:T(8,128)(2,1)}, bf16[128,2048]{1,0:T(8,128)(2,1)}, u32[]{:S(2)}, u32[]{:S(2)}) collective-permute-start(bf16[128,2048]{1,0:T(8,128)(2,1)} %get-tuple-element.299), channel_id=1, source_target_pairs={{0,2},{1,3},{2,0},{3,1},{4,6},{5,7},{6,4},{7,5},{8,10},{9,11},{10,... | collective-permute-start | bytes 1572872 | tf_op jit(solution)/shard_map/ppermute | solution.py:498
  573.8 14.7 %collective-permute-start.38 = (bf16[128,2048]{1,0:T(8,128)(2,1)}, bf16[128,2048]{1,0:T(8,128)(2,1)}, u32[]{:S(2)}, u32[]{:S(2)}) collective-permute-start(bf16[128,2048]{1,0:T(8,128)(2,1)} %get-tuple-element.300), channel_id=1, source_target_pairs={{0,4},{1,5},{2,6},{3,7},{4,0},{5,1},{6,2},{7,3},{8,12},{9,13},{10,... | collective-permute-start | bytes 1572872 | tf_op jit(solution)/shard_map/ppermute | solution.py:498
  592.5 15.2 %collective-permute-start.41 = (bf16[128,2048]{1,0:T(8,128)(2,1)}, bf16[128,2048]{1,0:T(8,128)(2,1)}, u32[]{:S(2)}, u32[]{:S(2)}) collective-permute-start(bf16[128,2048]{1,0:T(8,128)(2,1)} %get-tuple-element.308), channel_id=1, source_target_pairs={{0,4},{1,5},{2,6},{3,7},{4,0},{5,1},{6,2},{7,3},{8,12},{9,13},{10,... | collective-permute-start | bytes 1572872 | tf_op jit(solution)/shard_map/ppermute | solution.py:498
  594.2 13.5 %collective-permute-start.42 = (bf16[128,2048]{1,0:T(8,128)(2,1)}, bf16[128,2048]{1,0:T(8,128)(2,1)}, u32[]{:S(2)}, u32[]{:S(2)}) collective-permute-start(bf16[128,2048]{1,0:T(8,128)(2,1)} %get-tuple-element.309), channel_id=1, source_target_pairs={{0,2},{1,3},{2,0},{3,1},{4,6},{5,7},{6,4},{7,5},{8,10},{9,11},{10,... | collective-permute-start | bytes 1572872 | tf_op jit(solution)/shard_map/ppermute | solution.py:498
  594.9 12.8 %collective-permute-start.43 = (f32[32,128]{1,0:T(8,128)S(1)}, f32[32,128]{1,0:T(8,128)S(1)}, u32[]{:S(2)}, u32[]{:S(2)}) collective-permute-start(f32[32,128]{1,0:T(8,128)S(1)} %add.282), channel_id=1, source_target_pairs={{0,2},{1,3},{2,0},{3,1},{4,6},{5,7},{6,4},{7,5},{8,10},{9,11},{10,... | collective-permute-start | bytes 49160 | tf_op jit(solution)/shard_map/ppermute | solution.py:498
  623.4 13.6 %collective-permute-start.40 = (bf16[128,2048]{1,0:T(8,128)(2,1)}, bf16[128,2048]{1,0:T(8,128)(2,1)S(1)}, u32[]{:S(2)}, u32[]{:S(2)}) collective-permute-start(bf16[128,2048]{1,0:T(8,128)(2,1)} %add_convert_fusion.9), channel_id=1, source_target_pairs={{0,8},{8,0},{1,9},{9,1},{2,10},{10,2},{3,11},{11,3},{4,12},{12,4},... | collective-permute-start | bytes 1572872 | tf_op jit(solution)/shard_map/ppermute | solution.py:522
  626.8 19.7 %all-to-all-start.6 = ((bf16[8,64,1024]{2,1,0:T(8,128)(2,1)}), bf16[8,64,1024]{2,1,0:T(8,128)(2,1)}, u32[]{:S(2)}, u32[]{:S(2)}) async-start(bf16[8,64,1024]{2,1,0:T(8,128)(2,1)} %bitcast.83), calls=%async_computation.10 | async-start | bytes 2097152 | tf_op jit(solution)/shard_map/all_to_all | solution.py:666
  (53 other events, 417.8 us)
Sparse Core Ops, SparseCore 0:
  10.2 31.8 all-gather.7
  43.6 64.0 all-gather.5
  135.6 78.2 all-gather.9
  227.7 53.7 all-gather.11
  317.1 31.9 all-gather.13
  351.2 76.9 reduce-scatter.4
  430.5 77.0 reduce-scatter.6
  533.8 26.0 reduce-scatter.8
  563.8 59.5 reduce-scatter.10
